TPU v7x, 32 devices: a whole 2x2x4 slice. The times are simulated.
32 devices in a mesh: seq: 8 (over y, x, core), head: 4 (over z).
Axes of the slice: x: 2, y: 2, z: 4, core: 2. Of those that a mesh axis runs over, the one named last changes fastest.
Arguments:
- query_rows: bfloat16 [4096, 1024], P('seq', 'head'), may hold values from -100 to 100
- key_rows: bfloat16 [4096, 1024], P('seq', 'head'), may hold values from -4 to 4
- value_rows: bfloat16 [4096, 1024], P('seq', 'head'), may hold values from -6 to 6
- out_grad: bfloat16 [4096, 1024], P('seq', 'head'), may hold values from -6 to 6
- members: int32 [4096], P(('seq', 'head')), may hold values from 0 to 4095, as said below
Outputs:
- attn_out: bfloat16 [4096, 1024], P('seq', 'head')
- query_grad: bfloat16 [4096, 1024], P('seq', 'head')
- key_grad: bfloat16 [4096, 1024], P('seq', 'head')
- value_grad: bfloat16 [4096, 1024], P('seq', 'head')
Inputs may be any that keep to these rules, and one draw needn't show every extreme that they name: `members`: every position appears once; the 512 positions of each cluster stand in ascending order. Of the 512 positions of one index of seq a cluster takes 0, 64 or 128, and for each index of seq some clusters take 128. The positions may be sent packed, several to a 32-bit word, or in any narrower integer form that holds them exactly.
All inputs are finite; a program needn't handle non-finite values.
Results may differ from a plain program's by a relative error of at most 0.008.
Values may be sent and summed in bfloat16 or wider, within the bound.
No kernel may reach another device: no remote copies, remote signals or barrier semaphores. Data moves between devices by JAX's collectives and lax.ppermute only.
A program may use at most 64 MiB of HBM per device.

v0:
```python
import math

import jax
import jax.numpy as jnp
from jax import lax
from jax.sharding import PartitionSpec as P

CLUS = 512
WINDOW = 512


def from_behind(array, axis, by):
    count = lax.axis_size(axis)
    pairs = [(i, i + by) for i in range(count) if 0 <= i + by < count]
    return lax.ppermute(array, axis, pairs)


def attend(query_matrix, input_keys, value_matrix, upstream_gradient, allowed):
    logit_scale = 1.0 / math.sqrt(query_matrix.shape[-1])
    attention_scores = (
        jnp.einsum("vnw,vtw->vnt", query_matrix, input_keys, preferred_element_type=jnp.float32)
        * logit_scale
    )
    attention_scores = jnp.where(allowed, attention_scores, -jnp.inf)
    row_max = jnp.max(attention_scores, axis=-1, keepdims=True)
    exp_scores = jnp.exp(attention_scores - row_max)
    probability = exp_scores / jnp.sum(exp_scores, axis=-1, keepdims=True)
    attention_weights = probability.astype(jnp.bfloat16)
    attended_output = jnp.einsum(
        "yxs,ysl->yxl", attention_weights, value_matrix, preferred_element_type=jnp.float32
    )
    probability_gradient = jnp.einsum(
        "vnw,vtw->vnt", upstream_gradient, value_matrix, preferred_element_type=jnp.float32
    )
    row_delta = jnp.sum(probability * probability_gradient, axis=-1, keepdims=True)
    score_gradient = (probability * (probability_gradient - row_delta) * logit_scale).astype(
        jnp.bfloat16
    )
    query_gradient = jnp.einsum(
        "yxs,ysl->yxl", score_gradient, input_keys, preferred_element_type=jnp.float32
    )
    key_gradient = jnp.einsum(
        "ipy,ipg->iyg", score_gradient, query_matrix, preferred_element_type=jnp.float32
    )
    value_gradient = jnp.einsum(
        "ipy,ipg->iyg", attention_weights, upstream_gradient, preferred_element_type=jnp.float32
    )
    return (attended_output, query_gradient, key_gradient, value_gradient)


def window_head(query_matrix, input_keys, value_matrix, upstream_gradient):
    tok_rows = query_matrix.shape[0]
    window_len = WINDOW
    blocks = tok_rows // window_len
    rim_keys, rim_values = from_behind((input_keys, value_matrix), "seq", 1)
    extended_keys = jnp.concatenate([rim_keys, input_keys], axis=0)
    extended_values = jnp.concatenate([rim_values, value_matrix], axis=0)

    def framed(extended):
        return jnp.concatenate(
            [
                extended[:tok_rows].reshape(blocks, window_len, -1),
                extended[window_len:].reshape(blocks, window_len, -1),
            ],
            axis=1,
        )

    def unframe(blockwise):
        lower_half = blockwise[:, :window_len].reshape(tok_rows, -1)
        upper_half = blockwise[:, window_len:].reshape(tok_rows, -1)
        return jnp.pad(lower_half, ((0, window_len), (0, 0))) + jnp.pad(
            upper_half, ((window_len, 0), (0, 0))
        )

    offset = lax.axis_index("seq") * tok_rows
    query_pos = jnp.arange(window_len)[None, :, None]
    key_pos = jnp.arange(2 * window_len)[None, None, :]
    block_pos = jnp.arange(blocks)[:, None, None]
    allowed = (
        (key_pos > query_pos)
        & (key_pos <= query_pos + window_len)
        & (offset + block_pos * window_len + key_pos >= window_len)
    )
    attended_output, query_gradient, key_gradient, value_gradient = attend(
        query_matrix.reshape(blocks, window_len, -1),
        framed(extended_keys),
        framed(extended_values),
        upstream_gradient.reshape(blocks, window_len, -1),
        allowed,
    )
    full_keys = unframe(key_gradient)
    full_values = unframe(value_gradient)
    later_keys, later_values = (
        from_behind(full_keys[:window_len].astype(jnp.bfloat16), "seq", -1).astype(jnp.float32),
        from_behind(full_values[:window_len].astype(jnp.bfloat16), "seq", -1).astype(jnp.float32),
    )
    own_keys = full_keys[window_len:].at[tok_rows - window_len :].add(later_keys)
    own_values = full_values[window_len:].at[tok_rows - window_len :].add(later_values)
    return (
        attended_output.reshape(tok_rows, -1).astype(jnp.bfloat16),
        query_gradient.reshape(tok_rows, -1).astype(jnp.bfloat16),
        own_keys.astype(jnp.bfloat16),
        own_values.astype(jnp.bfloat16),
    )


def on_device(query_rows, key_rows, value_rows, out_grad, members):
    tok_rows = query_rows.shape[0]
    head_dim = query_rows.shape[1] // 2
    all_members = lax.all_gather(members, ("seq", "head"), axis=0, tiled=True)
    shards = lax.axis_size("seq")
    me_index = lax.axis_index("seq")
    clusters = all_members.shape[0] // CLUS
    per_dev = clusters // shards
    capacity = 2 * (CLUS // shards)
    total = clusters * capacity
    member_table = all_members.reshape(clusters, CLUS)
    source = member_table // tok_rows
    is_mine = source == me_index
    run_start = jnp.sum((source < me_index).astype(jnp.int32), axis=1, keepdims=True)
    ranking = jnp.arange(CLUS, dtype=jnp.int32)[None, :]
    cluster_ids = jnp.arange(clusters, dtype=jnp.int32)[:, None]
    flat_slot = cluster_ids * capacity + ranking - run_start
    local_row = member_table - me_index * tok_rows
    slot_rows = (
        jnp.full((total,), tok_rows, jnp.int32)
        .at[jnp.where(is_mine, flat_slot, total).reshape(-1)]
        .set(local_row.reshape(-1), mode="drop")
    )
    home_slot = (
        jnp.zeros((tok_rows,), jnp.int32)
        .at[jnp.where(is_mine, local_row, tok_rows).reshape(-1)]
        .set(flat_slot.reshape(-1), mode="drop")
    )
    own_table = lax.dynamic_slice_in_dim(member_table, me_index * per_dev, per_dev, 0)
    own_source = own_table // tok_rows
    bins = jnp.arange(shards, dtype=jnp.int32)
    starts = jnp.sum((own_source[:, :, None] < bins[None, None, :]).astype(jnp.int32), axis=1)
    own_start = jnp.take_along_axis(starts, own_source, axis=1)
    local_ids = jnp.arange(per_dev, dtype=jnp.int32)[:, None]
    gather_index = ((own_source * per_dev + local_ids) * capacity + ranking - own_start).reshape(-1)
    causal = (jnp.arange(CLUS)[:, None] >= jnp.arange(CLUS)[None, :])[None]
    route_query = query_rows[:, head_dim:]
    route_key = key_rows[:, head_dim:]
    route_value = value_rows[:, head_dim:]
    route_grad = out_grad[:, head_dim:]
    flat_rows = lax.all_to_all(
        jnp.take(
            jnp.concatenate([route_query, route_key, route_value, route_grad], axis=1),
            slot_rows,
            axis=0,
            mode="fill",
            fill_value=0,
        ).reshape(shards, per_dev * capacity, -1),
        "seq",
        split_axis=0,
        concat_axis=0,
        tiled=True,
    ).reshape(total, -1)
    arrived = jnp.take(flat_rows, gather_index, axis=0).reshape(per_dev, CLUS, -1)
    group_query = arrived[:, :, :head_dim]
    group_key = arrived[:, :, head_dim : 2 * head_dim]
    group_value = arrived[:, :, 2 * head_dim : 3 * head_dim]
    group_grad = arrived[:, :, 3 * head_dim :]
    results = attend(group_query, group_key, group_value, group_grad, causal)
    stacked = jnp.concatenate(results, axis=2).astype(jnp.bfloat16)
    res_width = stacked.shape[-1]
    spread = (
        jnp.zeros((total, res_width), stacked.dtype)
        .at[gather_index]
        .set(stacked.reshape(-1, res_width))
    )
    route_all = jnp.take(
        lax.all_to_all(
            spread.reshape(shards, per_dev * capacity, res_width),
            "seq",
            split_axis=0,
            concat_axis=0,
            tiled=True,
        ).reshape(total, -1),
        home_slot,
        axis=0,
    )
    route_out = route_all[:, :head_dim]
    route_grads = route_all[:, head_dim:]
    window_out, window_query, window_key, window_value = window_head(
        query_rows[:, :head_dim],
        key_rows[:, :head_dim],
        value_rows[:, :head_dim],
        out_grad[:, :head_dim],
    )
    attn_out = jnp.concatenate([window_out, route_out], axis=1)
    query_grad = jnp.concatenate([window_query, route_grads[:, :head_dim]], axis=1)
    key_grad = jnp.concatenate([window_key, route_grads[:, head_dim : 2 * head_dim]], axis=1)
    value_grad = jnp.concatenate([window_value, route_grads[:, 2 * head_dim :]], axis=1)
    return (attn_out, query_grad, key_grad, value_grad)


def solution(mesh):
    in_specs = (
        P("seq", "head"),
        P("seq", "head"),
        P("seq", "head"),
        P("seq", "head"),
        P(("seq", "head")),
    )
    out_specs = (P("seq", "head"), P("seq", "head"), P("seq", "head"), P("seq", "head"))
    return jax.shard_map(
        on_device, mesh=mesh, in_specs=in_specs, out_specs=out_specs, check_vma=False
    )
```

profile of v0, /device:TPU:0, one launch (start us, length us, event | category | flops | bytes accessed | tf_op | source)
XLA Modules:
  0.0 177.5 jit_solution(2421880484327010528)
XLA Ops:
  0.7 69.6 %all-gather = s32[32,1,128]{2,1,0:T(1,128)S(1)} all-gather(s32[1,1,128]{2,1,0:T(1,128)} %bitcast.112), channel_id=1, replica_groups=mesh['seq'=8,'head'=4] {'seq','head'}, dimensions={0}, use_global_device_ids=true | all-gather | bytes 16896 | tf_op jit(solution)/shard_map/all_gather | solution.py:110
  70.3 0.5 broadcast.339
  70.8 0.7 reduce.24
  71.7 15.5 %scatter_custom_fusion = s32[1024]{0:T(1024)S(1)} fusion(s32[4096]{0:T(1024)S(1)} %get-tuple-element.81, s32[4096]{0:T(1024)S(1)} %get-tuple-element.62, s32[]{:T(128)} %constant.147.clone.1), kind=kCustom, calls=%fused_computation.127 | custom fusion | bytes 4100 | tf_op jit(solution)/shard_map/scatter | solution.py:128
  87.3 1.7 fusion.54
  89.0 1.7 fusion.53
  90.7 4.0 %gather_fusion = bf16[1024,512]{1,0:T(8,128)(2,1)S(1)} fusion(bf16[512,512]{1,0:T(8,128)(2,1)S(1)} %pad_maximum_fusion, s32[1024]{0:T(1024)S(1)} %fusion.37), kind=kCustom, calls=%fused_computation.2 | custom fusion | bytes 2101248 | tf_op jit(solution)/shard_map/jit(_take)/gather | solution.py:148
  94.7 1.2 broadcast_select_fusion
  95.9 3.6 %all-to-all-start = ((bf16[8,128,512]{2,1,0:T(8,128)(2,1)}), bf16[8,128,512]{2,1,0:T(8,128)(2,1)S(1)}, u32[]{:S(2)}, u32[]{:S(2)}) async-start(bf16[8,128,512]{2,1,0:T(8,128)(2,1)} %broadcast_select_fusion), calls=%async_computation | async-start | bytes 2097152 | tf_op jit(solution)/shard_map/all_to_all | solution.py:147
  99.5 3.0 %collective-permute-start.1 = (bf16[512,128]{1,0:T(8,128)(2,1)}, bf16[512,128]{1,0:T(8,128)(2,1)}, u32[]{:S(2)}, u32[]{:S(2)}) collective-permute-start(bf16[512,128]{1,0:T(8,128)(2,1)} %get-tuple-element.78), channel_id=1, source_target_pairs={{0,4},{4,8},{8,12},{12,16},{16,20},{20,24},{24,28},{1,5},{5,9},{9,... | collective-permute-start | bytes 393224 | tf_op jit(solution)/shard_map/ppermute | solution.py:15
  102.4 2.9 %collective-permute-start = (bf16[512,128]{1,0:T(8,128)(2,1)S(1)}, bf16[512,128]{1,0:T(8,128)(2,1)S(1)}, u32[]{:S(2)}, u32[]{:S(2)}) collective-permute-start(bf16[512,128]{1,0:T(8,128)(2,1)S(1)} %get-tuple-element.75), channel_id=1, source_target_pairs={{0,4},{4,8},{8,12},{12,16},{16,20},{20,24},{24,28},{1,5},{5,9},{9,... | collective-permute-start | bytes 393224 | tf_op jit(solution)/shard_map/ppermute | solution.py:15
  105.5 0.7 fusion.55
  106.2 4.4 %compare_select_fusion.5 = s32[1,512]{1,0:T(1,128)S(1)} fusion(s32[]{:T(128)} %bitcast.11, s32[]{:T(128)} %bitcast.12, s32[]{:T(128)} %bitcast.13, s32[]{:T(128)} %bitcast.14, s32[]{:T(128)} %bitcast.15, s32[]{:T(128)} %bitcast.17, s32[]{:T(128)} %bitcast.16, s32[1,512]{1,0:T(1,128)S(1)} %get-tuple-element.66), kind=kLoop, calls=%fused_computation.108 | loop fusion | flops 7680 | bytes 4124 | tf_op jit(solution)/shard_map/jit(take_along_axis)/gather | solution.py:139
  110.6 0.7 broadcast_select_fusion.2
  111.2 0.6 compare_select_fusion.2
  111.8 0.6 compare_and_fusion.1
  112.4 15.5 %scatter_custom_fusion.2 = s32[512]{0:T(512)S(1)} fusion(s32[4096]{0:T(1024)S(1)} %get-tuple-element.61, s32[4096]{0:T(1024)S(1)} %bitcast.105, s32[]{:T(128)} %constant.154.clone.1), kind=kCustom, calls=%fused_computation.133 | custom fusion | bytes 2052 | tf_op jit(solution)/shard_map/scatter | solution.py:133
  127.9 0.6 compare_and_fusion
  128.6 0.6 copy-done.14
  129.2 1.5 fusion.57
  130.8 0.4 fusion.7
  131.2 0.6 copy-done.8
  131.7 1.4 fusion
  133.2 0.6 fusion.3
  133.8 0.5 convolution_bitcast_fusion.1
  134.3 0.7 copy-done.2
  135.0 0.7 fusion.22
  135.7 1.3 collective-permute-start.2
  137.0 0.6 convolution_bitcast_fusion
  137.6 0.8 fusion.21
  138.4 1.5 collective-permute-start.3
  139.9 2.6 %gather_fusion.1 = bf16[512,512]{1,0:T(8,128)(2,1)} fusion(bf16[1024,512]{1,0:T(8,128)(2,1)S(1)} %bitcast.99, s32[1024]{0:T(1024)S(1)} %pad_clamp_fusion.1), kind=kCustom, calls=%fused_computation.clone | custom fusion | bytes 1050624 | tf_op jit(solution)/shard_map/jit(_take)/gather | solution.py:160
  142.5 1.2 select_bitcast_fusion
  144.2 0.4 convolution_convert_fusion
  145.8 0.3 convolution_convert_fusion.3
  146.4 3.6 %scatter_custom_fusion.1 = bf16[1024,512]{1,0:T(8,128)(2,1)} fusion(s32[512]{0:T(512)} %bitcast.111, bf16[512,512]{1,0:T(8,128)(2,1)S(1)} %copy.26, bf16[]{:T(256)} %constant.153.clone.1), kind=kCustom, calls=%fused_computation.44 | custom fusion | bytes 1049088 | tf_op jit(solution)/shard_map/scatter | solution.py:171
  150.0 5.8 %all-to-all-start.1 = ((bf16[8,128,512]{2,1,0:T(8,128)(2,1)}), bf16[8,128,512]{2,1,0:T(8,128)(2,1)S(1)}, u32[]{:S(2)}, u32[]{:S(2)}) async-start(bf16[8,128,512]{2,1,0:T(8,128)(2,1)} %bitcast.102), calls=%async_computation.1 | async-start | bytes 2097152 | tf_op jit(solution)/shard_map/all_to_all | solution.py:174
  155.8 2.2 %convolution_convert_fusion.5 = bf16[512,128]{0,1:T(8,128)(2,1)} fusion(bf16[1,512,128]{2,1,0:T(8,128)(2,1)} %get-tuple-element.79, bf16[1,512,128]{2,1,0:T(8,128)(2,1)} %bitcast.4, f32[512,1024]{0,1:T(8,128)S(1)} %get-tuple-element.95, f32[512]{0:T(512)S(1)} %fusion.7, f32[512]{0:T(512)S(1)} %get-tuple-element.94), kind=kOutput, calls=%fused_computation.29 | convolution fusion | flops 136380416 | bytes 2494464 | tf_op jit(solution)/shard_map/yxs,ysl->yxl/dot_general | solution.py:29
  158.1 0.3 convolution_convert_fusion.4
  158.5 0.9 fusion.17
  159.4 0.9 fusion.20
  160.4 10.8 %all-to-all-done.1 = bf16[8,128,512]{2,1,0:T(8,128)(2,1)S(1)} async-done(((bf16[8,128,512]{2,1,0:T(8,128)(2,1)}), bf16[8,128,512]{2,1,0:T(8,128)(2,1)S(1)}, u32[]{:S(2)}, u32[]{:S(2)}) %all-to-all-start.1) | async-done | bytes 1048608 | tf_op jit(solution)/shard_map/all_to_all | solution.py:174
  171.2 2.0 %gather_fusion.2 = bf16[512,512]{1,0:T(8,128)(2,1)S(1)} fusion(bf16[1024,512]{1,0:T(8,128)(2,1)S(1)} %bitcast.100, s32[1024]{0:T(1024)S(1)} %pad_clamp_fusion), kind=kCustom, calls=%fused_computation.1.clone | custom fusion | bytes 1050624 | tf_op jit(solution)/shard_map/jit(_take)/gather | solution.py:173
  173.5 0.6 copy-done.12
  174.1 0.8 copy.28
  175.0 0.8 copy.29
  175.8 0.8 copy.30
  176.7 0.8 copy.31
  (70 shorter events, 3.1 us)
Async XLA Ops:
  0.6 90.0 %slice-start = ((bf16[512,256]{1,0:T(8,128)(2,1)}), bf16[512,128]{1,0:T(8,128)(2,1)S(1)}, s32[]{:S(2)}) async-start(bf16[512,256]{1,0:T(8,128)(2,1)} %param.18), calls=%async_computation.2 | async-start | bytes 262144 | tf_op jit(solution)/shard_map/slice | solution.py:146
  0.6 90.0 %slice-start.1 = ((bf16[512,256]{1,0:T(8,128)(2,1)}), bf16[512,128]{1,0:T(8,128)(2,1)S(1)}, s32[]{:S(2)}) async-start(bf16[512,256]{1,0:T(8,128)(2,1)} %param.15), calls=%async_computation.3 | async-start | bytes 262144 | tf_op jit(solution)/shard_map/slice | solution.py:143
  94.7 34.5 %copy-start.9 = (bf16[512,256]{1,0:T(8,128)(2,1)S(1)}, bf16[512,256]{1,0:T(8,128)(2,1)}, u32[]{:S(2)}) copy-start(bf16[512,256]{1,0:T(8,128)(2,1)} %param.15) | copy-start | bytes 786436
  94.7 34.5 %copy-start.10 = (bf16[1,512,128]{2,1,0:T(8,128)(2,1)S(1)}, bf16[1,512,128]{2,1,0:T(8,128)(2,1)}, u32[]{:S(2)}) copy-start(bf16[1,512,128]{2,1,0:T(8,128)(2,1)} %get-tuple-element.76) | copy-start | bytes 393220
  95.9 44.0 %all-to-all-start = ((bf16[8,128,512]{2,1,0:T(8,128)(2,1)}), bf16[8,128,512]{2,1,0:T(8,128)(2,1)S(1)}, u32[]{:S(2)}, u32[]{:S(2)}) async-start(bf16[8,128,512]{2,1,0:T(8,128)(2,1)} %broadcast_select_fusion), calls=%async_computation | async-start | bytes 2097152 | tf_op jit(solution)/shard_map/all_to_all | solution.py:147
  99.5 31.7 %collective-permute-start.1 = (bf16[512,128]{1,0:T(8,128)(2,1)}, bf16[512,128]{1,0:T(8,128)(2,1)}, u32[]{:S(2)}, u32[]{:S(2)}) collective-permute-start(bf16[512,128]{1,0:T(8,128)(2,1)} %get-tuple-element.78), channel_id=1, source_target_pairs={{0,4},{4,8},{8,12},{12,16},{16,20},{20,24},{24,28},{1,5},{5,9},{9,... | collective-permute-start | bytes 393224 | tf_op jit(solution)/shard_map/ppermute | solution.py:15
  102.4 26.1 %collective-permute-start = (bf16[512,128]{1,0:T(8,128)(2,1)S(1)}, bf16[512,128]{1,0:T(8,128)(2,1)S(1)}, u32[]{:S(2)}, u32[]{:S(2)}) collective-permute-start(bf16[512,128]{1,0:T(8,128)(2,1)S(1)} %get-tuple-element.75), channel_id=1, source_target_pairs={{0,4},{4,8},{8,12},{12,16},{16,20},{20,24},{24,28},{1,5},{5,9},{9,... | collective-permute-start | bytes 393224 | tf_op jit(solution)/shard_map/ppermute | solution.py:15
  128.6 0.6 copy-start.14
  130.8 1.0 copy-start.8
  130.8 1.0 copy-start.11
  133.8 3.8 %copy-start = (bf16[512,1024]{0,1:T(8,128)(2,1)}, bf16[512,1024]{0,1:T(8,128)(2,1)S(1)}, u32[]{:S(2)}) copy-start(bf16[512,1024]{0,1:T(8,128)(2,1)S(1)} %fusion.3) | copy-start | bytes 3145732
  134.3 0.7 copy-start.2
  135.7 22.8 %collective-permute-start.2 = (bf16[512,128]{0,1:T(8,128)(2,1)}, bf16[512,128]{0,1:T(8,128)(2,1)}, u32[]{:S(2)}, u32[]{:S(2)}) collective-permute-start(bf16[512,128]{0,1:T(8,128)(2,1)} %fusion.22), channel_id=1, source_target_pairs={{4,0},{8,4},{12,8},{16,12},{20,16},{24,20},{28,24},{5,1},{9,5},{13... | collective-permute-start | bytes 393224 | tf_op jit(solution)/shard_map/ppermute | solution.py:15
  137.6 0.8 copy-start.4
  137.6 0.8 copy-start.6
  138.4 21.0 %collective-permute-start.3 = (bf16[512,128]{0,1:T(8,128)(2,1)}, bf16[512,128]{0,1:T(8,128)(2,1)}, u32[]{:S(2)}, u32[]{:S(2)}) collective-permute-start(bf16[512,128]{0,1:T(8,128)(2,1)} %fusion.21), channel_id=1, source_target_pairs={{4,0},{8,4},{12,8},{16,12},{20,16},{24,20},{28,24},{5,1},{9,5},{13... | collective-permute-start | bytes 393224 | tf_op jit(solution)/shard_map/ppermute | solution.py:15
  150.0 21.2 %all-to-all-start.1 = ((bf16[8,128,512]{2,1,0:T(8,128)(2,1)}), bf16[8,128,512]{2,1,0:T(8,128)(2,1)S(1)}, u32[]{:S(2)}, u32[]{:S(2)}) async-start(bf16[8,128,512]{2,1,0:T(8,128)(2,1)} %bitcast.102), calls=%async_computation.1 | async-start | bytes 2097152 | tf_op jit(solution)/shard_map/all_to_all | solution.py:174
  155.8 2.3 %copy-start.1 = (bf16[512,1024]{0,1:T(8,128)(2,1)S(1)}, bf16[512,1024]{0,1:T(8,128)(2,1)}, u32[]{:S(2)}) copy-start(bf16[512,1024]{0,1:T(8,128)(2,1)} %copy-done) | copy-start | bytes 3145732
  155.8 2.3 %copy-start.15 = (bf16[512,128]{1,0:T(8,128)(2,1)S(1)}, bf16[512,128]{1,0:T(8,128)(2,1)}, u32[]{:S(2)}) copy-start(bf16[512,128]{1,0:T(8,128)(2,1)} %copy-done.14) | copy-start | bytes 393220
  155.8 2.6 %copy-start.3 = (f32[512,128]{0,1:T(8,128)S(1)}, f32[512,128]{0,1:T(8,128)}, u32[]{:S(2)}) copy-start(f32[512,128]{0,1:T(8,128)} %copy-done.2) | copy-start | bytes 786436
  158.1 1.3 copy-start.5
  158.1 1.3 copy-start.7
  171.2 2.2 %copy-start.13 = (pred[512]{0:T(512)(128)(4,1)S(1)}, pred[512]{0:T(512)(128)(4,1)}, u32[]{:S(2)}) copy-start(pred[512]{0:T(512)(128)(4,1)} %compare_and_fusion) | copy-start | bytes 1540
  173.2 0.9 copy-start.12
where the time goes:
time: 178 us
  blocking collectives  69.6 us (39%)
  local copies, waits for them, and re-layouts  54.2 us (30%)
  starting transfers between devices  17.9 us (10%)
  other arithmetic  15.2 us (9%)
  waiting for transfers between devices  10.9 us (6%)
  matrix products  8.52 us (5%)
    all_gather x1, blocking collectives, on_device(): all_members = lax.all_gather(members, ('seq', 'head'), axis=0, tiled=True)  69.6 us
    scatter x1, local copies, waits for them, and re-layouts, on_device(): slot_rows = jnp.full((total,), tok_rows, jnp.int32).at[jnp.where(is_mine,...  15.5 us
    scatter x1, local copies, waits for them, and re-layouts, on_device(): home_slot = jnp.zeros((tok_rows,), jnp.int32).at[jnp.where(is_mine, local...  15.5 us
    all_to_all x1, waiting for transfers between devices, on_device(): lax.all_to_all(spread.reshape(shards, per_dev * capacity, res_width), 'se...  10.8 us
    ppermute x4, starting transfers between devices, from_behind(): return lax.ppermute(array, axis, pairs)  8.6 us
    unnamed x37, local copies, waits for them, and re-layouts  5.97 us
    all_to_all x1, starting transfers between devices, on_device(): lax.all_to_all(spread.reshape(shards, per_dev * capacity, res_width), 'se...  5.77 us
    gather x3, other arithmetic, on_device(): own_start = jnp.take_along_axis(starts, own_source, axis=1)  5.06 us
  transfers between devices with their start and end apart: 6, of which 1 were waited for; matrix products, arithmetic and copies ran while one was open for 25% of the time, Pallas kernels for 0%

commit v1 on v0

v1 whole, which is shorter than its diff:
```python
import functools
import math

import jax
import jax.numpy as jnp
from jax import lax
from jax.experimental import pallas as pl
from jax.experimental.pallas import tpu as pltpu
from jax.sharding import PartitionSpec as P

CLUS = 512
WINDOW = 512
F32 = jnp.float32
BF16 = jnp.bfloat16
NEG = -1e30
VMEM_LIMIT = 60 * 1024 * 1024

NN = (((1,), (0,)), ((), ()))
NT = (((1,), (1,)), ((), ()))
TN = (((0,), (0,)), ((), ()))


def dot(left, right, dims=NN):
    return lax.dot_general(left, right, dims, preferred_element_type=F32)


def call(body, outs, inputs, scratch=(), smem=(), flops=0, smem_outs=()):
    in_specs = [
        pl.BlockSpec(memory_space=pltpu.SMEM if i in smem else pltpu.VMEM)
        for i in range(len(inputs))
    ]
    out_specs = [
        pl.BlockSpec(memory_space=pltpu.SMEM if i in smem_outs else pltpu.VMEM)
        for i in range(len(outs))
    ]
    moved = sum(x.size * x.dtype.itemsize for x in list(inputs) + list(outs))
    return pl.pallas_call(
        body,
        out_shape=outs,
        in_specs=in_specs,
        out_specs=out_specs,
        scratch_shapes=list(scratch),
        compiler_params=pltpu.CompilerParams(vmem_limit_bytes=VMEM_LIMIT),
        cost_estimate=pl.CostEstimate(flops=flops, bytes_accessed=moved, transcendentals=0),
    )(*inputs)


def shape(*dims, dtype=BF16):
    return jax.ShapeDtypeStruct(dims, dtype)


def to_row(column):
    n = column.shape[0]
    same = lax.broadcasted_iota(jnp.int32, (n, n), 0) == lax.broadcasted_iota(jnp.int32, (n, n), 1)
    return jnp.sum(jnp.where(same, column, 0.0), axis=0, keepdims=True)


def window_queries(tok, hd, tile, me_ref, q_ref, k_ref, v_ref, g_ref, halo_ref, out_ref, dq_ref, st_ref, kx, vx):
    scale = 1.0 / math.sqrt(hd)
    kx[0:tok] = halo_ref[:, 0:hd]
    kx[tok:] = k_ref[:, 0:hd]
    vx[0:tok] = halo_ref[:, hd:]
    vx[tok:] = v_ref[:, 0:hd]
    first = jnp.where(me_ref[0] == 0, tok, 0)
    span = tok + tile
    row = lax.broadcasted_iota(jnp.int32, (tile, span), 0)
    col = lax.broadcasted_iota(jnp.int32, (tile, span), 1)
    st_ref[...] = jnp.zeros_like(st_ref)
    for r in range(tok // tile):
        lo = r * tile
        q = q_ref[lo : lo + tile, 0:hd]
        g = g_ref[lo : lo + tile, 0:hd]
        keys = kx[lo : lo + span]
        values = vx[lo : lo + span]
        allowed = (col > row) & (col <= row + tok) & (col + lo >= first)
        s = jnp.where(allowed, dot(q, keys, NT) * scale, NEG)
        top = jnp.max(s, axis=1, keepdims=True)
        e = jnp.exp(s - top)
        total = jnp.sum(e, axis=1, keepdims=True)
        p = e * (1.0 / total)
        out_ref[lo : lo + tile] = dot(p.astype(BF16), values).astype(BF16)
        dp = dot(g, values, NT)
        delta = jnp.sum(p * dp, axis=1, keepdims=True)
        ds = (p * (dp - delta) * scale).astype(BF16)
        dq_ref[lo : lo + tile] = dot(ds, keys).astype(BF16)
        st_ref[0:1, lo : lo + tile] = to_row(top + jnp.log(total))
        st_ref[1:2, lo : lo + tile] = to_row(delta)


def window_keys(tok, hd, tile, me_ref, q_ref, k_ref, v_ref, g_ref, halo_ref, st_ref, stn_ref, dk_ref, dv_ref, qx, gx):
    scale = 1.0 / math.sqrt(hd)
    qx[0:tok] = q_ref[:, 0:hd]
    qx[tok:] = halo_ref[:, 0:hd]
    gx[0:tok] = g_ref[:, 0:hd]
    gx[tok:] = halo_ref[:, hd:]
    last = jnp.where(me_ref[1] == 1, tok, 2 * tok)
    span = tok + tile
    row = lax.broadcasted_iota(jnp.int32, (tile, span), 0)
    col = lax.broadcasted_iota(jnp.int32, (tile, span), 1)
    for r in range(tok // tile):
        lo = r * tile
        k = k_ref[lo : lo + tile, 0:hd]
        v = v_ref[lo : lo + tile, 0:hd]
        queries = qx[lo : lo + span]
        grads = gx[lo : lo + span]
        stats = jnp.concatenate([st_ref[0:2, lo:], stn_ref[0:2, 0 : lo + tile]], axis=1)
        allowed = (col >= row) & (col < row + tok) & (col + lo < last)
        s = dot(k, queries, NT) * scale
        p = jnp.where(allowed, jnp.exp(jnp.where(allowed, s - stats[0:1], NEG)), 0.0)
        dv_ref[lo : lo + tile] = dot(p.astype(BF16), grads).astype(BF16)
        dp = dot(v, grads, NT)
        ds = (jnp.where(allowed, p * (dp - stats[1:2]), 0.0) * scale).astype(BF16)
        dk_ref[lo : lo + tile] = dot(ds, queries).astype(BF16)


def list_row(m, cfg, me_seq, me_head):
    row = m // cfg["per_row"]
    seq = row // cfg["heads"]
    head = row % cfg["heads"]
    mask = seq ^ me_seq
    at = (mask % 2) * (cfg["shards"] // 2 * cfg["heads"]) + (mask // 2) * cfg["heads"] + (head ^ me_head)
    return at, m % cfg["per_row"]


def make_tables(cfg, me_ref, lists_smem, src_tab, pos_tab, chunk_tab, count):
    shards, g, tok = cfg["shards"], cfg["g"], cfg["tok"]
    me_seq, me_head = me_ref[0], me_ref[2]
    for s in range(shards):
        count[s] = 0

    def step(m, carry):
        at, half = list_row(m, cfg, me_seq, me_head)
        s = lists_smem[at, half * g] // tok
        pos = count[s]
        count[s] = pos + 1
        src_tab[m] = s
        pos_tab[m] = pos
        chunk_tab[s * shards + pos] = m
        return carry

    lax.fori_loop(0, cfg["chunks"], step, 0)


def build_order(cfg, me_ref, lists_ref, chunk_tab, s, order_ref):
    shards, g, tok, per = cfg["shards"], cfg["g"], cfg["tok"], cfg["per"]
    sub = lax.broadcasted_iota(jnp.int32, (g, per), 0)
    lane = lax.broadcasted_iota(jnp.int32, (g, per), 1)
    token = lax.broadcasted_iota(jnp.int32, (g, tok), 1)

    def step(k, carry):
        m = chunk_tab[s * shards + k]
        at, half = list_row(m, cfg, me_ref[0], me_ref[2])
        row = lists_ref[pl.ds(at, 1), :] - s * tok
        picked = jnp.where(lane == sub + half * g, row, 0).astype(F32)
        column = jnp.sum(picked, axis=1, keepdims=True).astype(jnp.int32)
        order_ref[pl.ds(pl.multiple_of(k * g, g), g), :] = jnp.where(column == token, 1.0, 0.0).astype(BF16)
        return carry

    lax.fori_loop(0, shards, step, 0, unroll=min(shards, 8))


def place(cfg, chunk_tab, s, rows_ref, to_ref):
    shards, g = cfg["shards"], cfg["g"]

    def step(k, carry):
        m = chunk_tab[s * shards + k]
        to_ref[pl.ds(pl.multiple_of(m * g, g), g), :] = rows_ref[pl.ds(pl.multiple_of(k * g, g), g), :]
        return carry

    lax.fori_loop(0, shards, step, 0, unroll=min(shards, 8))


def cluster_queries(cfg, *refs):
    shards, g, tok, hd = cfg["shards"], cfg["g"], cfg["tok"], cfg["hd"]
    (me_ref, lists_smem, lists_ref, q_ref, k_ref, v_ref, g_ref, ow_ref, dqw_ref), refs = refs[:9], refs[9:]
    arrived, refs = refs[: shards - 1], refs[shards - 1 :]
    out_ref, dq_ref, st_ref, rows_ref, kv_ref, order_ref, src_tab, pos_tab, chunk_tab = refs[:9]
    count, order, sorted_rows, qg, stats, outs = refs[9:]
    scale = 1.0 / math.sqrt(hd)
    me = me_ref[0]
    make_tables(cfg, me_ref, lists_smem, src_tab, pos_tab, chunk_tab, count)
    build_order(cfg, me_ref, lists_ref, chunk_tab, me, order_ref)
    own_order = order_ref[...]
    qg[:, 0:hd] = dot(own_order, q_ref[:, hd:]).astype(BF16)
    qg[:, hd:] = dot(own_order, g_ref[:, hd:]).astype(BF16)
    kv_ref[:, 0:hd] = dot(own_order, k_ref[:, hd:]).astype(BF16)
    kv_ref[:, hd:] = dot(own_order, v_ref[:, hd:]).astype(BF16)
    place(cfg, chunk_tab, me, kv_ref, rows_ref)
    for mask in range(1, shards):
        s = me ^ mask
        build_order(cfg, me_ref, lists_ref, chunk_tab, s, order)
        sorted_rows[...] = dot(order[...], arrived[mask - 1][...]).astype(BF16)
        place(cfg, chunk_tab, s, sorted_rows, rows_ref)
    key_at = lax.broadcasted_iota(jnp.int32, (g, CLUS), 1)
    query_at = lax.broadcasted_iota(jnp.int32, (g, CLUS), 0)

    def step(k, carry):
        m = chunk_tab[me * shards + k]
        cluster = m // shards
        rank = (m % shards) * g
        mine = pl.ds(pl.multiple_of(k * g, g), g)
        whole = pl.ds(pl.multiple_of(cluster * CLUS, CLUS), CLUS)
        q = qg[mine, 0:hd]
        gr = qg[mine, hd:]
        keys = rows_ref[whole, 0:hd]
        values = rows_ref[whole, hd:]
        s = jnp.where(key_at <= query_at + rank, dot(q, keys, NT) * scale, NEG)
        top = jnp.max(s, axis=1, keepdims=True)
        e = jnp.exp(s - top)
        total = jnp.sum(e, axis=1, keepdims=True)
        p = e * (1.0 / total)
        outs[mine, 0:hd] = dot(p.astype(BF16), values).astype(BF16)
        dp = dot(gr, values, NT)
        delta = jnp.sum(p * dp, axis=1, keepdims=True)
        ds = (p * (dp - delta) * scale).astype(BF16)
        outs[mine, hd:] = dot(ds, keys).astype(BF16)
        stats[mine, 0:1] = top + jnp.log(total)
        stats[mine, 1:2] = delta
        return carry

    lax.fori_loop(0, shards, step, 0, unroll=min(shards, 4))
    back = dot(own_order, outs[...], TN).astype(BF16)
    out_ref[:, 0:hd] = ow_ref[...]
    out_ref[:, hd:] = back[:, 0:hd]
    dq_ref[:, 0:hd] = dqw_ref[...]
    dq_ref[:, hd:] = back[:, hd:]
    st_ref[...] = jnp.zeros_like(st_ref)
    for lo in range(0, tok, 128):
        st_ref[0:1, lo : lo + 128] = to_row(stats[lo : lo + 128, 0:1])
        st_ref[1:2, lo : lo + 128] = to_row(stats[lo : lo + 128, 1:2])
    place(cfg, chunk_tab, me, qg, rows_ref)


def cluster_keys(cfg, *refs):
    shards, g, tok, hd = cfg["shards"], cfg["g"], cfg["tok"], cfg["hd"]
    (me_ref, src_tab, pos_tab, chunk_tab, rows_ref, kv_ref, order_ref, dkw_ref, dvw_ref, st_ref), refs = refs[:10], refs[10:]
    arrived, refs = refs[: shards - 1], refs[shards - 1 :]
    dk_ref, dv_ref, columns, stats, outs = refs
    scale = 1.0 / math.sqrt(hd)
    me = me_ref[0]
    for mask in range(shards):
        s = me ^ mask
        st = st_ref if mask == 0 else arrived[mask - 1]
        columns[:, 0:8] = jnp.transpose(st[...])
        place(cfg, chunk_tab, s, columns, stats)
    query_at = lax.broadcasted_iota(jnp.int32, (CLUS, g), 0)
    key_at = lax.broadcasted_iota(jnp.int32, (CLUS, g), 1)

    def step(k, carry):
        m = chunk_tab[me * shards + k]
        cluster = m // shards
        rank = (m % shards) * g
        mine = pl.ds(pl.multiple_of(k * g, g), g)
        whole = pl.ds(pl.multiple_of(cluster * CLUS, CLUS), CLUS)
        keys = kv_ref[mine, 0:hd]
        values = kv_ref[mine, hd:]
        queries = rows_ref[whole, 0:hd]
        grads = rows_ref[whole, hd:]
        allowed = query_at >= key_at + rank
        s = dot(queries, keys, NT) * scale
        p = jnp.where(allowed, jnp.exp(jnp.where(allowed, s - stats[whole, 0:1], NEG)), 0.0)
        dp = dot(grads, values, NT)
        ds = (jnp.where(allowed, p * (dp - stats[whole, 1:2]), 0.0) * scale).astype(BF16)
        outs[mine, 0:hd] = dot(ds, queries, TN).astype(BF16)
        outs[mine, hd:] = dot(p.astype(BF16), grads, TN).astype(BF16)
        return carry

    lax.fori_loop(0, shards, step, 0, unroll=min(shards, 4))
    back = dot(order_ref[...], outs[...], TN).astype(BF16)
    dk_ref[:, 0:hd] = dkw_ref[...]
    dk_ref[:, hd:] = back[:, 0:hd]
    dv_ref[:, 0:hd] = dvw_ref[...]
    dv_ref[:, hd:] = back[:, hd:]


def partner(array, axis, mask):
    size = lax.axis_size(axis)
    return lax.ppermute(array, axis, [(i, i ^ mask) for i in range(size)])


def all_partners(pieces, shards):
    got = {1: partner(pieces[0], "seq", 1)}
    for mask in range(2, shards, 2):
        got[mask] = partner(pieces[mask.bit_length() - 1], "seq", mask)
    for mask in range(2, shards, 2):
        got[mask + 1] = partner(got[mask], "seq", 1)
    return [got[mask] for mask in range(1, shards)]


def on_device(query_rows, key_rows, value_rows, out_grad, members):
    tok, width = query_rows.shape
    hd = width // 2
    shards = lax.axis_size("seq")
    heads = lax.axis_size("head")
    me = lax.axis_index("seq")
    per = members.shape[0]
    total = per * shards * heads
    g = CLUS // shards
    cfg = dict(
        shards=shards, heads=heads, tok=tok, hd=hd, per=per, g=g, chunks=total // g, per_row=per // g
    )
    place_ref = jnp.stack([me, (me == shards - 1).astype(jnp.int32), lax.axis_index("head")])

    lists = members.reshape(1, per)
    lists = jnp.concatenate([lists] + [partner(lists, "head", mask) for mask in range(1, heads)], axis=0)
    lists = jnp.concatenate([lists] + [partner(lists, "seq", mask) for mask in range(2, shards, 2)], axis=0)
    lists = jnp.concatenate([lists, partner(lists, "seq", 1)], axis=0)

    key_side = jnp.concatenate([key_rows[:, hd:], value_rows[:, hd:]], axis=1)
    query_side = jnp.concatenate([query_rows[:, hd:], out_grad[:, hd:]], axis=1)
    pieces = [
        jnp.where((me >> bit) % 2 == 0, key_side, query_side) for bit in range(shards.bit_length() - 1)
    ]
    arrived = all_partners(pieces, shards)
    before = lax.ppermute(
        jnp.concatenate([key_rows[:, :hd], value_rows[:, :hd]], axis=1),
        "seq",
        [(i, i + 1) for i in range(shards - 1)],
    )
    after = lax.ppermute(
        jnp.concatenate([query_rows[:, :hd], out_grad[:, :hd]], axis=1),
        "seq",
        [(i + 1, i) for i in range(shards - 1)],
    )

    tile = 128
    half = shape(tok, hd)
    full = shape(tok, width)
    stat = shape(8, tok, dtype=F32)
    wide = 6 * 2 * tok * (tok + tile) * hd
    out_w, dq_w, st_w = call(
        functools.partial(window_queries, tok, hd, tile),
        [half, half, stat],
        [place_ref, query_rows, key_rows, value_rows, out_grad, before],
        scratch=[pltpu.VMEM((2 * tok, hd), BF16)] * 2,
        smem=(0,),
        flops=wide,
    )
    st_next = lax.ppermute(st_w, "seq", [(i + 1, i) for i in range(shards - 1)])
    table = shape(total // g, dtype=jnp.int32)
    attn_out, query_grad, st_c, rows, kv, order, src, pos, chunk = call(
        functools.partial(cluster_queries, cfg),
        [full, full, stat, shape(total, 2 * hd), full, shape(tok, tok), table, table, table],
        [place_ref, lists, lists, query_rows, key_rows, value_rows, out_grad, out_w, dq_w] + arrived,
        scratch=[
            pltpu.SMEM((shards,), jnp.int32),
            pltpu.VMEM((tok, tok), BF16),
            pltpu.VMEM((tok, 2 * hd), BF16),
            pltpu.VMEM((tok, 2 * hd), BF16),
            pltpu.VMEM((tok, 128), F32),
            pltpu.VMEM((tok, 2 * hd), BF16),
        ],
        smem=(0, 1),
        smem_outs=(6, 7, 8),
        flops=wide * 2,
    )
    st_all = all_partners([st_c] * (shards.bit_length() - 1), shards)
    dk_w, dv_w = call(
        functools.partial(window_keys, tok, hd, tile),
        [half, half],
        [place_ref, query_rows, key_rows, value_rows, out_grad, after, st_w, st_next],
        scratch=[pltpu.VMEM((2 * tok, hd), BF16)] * 2,
        smem=(0,),
        flops=wide,
    )
    key_grad, value_grad = call(
        functools.partial(cluster_keys, cfg),
        [full, full],
        [place_ref, src, pos, chunk, rows, kv, order, dk_w, dv_w, st_c] + st_all,
        scratch=[
            pltpu.VMEM((tok, 128), F32),
            pltpu.VMEM((total, 128), F32),
            pltpu.VMEM((tok, 2 * hd), BF16),
        ],
        smem=(0, 1, 2, 3),
        flops=wide,
    )
    return (attn_out, query_grad, key_grad, value_grad)


def solution(mesh):
    rows = P("seq", "head")
    return jax.shard_map(
        on_device,
        mesh=mesh,
        in_specs=(rows, rows, rows, rows, P(("seq", "head"))),
        out_specs=(rows, rows, rows, rows),
        check_vma=False,
    )
```

time: 178 us -> 82.3 us (0.46)
  blocking collectives: 69.6 us -> 0 us
  local copies, waits for them, and re-layouts: 54.2 us -> 6.19 us
  Pallas kernels: 0 us -> 29.4 us
  other arithmetic: 15.2 us -> 0.84 us
  starting transfers between devices: 17.9 us -> 30.5 us
  matrix products: 8.52 us -> 0 us
  waiting for transfers between devices: 10.9 us -> 13 us
    all_gather x1 -> x0, blocking collectives: 69.6 us -> none  [on_device(): all_members = lax.all_gather(members, ('seq', 'head'), axis=0, tiled=True)]
    scatter x3 -> x0, local copies, waits for them, and re-layouts: 34.6 us -> none  [the longest x1 15.5 us: on_device(): slot_rows = jnp.full((total,), tok_rows, jnp.int32).at[jnp.where(is_mine,...]
    pallas_call x0 -> x4, Pallas kernels: none -> 29.4 us  [call(): pl.pallas_call(body, out_shape=outs, in_specs=in_specs, out_specs=out_spe...]
    ppermute x4 -> x24, starting transfers between devices: 8.6 us -> 30.5 us  [the longest x21 26.6 us: partner(): return lax.ppermute(array, axis, [(i, i ^ mask) for i in range(size)])]
    ppermute x4 -> x24, waiting for transfers between devices: 0.01 us -> 13 us  [the longest x21 13 us: partner(): return lax.ppermute(array, axis, [(i, i ^ mask) for i in range(size)])]
    all_to_all x2 -> x0, waiting for transfers between devices: 10.8 us -> none  [the longest x1 10.8 us: on_device(): lax.all_to_all(spread.reshape(shards, per_dev * capacity, res_width), 'se...]
    gather x5 -> x0, local copies, waits for them, and re-layouts: 9.45 us -> none  [the longest x1 3.97 us: on_device(): jnp.take(jnp.concatenate([route_query, route_key, route_value, route_grad...]
    all_to_all x2 -> x0, starting transfers between devices: 9.33 us -> none  [the longest x1 5.77 us: on_device(): lax.all_to_all(spread.reshape(shards, per_dev * capacity, res_width), 'se...]
  transfers between devices with their start and end apart: 6 -> 24, of which waited for: 1 -> 7; matrix products, arithmetic and copies ran while one was open for 25% -> 3% of each run, Pallas kernels for 0% -> 28%
where the time goes in v1:
time: 82.3 us; the launch traced here: 81 us
  starting transfers between devices  30.5 us (37%)
  Pallas kernels  29.4 us (36%)
  waiting for transfers between devices  13 us (16%)
  local copies, waits for them, and re-layouts  6.19 us (8%)
  between operations  0.96 us (1%)
  other arithmetic  0.84 us (1%)
    pallas_call x4, Pallas kernels, call(): pl.pallas_call(body, out_shape=outs, in_specs=in_specs, out_specs=out_spe...  29.4 us
    ppermute x21, starting transfers between devices, partner(): return lax.ppermute(array, axis, [(i, i ^ mask) for i in range(size)])  26.6 us
    ppermute x21, waiting for transfers between devices, partner(): return lax.ppermute(array, axis, [(i, i ^ mask) for i in range(size)])  13 us
    unnamed x38, local copies, waits for them, and re-layouts  2.09 us
    concatenate x1, local copies, waits for them, and re-layouts, on_device(): lists = jnp.concatenate([lists, partner(lists, 'seq', 1)], axis=0)  1.79 us
  transfers between devices with their start and end apart: 24, of which 7 were waited for; matrix products, arithmetic and copies ran while one was open for 3% of the time, Pallas kernels for 28%

profile of v1, /device:TPU:0, one launch (start us, length us, event | category | flops | bytes accessed | tf_op | source)
XLA Modules:
  0.0 81.0 jit_solution(4018004728935601458)
XLA Ops:
  0.7 1.1 %fusion = (bf16[512,128]{1,0:T(8,128)(2,1)S(1)}, bf16[512,128]{1,0:T(8,128)(2,1)S(1)}, bf16[512,128]{1,0:T(8,128)(2,1)S(1)}, bf16[512,128]{1,0:T(8,128)(2,1)S(1)}) fusion(bf16[512,256]{1,0:T(8,128)(2,1)} %q_ref.3, bf16[512,256]{1,0:T(8,128)(2,1)} %g_ref.3), kind=kLoop, calls=%fused_computation.9 | loop fusion | bytes 1048576 | tf_op jit(solution)/shard_map/slice | solution.py:321
  1.8 1.1 %fusion.2 = (bf16[512,128]{1,0:T(8,128)(2,1)S(1)}, bf16[512,128]{1,0:T(8,128)(2,1)S(1)}, bf16[512,128]{1,0:T(8,128)(2,1)S(1)}, bf16[512,128]{1,0:T(8,128)(2,1)S(1)}) fusion(bf16[512,256]{1,0:T(8,128)(2,1)} %k_ref.3, bf16[512,256]{1,0:T(8,128)(2,1)} %v_ref.3), kind=kLoop, calls=%fused_computation.11 | loop fusion | bytes 1048576 | tf_op jit(solution)/shard_map/slice | solution.py:309
  3.0 0.2 broadcast_select_fusion
  3.1 3.0 %collective-permute-start.9 = (bf16[512,256]{1,0:T(8,128)(2,1)S(1)}, bf16[512,256]{1,0:T(8,128)(2,1)S(1)}, u32[]{:S(2)}, u32[]{:S(2)}) collective-permute-start(bf16[512,256]{1,0:T(8,128)(2,1)S(1)} %get-tuple-element.37), channel_id=1, source_target_pairs={{0,8},{4,12},{8,0},{12,4},{16,24},{20,28},{24,16},{28,20},{1,9},{5... | collective-permute-start | bytes 786440 | tf_op jit(solution)/shard_map/ppermute | solution.py:278
  6.1 1.5 %collective-permute-start.13 = (bf16[512,256]{1,0:T(8,128)(2,1)S(1)}, bf16[512,256]{1,0:T(8,128)(2,1)S(1)}, u32[]{:S(2)}, u32[]{:S(2)}) collective-permute-start(bf16[512,256]{1,0:T(8,128)(2,1)S(1)} %get-tuple-element.36), channel_id=1, source_target_pairs={{0,24},{4,28},{8,16},{12,20},{16,8},{20,12},{24,0},{28,4},{1,25},{... | collective-permute-start | bytes 786440 | tf_op jit(solution)/shard_map/ppermute | solution.py:278
  7.6 0.1 collective-permute-start.11
  7.7 1.3 %collective-permute-start.7 = (bf16[512,256]{1,0:T(8,128)(2,1)S(1)}, bf16[512,256]{1,0:T(8,128)(2,1)S(1)}, u32[]{:S(2)}, u32[]{:S(2)}) collective-permute-start(bf16[512,256]{1,0:T(8,128)(2,1)S(1)} %pad_maximum_fusion), channel_id=1, source_target_pairs={{0,4},{4,8},{8,12},{12,16},{16,20},{20,24},{24,28},{1,5},{5,9},{9,... | collective-permute-start | bytes 786440 | tf_op jit(solution)/shard_map/ppermute | solution.py:315
  9.0 4.1 %collective-permute-start.2 = (s32[1,128]{1,0:T(1,128)S(1)}, s32[1,128]{1,0:T(1,128)S(1)}, u32[]{:S(2)}, u32[]{:S(2)}) collective-permute-start(s32[1,128]{1,0:T(1,128)S(1)} %bitcast.4), channel_id=1, source_target_pairs={{0,3},{1,2},{2,1},{3,0},{4,7},{5,6},{6,5},{7,4},{8,11},{9,10},{10,... | collective-permute-start | bytes 1544 | tf_op jit(solution)/shard_map/ppermute | solution.py:278
  13.1 1.5 %collective-permute-done.2 = s32[1,128]{1,0:T(1,128)S(1)} collective-permute-done((s32[1,128]{1,0:T(1,128)S(1)}, s32[1,128]{1,0:T(1,128)S(1)}, u32[]{:S(2)}, u32[]{:S(2)}) %collective-permute-start.2) | collective-permute-done | bytes 544 | tf_op jit(solution)/shard_map/ppermute | solution.py:278
  14.7 1.0 %collective-permute-start.1 = (s32[1,128]{1,0:T(1,128)S(1)}, s32[1,128]{1,0:T(1,128)S(1)}, u32[]{:S(2)}, u32[]{:S(2)}) collective-permute-start(s32[1,128]{1,0:T(1,128)S(1)} %bitcast.5), channel_id=1, source_target_pairs={{0,2},{1,3},{2,0},{3,1},{4,6},{5,7},{6,4},{7,5},{8,10},{9,11},{10,... | collective-permute-start | bytes 1544 | tf_op jit(solution)/shard_map/ppermute | solution.py:278
  15.7 3.4 %collective-permute-done.1 = s32[1,128]{1,0:T(1,128)S(1)} collective-permute-done((s32[1,128]{1,0:T(1,128)S(1)}, s32[1,128]{1,0:T(1,128)S(1)}, u32[]{:S(2)}, u32[]{:S(2)}) %collective-permute-start.1) | collective-permute-done | bytes 544 | tf_op jit(solution)/shard_map/ppermute | solution.py:278
  19.1 1.5 %collective-permute-start = (s32[1,128]{1,0:T(1,128)S(1)}, s32[1,128]{1,0:T(1,128)S(1)}, u32[]{:S(2)}, u32[]{:S(2)}) collective-permute-start(s32[1,128]{1,0:T(1,128)S(1)} %bitcast.6), channel_id=1, source_target_pairs={{0,1},{1,0},{2,3},{3,2},{4,5},{5,4},{6,7},{7,6},{8,9},{9,8},{10,11... | collective-permute-start | bytes 1544 | tf_op jit(solution)/shard_map/ppermute | solution.py:278
  20.6 2.1 %collective-permute-done = s32[1,128]{1,0:T(1,128)S(1)} collective-permute-done((s32[1,128]{1,0:T(1,128)S(1)}, s32[1,128]{1,0:T(1,128)S(1)}, u32[]{:S(2)}, u32[]{:S(2)}) %collective-permute-start) | collective-permute-done | bytes 544 | tf_op jit(solution)/shard_map/ppermute | solution.py:278
  22.7 3.3 %collective-permute-start.5 = (s32[4,128]{1,0:T(4,128)S(1)}, s32[4,128]{1,0:T(4,128)S(1)}, u32[]{:S(2)}, u32[]{:S(2)}) collective-permute-start(s32[4,128]{1,0:T(4,128)S(1)} %pad_add_fusion), channel_id=1, source_target_pairs={{0,24},{4,28},{8,16},{12,20},{16,8},{20,12},{24,0},{28,4},{1,25},{... | collective-permute-start | bytes 6152 | tf_op jit(solution)/shard_map/ppermute | solution.py:278
  26.0 1.6 %collective-permute-done.5 = s32[4,128]{1,0:T(4,128)S(1)} collective-permute-done((s32[4,128]{1,0:T(4,128)S(1)}, s32[4,128]{1,0:T(4,128)S(1)}, u32[]{:S(2)}, u32[]{:S(2)}) %collective-permute-start.5) | collective-permute-done | bytes 2080 | tf_op jit(solution)/shard_map/ppermute | solution.py:278
  27.6 2.0 %collective-permute-start.4 = (s32[4,128]{1,0:T(4,128)S(1)}, s32[4,128]{1,0:T(4,128)S(1)}, u32[]{:S(2)}, u32[]{:S(2)}) collective-permute-start(s32[4,128]{1,0:T(4,128)S(1)} %pad_add_fusion), channel_id=1, source_target_pairs={{0,16},{4,20},{8,24},{12,28},{16,0},{20,4},{24,8},{28,12},{1,17},{... | collective-permute-start | bytes 6152 | tf_op jit(solution)/shard_map/ppermute | solution.py:278
  29.6 1.6 %collective-permute-done.4 = s32[4,128]{1,0:T(4,128)S(1)} collective-permute-done((s32[4,128]{1,0:T(4,128)S(1)}, s32[4,128]{1,0:T(4,128)S(1)}, u32[]{:S(2)}, u32[]{:S(2)}) %collective-permute-start.4) | collective-permute-done | bytes 2080 | tf_op jit(solution)/shard_map/ppermute | solution.py:278
  31.2 2.0 %collective-permute-start.3 = (s32[4,128]{1,0:T(4,128)S(1)}, s32[4,128]{1,0:T(4,128)S(1)}, u32[]{:S(2)}, u32[]{:S(2)}) collective-permute-start(s32[4,128]{1,0:T(4,128)S(1)} %pad_add_fusion), channel_id=1, source_target_pairs={{0,8},{4,12},{8,0},{12,4},{16,24},{20,28},{24,16},{28,20},{1,9},{5... | collective-permute-start | bytes 6152 | tf_op jit(solution)/shard_map/ppermute | solution.py:278
  33.1 1.6 %collective-permute-done.3 = s32[4,128]{1,0:T(4,128)S(1)} collective-permute-done((s32[4,128]{1,0:T(4,128)S(1)}, s32[4,128]{1,0:T(4,128)S(1)}, u32[]{:S(2)}, u32[]{:S(2)}) %collective-permute-start.3) | collective-permute-done | bytes 2080 | tf_op jit(solution)/shard_map/ppermute | solution.py:278
  34.8 0.1 collective-permute-start.6
  34.9 1.2 %collective-permute-done.6 = s32[16,128]{1,0:T(8,128)S(1)} collective-permute-done((s32[16,128]{1,0:T(8,128)S(1)}, s32[16,128]{1,0:T(8,128)S(1)}, u32[]{:S(2)}, u32[]{:S(2)}) %collective-permute-start.6) | collective-permute-done | bytes 8224 | tf_op jit(solution)/shard_map/ppermute | solution.py:278
  36.0 0.2 collective-permute-start.8
  36.2 0.3 collective-permute-start.10
  36.5 0.2 collective-permute-start.14
  36.7 0.3 collective-permute-start.12
  37.1 1.3 %collective-permute-start.15 = (bf16[512,256]{1,0:T(8,128)(2,1)S(1)}, bf16[512,256]{1,0:T(8,128)(2,1)S(1)}, u32[]{:S(2)}, u32[]{:S(2)}) collective-permute-start(bf16[512,256]{1,0:T(8,128)(2,1)S(1)} %pad_maximum_fusion.3), channel_id=1, source_target_pairs={{4,0},{8,4},{12,8},{16,12},{20,16},{24,20},{28,24},{5,1},{9,5},{13... | collective-permute-start | bytes 786440 | tf_op jit(solution)/shard_map/ppermute | solution.py:320
  38.4 0.6 pad_add_fusion.1.me_ref.refs_0_
  39.0 1.8 %concatenate.25.refs_1_.refs_2_ = s32[32,128]{1,0:T(8,128)} concatenate(s32[1,128]{1,0:T(1,128)S(1)} %bitcast.9, s32[1,128]{1,0:T(1,128)S(1)} %collective-permute-done, s32[1,128]{1,0:T(1,128)S(1)} %collective-permute-done.1, s32[1,128]{1,0:T(1,128)S(1)} %collective-permute-done.2, s32[4,128]{1,0:T(4,128)S(1)} %collective-permute-done.3, s32[4,128]{1,0:T(4,128)S(1)} %collective-permute-done.4, ...), dimensions={0} | concatenate | bytes 32768 | tf_op jit(solution)/shard_map/concatenate | solution.py:307
  40.8 4.9 %shard_map.84 = (bf16[512,128]{1,0:T(8,128)(2,1)}, bf16[512,128]{1,0:T(8,128)(2,1)}, f32[8,512]{1,0:T(8,128)}) custom-call(s32[3]{0:T(128)} %pad_add_fusion.1.me_ref.refs_0_, bf16[512,256]{1,0:T(8,128)(2,1)} %q_ref.3, bf16[512,256]{1,0:T(8,128)(2,1)} %k_ref.3, bf16[512,256]{1,0:T(8,128)(2,1)} %v_ref.3, bf16[512,256]{1,0:T(8,128)(2,1)} %g_ref.3, ...), custom_call_target="tpu_custom_call" | custom-call | flops 503316480 | bytes 1589260 | tf_op jit(solution)/shard_map/pallas_call | solution.py:37
  45.8 0.6 copy-done.13
  46.4 0.1 copy-done.14
  46.5 0.1 copy-done.15
  46.6 0.1 copy-done.16
  46.7 14.0 %shard_map.85 = (bf16[512,256]{1,0:T(8,128)(2,1)}, bf16[512,256]{1,0:T(8,128)(2,1)}, f32[8,512]{1,0:T(8,128)}, bf16[4096,256]{1,0:T(8,128)(2,1)}, bf16[512,256]{...) custom-call(s32[3]{0:T(128)} %pad_add_fusion.1.me_ref.refs_0_, ...), custom_call_target="tpu_custom_call" | custom-call | flops 1006632960 | bytes 6603532 | tf_op jit(solution)/shard_map/pallas_call | solution.py:37
  60.7 3.9 %collective-permute-start.22 = (f32[8,512]{1,0:T(8,128)}, f32[8,512]{1,0:T(8,128)S(1)}, u32[]{:S(2)}, u32[]{:S(2)}) collective-permute-start(f32[8,512]{1,0:T(8,128)} %get-tuple-element.33.refs_9_), channel_id=1, source_target_pairs={{0,24},{4,28},{8,16},{12,20},{16,8},{20,12},{24,0},{28,4},{1,25},{... | collective-permute-start | bytes 49160 | tf_op jit(solution)/shard_map/ppermute | solution.py:278
  64.6 0.2 collective-permute-start.20
  64.8 1.2 %collective-permute-start.18 = (f32[8,512]{1,0:T(8,128)}, f32[8,512]{1,0:T(8,128)S(1)}, u32[]{:S(2)}, u32[]{:S(2)}) collective-permute-start(f32[8,512]{1,0:T(8,128)} %get-tuple-element.33.refs_9_), channel_id=1, source_target_pairs={{0,8},{4,12},{8,0},{12,4},{16,24},{20,28},{24,16},{28,20},{1,9},{5... | collective-permute-start | bytes 49160 | tf_op jit(solution)/shard_map/ppermute | solution.py:278
  66.0 1.3 %collective-permute-start.16 = (f32[8,512]{1,0:T(8,128)S(1)}, f32[8,512]{1,0:T(8,128)S(1)}, u32[]{:S(2)}, u32[]{:S(2)}) collective-permute-start(f32[8,512]{1,0:T(8,128)S(1)} %copy-done.17), channel_id=1, source_target_pairs={{4,0},{8,4},{12,8},{16,12},{20,16},{24,20},{28,24},{5,1},{9,5},{13... | collective-permute-start | bytes 49160 | tf_op jit(solution)/shard_map/ppermute | solution.py:339
  67.3 1.2 %collective-permute-start.17 = (f32[8,512]{1,0:T(8,128)}, f32[8,512]{1,0:T(8,128)S(1)}, u32[]{:S(2)}, u32[]{:S(2)}) collective-permute-start(f32[8,512]{1,0:T(8,128)} %get-tuple-element.33.refs_9_), channel_id=1, source_target_pairs={{0,4},{4,0},{8,12},{12,8},{16,20},{20,16},{24,28},{28,24},{1,5},{5... | collective-permute-start | bytes 49160 | tf_op jit(solution)/shard_map/ppermute | solution.py:278
  68.5 0.1 collective-permute-start.23
  68.6 0.4 collective-permute-start.21
  69.1 0.1 collective-permute-start.19
  69.2 0.6 copy-done.18
  69.8 3.7 %shard_map.86 = (bf16[512,128]{1,0:T(8,128)(2,1)}, bf16[512,128]{1,0:T(8,128)(2,1)}) custom-call(s32[3]{0:T(128)} %pad_add_fusion.1.me_ref.refs_0_, bf16[512,256]{1,0:T(8,128)(2,1)} %q_ref.3, bf16[512,256]{1,0:T(8,128)(2,1)} %k_ref.3, bf16[512,256]{1,0:T(8,128)(2,1)} %v_ref.3, bf16[512,256]{1,0:T(8,128)(2,1)} %g_ref.3, bf16[512,256]{1,0:T(8,128)(2,1)} %copy-done.12, ...), custom_call_target="tpu_custom_call" | custom-call | flops 503316480 | bytes 1605644 | tf_op jit(solution)/shard_map/pallas_call | solution.py:37
  73.6 0.5 copy-done.3
  74.1 0.0 copy-done.5
  74.1 0.0 copy-done.6
  74.1 6.8 %shard_map.87 = (bf16[512,256]{1,0:T(8,128)(2,1)}, bf16[512,256]{1,0:T(8,128)(2,1)}) custom-call(s32[3]{0:T(128)} %pad_add_fusion.1.me_ref.refs_0_, s32[64]{0:T(128)} %get-tuple-element.24.refs_1_, s32[64]{0:T(128)} %get-tuple-element.25.refs_2_, s32[64]{0:T(128)} %get-tuple-element.26.refs_3_, bf16[4096,256]{1,0:T(8,128)(2,1)} %get-tuple-element.27.refs_4_, ...), custom_call_target="tpu_custom_call" | custom-call | flops 503316480 | bytes 3801868 | tf_op jit(solution)/shard_map/pallas_call | solution.py:37
  (51 shorter events, 0.2 us)
Async XLA Ops:
  0.6 8.4 %copy-start.7 = (s32[128]{0:T(128)S(1)}, s32[128]{0:T(128)}, u32[]{:S(2)}) copy-start(s32[128]{0:T(128)} %param.9) | copy-start | bytes 1540
  3.1 33.1 %collective-permute-start.9 = (bf16[512,256]{1,0:T(8,128)(2,1)S(1)}, bf16[512,256]{1,0:T(8,128)(2,1)S(1)}, u32[]{:S(2)}, u32[]{:S(2)}) collective-permute-start(bf16[512,256]{1,0:T(8,128)(2,1)S(1)} %get-tuple-element.37), channel_id=1, source_target_pairs={{0,8},{4,12},{8,0},{12,4},{16,24},{20,28},{24,16},{28,20},{1,9},{5... | collective-permute-start | bytes 786440 | tf_op jit(solution)/shard_map/ppermute | solution.py:278
  6.1 30.4 %collective-permute-start.13 = (bf16[512,256]{1,0:T(8,128)(2,1)S(1)}, bf16[512,256]{1,0:T(8,128)(2,1)S(1)}, u32[]{:S(2)}, u32[]{:S(2)}) collective-permute-start(bf16[512,256]{1,0:T(8,128)(2,1)S(1)} %get-tuple-element.36), channel_id=1, source_target_pairs={{0,24},{4,28},{8,16},{12,20},{16,8},{20,12},{24,0},{28,4},{1,25},{... | collective-permute-start | bytes 786440 | tf_op jit(solution)/shard_map/ppermute | solution.py:278
  7.6 29.1 %collective-permute-start.11 = (bf16[512,256]{1,0:T(8,128)(2,1)S(1)}, bf16[512,256]{1,0:T(8,128)(2,1)S(1)}, u32[]{:S(2)}, u32[]{:S(2)}) collective-permute-start(bf16[512,256]{1,0:T(8,128)(2,1)S(1)} %get-tuple-element.36), channel_id=1, source_target_pairs={{0,16},{4,20},{8,24},{12,28},{16,0},{20,4},{24,8},{28,12},{1,17},{... | collective-permute-start | bytes 786440 | tf_op jit(solution)/shard_map/ppermute | solution.py:278
  7.7 29.4 %collective-permute-start.7 = (bf16[512,256]{1,0:T(8,128)(2,1)S(1)}, bf16[512,256]{1,0:T(8,128)(2,1)S(1)}, u32[]{:S(2)}, u32[]{:S(2)}) collective-permute-start(bf16[512,256]{1,0:T(8,128)(2,1)S(1)} %pad_maximum_fusion), channel_id=1, source_target_pairs={{0,4},{4,8},{8,12},{12,16},{16,20},{20,24},{24,28},{1,5},{5,9},{9,... | collective-permute-start | bytes 786440 | tf_op jit(solution)/shard_map/ppermute | solution.py:315
  9.0 5.6 %collective-permute-start.2 = (s32[1,128]{1,0:T(1,128)S(1)}, s32[1,128]{1,0:T(1,128)S(1)}, u32[]{:S(2)}, u32[]{:S(2)}) collective-permute-start(s32[1,128]{1,0:T(1,128)S(1)} %bitcast.4), channel_id=1, source_target_pairs={{0,3},{1,2},{2,1},{3,0},{4,7},{5,6},{6,5},{7,4},{8,11},{9,10},{10,... | collective-permute-start | bytes 1544 | tf_op jit(solution)/shard_map/ppermute | solution.py:278
  14.7 4.4 %collective-permute-start.1 = (s32[1,128]{1,0:T(1,128)S(1)}, s32[1,128]{1,0:T(1,128)S(1)}, u32[]{:S(2)}, u32[]{:S(2)}) collective-permute-start(s32[1,128]{1,0:T(1,128)S(1)} %bitcast.5), channel_id=1, source_target_pairs={{0,2},{1,3},{2,0},{3,1},{4,6},{5,7},{6,4},{7,5},{8,10},{9,11},{10,... | collective-permute-start | bytes 1544 | tf_op jit(solution)/shard_map/ppermute | solution.py:278
  19.1 3.5 %collective-permute-start = (s32[1,128]{1,0:T(1,128)S(1)}, s32[1,128]{1,0:T(1,128)S(1)}, u32[]{:S(2)}, u32[]{:S(2)}) collective-permute-start(s32[1,128]{1,0:T(1,128)S(1)} %bitcast.6), channel_id=1, source_target_pairs={{0,1},{1,0},{2,3},{3,2},{4,5},{5,4},{6,7},{7,6},{8,9},{9,8},{10,11... | collective-permute-start | bytes 1544 | tf_op jit(solution)/shard_map/ppermute | solution.py:278
  22.7 4.9 %collective-permute-start.5 = (s32[4,128]{1,0:T(4,128)S(1)}, s32[4,128]{1,0:T(4,128)S(1)}, u32[]{:S(2)}, u32[]{:S(2)}) collective-permute-start(s32[4,128]{1,0:T(4,128)S(1)} %pad_add_fusion), channel_id=1, source_target_pairs={{0,24},{4,28},{8,16},{12,20},{16,8},{20,12},{24,0},{28,4},{1,25},{... | collective-permute-start | bytes 6152 | tf_op jit(solution)/shard_map/ppermute | solution.py:278
  27.6 3.6 %collective-permute-start.4 = (s32[4,128]{1,0:T(4,128)S(1)}, s32[4,128]{1,0:T(4,128)S(1)}, u32[]{:S(2)}, u32[]{:S(2)}) collective-permute-start(s32[4,128]{1,0:T(4,128)S(1)} %pad_add_fusion), channel_id=1, source_target_pairs={{0,16},{4,20},{8,24},{12,28},{16,0},{20,4},{24,8},{28,12},{1,17},{... | collective-permute-start | bytes 6152 | tf_op jit(solution)/shard_map/ppermute | solution.py:278
  31.2 3.6 %collective-permute-start.3 = (s32[4,128]{1,0:T(4,128)S(1)}, s32[4,128]{1,0:T(4,128)S(1)}, u32[]{:S(2)}, u32[]{:S(2)}) collective-permute-start(s32[4,128]{1,0:T(4,128)S(1)} %pad_add_fusion), channel_id=1, source_target_pairs={{0,8},{4,12},{8,0},{12,4},{16,24},{20,28},{24,16},{28,20},{1,9},{5... | collective-permute-start | bytes 6152 | tf_op jit(solution)/shard_map/ppermute | solution.py:278
  34.8 1.2 %collective-permute-start.6 = (s32[16,128]{1,0:T(8,128)S(1)}, s32[16,128]{1,0:T(8,128)S(1)}, u32[]{:S(2)}, u32[]{:S(2)}) collective-permute-start(s32[16,128]{1,0:T(8,128)S(1)} %concatenate.24), channel_id=1, source_target_pairs={{0,4},{4,0},{8,12},{12,8},{16,20},{20,16},{24,28},{28,24},{1,5},{5... | collective-permute-start | bytes 24584 | tf_op jit(solution)/shard_map/ppermute | solution.py:278
  36.0 9.7 %collective-permute-start.8 = (bf16[512,256]{1,0:T(8,128)(2,1)S(1)}, bf16[512,256]{1,0:T(8,128)(2,1)S(1)}, u32[]{:S(2)}, u32[]{:S(2)}) collective-permute-start(bf16[512,256]{1,0:T(8,128)(2,1)S(1)} %get-tuple-element.38), channel_id=1, source_target_pairs={{0,4},{4,0},{8,12},{12,8},{16,20},{20,16},{24,28},{28,24},{1,5},{5... | collective-permute-start | bytes 786440 | tf_op jit(solution)/shard_map/ppermute | solution.py:278
  36.2 9.6 %copy-start.8 = (bf16[512,256]{1,0:T(8,128)(2,1)}, bf16[512,256]{1,0:T(8,128)(2,1)S(1)}, u32[]{:S(2)}) copy-start(bf16[512,256]{1,0:T(8,128)(2,1)S(1)} %collective-permute-done.9.refs_10_) | copy-start | bytes 786436
  36.2 9.5 %collective-permute-start.10 = (bf16[512,256]{1,0:T(8,128)(2,1)S(1)}, bf16[512,256]{1,0:T(8,128)(2,1)S(1)}, u32[]{:S(2)}, u32[]{:S(2)}) collective-permute-start(bf16[512,256]{1,0:T(8,128)(2,1)S(1)} %collective-permute-done.9.refs_10_), channel_id=1, source_target_pairs={{0,4},{4,0},{8,12},{12,8},{16,20},{20,16},{24,28},{28,24},{1,5},{5... | collective-permute-start | bytes 786440 | tf_op jit(solution)/shard_map/ppermute | solution.py:278
  36.5 9.2 %copy-start.9 = (bf16[512,256]{1,0:T(8,128)(2,1)}, bf16[512,256]{1,0:T(8,128)(2,1)S(1)}, u32[]{:S(2)}) copy-start(bf16[512,256]{1,0:T(8,128)(2,1)S(1)} %collective-permute-done.13.refs_14_) | copy-start | bytes 786436
  36.5 9.2 %collective-permute-start.14 = (bf16[512,256]{1,0:T(8,128)(2,1)S(1)}, bf16[512,256]{1,0:T(8,128)(2,1)S(1)}, u32[]{:S(2)}, u32[]{:S(2)}) collective-permute-start(bf16[512,256]{1,0:T(8,128)(2,1)S(1)} %collective-permute-done.13.refs_14_), channel_id=1, source_target_pairs={{0,4},{4,0},{8,12},{12,8},{16,20},{20,16},{24,28},{28,24},{1,5},{5... | collective-permute-start | bytes 786440 | tf_op jit(solution)/shard_map/ppermute | solution.py:278
  36.7 9.1 %copy-start.10 = (bf16[512,256]{1,0:T(8,128)(2,1)}, bf16[512,256]{1,0:T(8,128)(2,1)S(1)}, u32[]{:S(2)}) copy-start(bf16[512,256]{1,0:T(8,128)(2,1)S(1)} %collective-permute-done.11.refs_12_) | copy-start | bytes 786436
  36.7 9.0 %collective-permute-start.12 = (bf16[512,256]{1,0:T(8,128)(2,1)S(1)}, bf16[512,256]{1,0:T(8,128)(2,1)S(1)}, u32[]{:S(2)}, u32[]{:S(2)}) collective-permute-start(bf16[512,256]{1,0:T(8,128)(2,1)S(1)} %collective-permute-done.11.refs_12_), channel_id=1, source_target_pairs={{0,4},{4,0},{8,12},{12,8},{16,20},{20,16},{24,28},{28,24},{1,5},{5... | collective-permute-start | bytes 786440 | tf_op jit(solution)/shard_map/ppermute | solution.py:278
  37.1 3.7 %copy-start.11 = (bf16[512,256]{1,0:T(8,128)(2,1)}, bf16[512,256]{1,0:T(8,128)(2,1)S(1)}, u32[]{:S(2)}) copy-start(bf16[512,256]{1,0:T(8,128)(2,1)S(1)} %collective-permute-done.7.halo_ref) | copy-start | bytes 786436
  37.1 30.2 %collective-permute-start.15 = (bf16[512,256]{1,0:T(8,128)(2,1)S(1)}, bf16[512,256]{1,0:T(8,128)(2,1)S(1)}, u32[]{:S(2)}, u32[]{:S(2)}) collective-permute-start(bf16[512,256]{1,0:T(8,128)(2,1)S(1)} %pad_maximum_fusion.3), channel_id=1, source_target_pairs={{4,0},{8,4},{12,8},{16,12},{20,16},{24,20},{28,24},{5,1},{9,5},{13... | collective-permute-start | bytes 786440 | tf_op jit(solution)/shard_map/ppermute | solution.py:320
  45.7 20.3 %copy-start.17 = (f32[8,512]{1,0:T(8,128)S(1)}, f32[8,512]{1,0:T(8,128)}, u32[]{:S(2)}) copy-start(f32[8,512]{1,0:T(8,128)} %get-tuple-element.30.st_ref) | copy-start | bytes 49156
  45.7 0.7 copy-start.13
  45.7 0.8 copy-start.14
  45.7 0.8 %copy-start.15 = (bf16[512,256]{1,0:T(8,128)(2,1)}, bf16[512,256]{1,0:T(8,128)(2,1)S(1)}, u32[]{:S(2)}) copy-start(bf16[512,256]{1,0:T(8,128)(2,1)S(1)} %collective-permute-done.14.refs_15_) | copy-start | bytes 786436
  45.7 0.9 %copy-start.16 = (bf16[512,256]{1,0:T(8,128)(2,1)}, bf16[512,256]{1,0:T(8,128)(2,1)S(1)}, u32[]{:S(2)}) copy-start(bf16[512,256]{1,0:T(8,128)(2,1)S(1)} %collective-permute-done.12.refs_13_) | copy-start | bytes 786436
  60.7 7.8 %collective-permute-start.22 = (f32[8,512]{1,0:T(8,128)}, f32[8,512]{1,0:T(8,128)S(1)}, u32[]{:S(2)}, u32[]{:S(2)}) collective-permute-start(f32[8,512]{1,0:T(8,128)} %get-tuple-element.33.refs_9_), channel_id=1, source_target_pairs={{0,24},{4,28},{8,16},{12,20},{16,8},{20,12},{24,0},{28,4},{1,25},{... | collective-permute-start | bytes 49160 | tf_op jit(solution)/shard_map/ppermute | solution.py:278
  64.6 4.0 %collective-permute-start.20 = (f32[8,512]{1,0:T(8,128)}, f32[8,512]{1,0:T(8,128)S(1)}, u32[]{:S(2)}, u32[]{:S(2)}) collective-permute-start(f32[8,512]{1,0:T(8,128)} %get-tuple-element.33.refs_9_), channel_id=1, source_target_pairs={{0,16},{4,20},{8,24},{12,28},{16,0},{20,4},{24,8},{28,12},{1,17},{... | collective-permute-start | bytes 49160 | tf_op jit(solution)/shard_map/ppermute | solution.py:278
  64.8 4.3 %collective-permute-start.18 = (f32[8,512]{1,0:T(8,128)}, f32[8,512]{1,0:T(8,128)S(1)}, u32[]{:S(2)}, u32[]{:S(2)}) collective-permute-start(f32[8,512]{1,0:T(8,128)} %get-tuple-element.33.refs_9_), channel_id=1, source_target_pairs={{0,8},{4,12},{8,0},{12,4},{16,24},{20,28},{24,16},{28,20},{1,9},{5... | collective-permute-start | bytes 49160 | tf_op jit(solution)/shard_map/ppermute | solution.py:278
  66.0 3.1 %collective-permute-start.16 = (f32[8,512]{1,0:T(8,128)S(1)}, f32[8,512]{1,0:T(8,128)S(1)}, u32[]{:S(2)}, u32[]{:S(2)}) collective-permute-start(f32[8,512]{1,0:T(8,128)S(1)} %copy-done.17), channel_id=1, source_target_pairs={{4,0},{8,4},{12,8},{16,12},{20,16},{24,20},{28,24},{5,1},{9,5},{13... | collective-permute-start | bytes 49160 | tf_op jit(solution)/shard_map/ppermute | solution.py:339
  67.3 1.8 %copy-start.12 = (bf16[512,256]{1,0:T(8,128)(2,1)}, bf16[512,256]{1,0:T(8,128)(2,1)S(1)}, u32[]{:S(2)}) copy-start(bf16[512,256]{1,0:T(8,128)(2,1)S(1)} %collective-permute-done.15.halo_ref) | copy-start | bytes 786436
  67.3 6.1 %collective-permute-start.17 = (f32[8,512]{1,0:T(8,128)}, f32[8,512]{1,0:T(8,128)S(1)}, u32[]{:S(2)}, u32[]{:S(2)}) collective-permute-start(f32[8,512]{1,0:T(8,128)} %get-tuple-element.33.refs_9_), channel_id=1, source_target_pairs={{0,4},{4,0},{8,12},{12,8},{16,20},{20,16},{24,28},{28,24},{1,5},{5... | collective-permute-start | bytes 49160 | tf_op jit(solution)/shard_map/ppermute | solution.py:278
  68.5 5.0 %copy-start = (f32[8,512]{1,0:T(8,128)}, f32[8,512]{1,0:T(8,128)S(1)}, u32[]{:S(2)}) copy-start(f32[8,512]{1,0:T(8,128)S(1)} %collective-permute-done.22.refs_15_) | copy-start | bytes 49156
  68.5 4.9 %collective-permute-start.23 = (f32[8,512]{1,0:T(8,128)S(1)}, f32[8,512]{1,0:T(8,128)S(1)}, u32[]{:S(2)}, u32[]{:S(2)}) collective-permute-start(f32[8,512]{1,0:T(8,128)S(1)} %collective-permute-done.22.refs_15_), channel_id=1, source_target_pairs={{0,4},{4,0},{8,12},{12,8},{16,20},{20,16},{24,28},{28,24},{1,5},{5... | collective-permute-start | bytes 49160 | tf_op jit(solution)/shard_map/ppermute | solution.py:278
  68.6 4.9 %copy-start.1 = (f32[8,512]{1,0:T(8,128)}, f32[8,512]{1,0:T(8,128)S(1)}, u32[]{:S(2)}) copy-start(f32[8,512]{1,0:T(8,128)S(1)} %collective-permute-done.20.refs_13_) | copy-start | bytes 49156
  68.6 4.9 %collective-permute-start.21 = (f32[8,512]{1,0:T(8,128)S(1)}, f32[8,512]{1,0:T(8,128)S(1)}, u32[]{:S(2)}, u32[]{:S(2)}) collective-permute-start(f32[8,512]{1,0:T(8,128)S(1)} %collective-permute-done.20.refs_13_), channel_id=1, source_target_pairs={{0,4},{4,0},{8,12},{12,8},{16,20},{20,16},{24,28},{28,24},{1,5},{5... | collective-permute-start | bytes 49160 | tf_op jit(solution)/shard_map/ppermute | solution.py:278
  69.1 4.5 %copy-start.2 = (f32[8,512]{1,0:T(8,128)}, f32[8,512]{1,0:T(8,128)S(1)}, u32[]{:S(2)}) copy-start(f32[8,512]{1,0:T(8,128)S(1)} %collective-permute-done.18.refs_11_) | copy-start | bytes 49156
  69.1 4.5 %collective-permute-start.19 = (f32[8,512]{1,0:T(8,128)S(1)}, f32[8,512]{1,0:T(8,128)S(1)}, u32[]{:S(2)}, u32[]{:S(2)}) collective-permute-start(f32[8,512]{1,0:T(8,128)S(1)} %collective-permute-done.18.refs_11_), channel_id=1, source_target_pairs={{0,4},{4,0},{8,12},{12,8},{16,20},{20,16},{24,28},{28,24},{1,5},{5... | collective-permute-start | bytes 49160 | tf_op jit(solution)/shard_map/ppermute | solution.py:278
  69.2 0.6 copy-start.18
  73.5 0.6 copy-start.3
  73.5 0.6 copy-start.4
  73.5 0.6 copy-start.5
  73.5 0.6 copy-start.6

commit v2 on v1

v2 whole, which is shorter than its diff:
```python
import functools
import math

import jax
import jax.numpy as jnp
from jax import lax
from jax.experimental import pallas as pl
from jax.experimental.pallas import tpu as pltpu
from jax.sharding import PartitionSpec as P

CLUS = 512
WINDOW = 512
F32 = jnp.float32
BF16 = jnp.bfloat16
NEG = -1e30
LANES = 128

NN = (((1,), (0,)), ((), ()))
NT = (((1,), (1,)), ((), ()))


def dot(left, right, dims=NN):
    return lax.dot_general(left, right, dims, preferred_element_type=F32)


def call(body, outs, inputs, scratch=(), smem=(), smem_outs=(), anywhere=(), us=0.0, aliases=None, vmem=8):
    def space(i, scalar):
        if i in scalar:
            return pltpu.SMEM
        return pl.ANY if i in anywhere else pltpu.VMEM

    moved = sum(x.size * x.dtype.itemsize for x in list(inputs) + list(outs))
    return pl.pallas_call(
        body,
        out_shape=outs,
        in_specs=[pl.BlockSpec(memory_space=space(i, smem)) for i in range(len(inputs))],
        out_specs=[
            pl.BlockSpec(memory_space=pltpu.SMEM if i in smem_outs else pltpu.VMEM) for i in range(len(outs))
        ],
        scratch_shapes=list(scratch),
        input_output_aliases=aliases or {},
        compiler_params=pltpu.CompilerParams(vmem_limit_bytes=vmem * 1024 * 1024),
        cost_estimate=pl.CostEstimate(flops=int(us * 1.15e9), bytes_accessed=moved, transcendentals=0),
    )(*inputs)


def shape(*dims, dtype=BF16):
    return jax.ShapeDtypeStruct(dims, dtype)


def to_row(column):
    n = column.shape[0]
    same = lax.broadcasted_iota(jnp.int32, (n, n), 0) == lax.broadcasted_iota(jnp.int32, (n, n), 1)
    return jnp.sum(jnp.where(same, column, 0.0), axis=0, keepdims=True)


def aligned(index, size):
    return pl.ds(pl.multiple_of(index * size, size), size)


def payloads(bits, hd, members_ref, q, k, v, g, *refs):
    kv_c, qg_c, kv_w, qg_w = refs[:4]
    pieces, (both, rim, spread, entries, sems) = refs[4 : 3 + bits], refs[3 + bits :]
    me = lax.axis_index("seq")
    width = 2 * hd
    copies = [pltpu.make_async_copy(members_ref, entries, sems.at[8])]
    for i, (source, target, lo, at) in enumerate(
        (
            (k, kv_c, hd, 0),
            (v, kv_c, hd, hd),
            (q, qg_c, hd, 0),
            (g, qg_c, hd, hd),
            (k, kv_w, 0, 0),
            (v, kv_w, 0, hd),
            (q, qg_w, 0, 0),
            (g, qg_w, 0, hd),
        )
    ):
        copies.append(
            pltpu.make_async_copy(source.at[:, lo : lo + hd], target.at[:, at : at + hd], sems.at[i])
        )
    for copy in copies:
        copy.start()
    copies[0].wait()
    spread[...] = jnp.broadcast_to(entries[...], spread.shape)
    for copy in copies[1:5]:
        copy.wait()

    def choose(bit, target, zero, one):
        low = ((me >> bit) & 1) == 0

        @pl.when(low)
        def _():
            target[:, 0:width] = zero[...]

        @pl.when(jnp.logical_not(low))
        def _():
            target[:, 0:width] = one[...]

    for bit in range(1, bits):
        choose(bit, pieces[bit - 1], kv_c, qg_c)
    choose(0, both, kv_c, qg_c)
    for copy in copies[5:]:
        copy.wait()
    choose(0, rim, qg_w, kv_w)
    both[:, width : 2 * width] = kv_w[...]
    both[:, 2 * width :] = qg_w[...]


def neighbour(parity, near_ref, block, far_ref, targets, at):
    tok, width = far_ref.shape
    hd = width // 2
    near = (lax.axis_index("seq") & 1) == parity

    @pl.when(near)
    def _():
        for i, target in enumerate(targets):
            lo = block * width + i * hd
            target[at : at + tok] = near_ref[:, lo : lo + hd]

    @pl.when(jnp.logical_not(near))
    def _():
        for i, target in enumerate(targets):
            target[at : at + tok] = far_ref[:, i * hd : (i + 1) * hd]


def window_rows(q, g, keys, values, allowed, scale):
    s = jnp.where(allowed, dot(q, keys, NT) * scale, NEG)
    dp = dot(g, values, NT)
    top = jnp.max(s, axis=1, keepdims=True)
    e = jnp.exp(s - top)
    total = jnp.sum(e, axis=1, keepdims=True)
    p = e * (1.0 / total)
    delta = jnp.sum(p * dp, axis=1, keepdims=True)
    return p, dp, to_row(top + jnp.log(total)), to_row(delta)


def window_queries(tok, hd, tile, kv_ref, qg_ref, near_ref, far_ref, out_ref, dq_ref, st_ref, kx, vx):
    scale = 1.0 / math.sqrt(hd)
    neighbour(1, near_ref, 1, far_ref, (kx, vx), 0)
    kx[tok:] = kv_ref[:, 0:hd]
    vx[tok:] = kv_ref[:, hd:]
    first = jnp.where(lax.axis_index("seq") == 0, tok, 0)
    span = tok + tile
    row = lax.broadcasted_iota(jnp.int32, (tile, span), 0)
    col = lax.broadcasted_iota(jnp.int32, (tile, span), 1)
    for lo in range(0, tok, tile):
        here = slice(lo, lo + tile)
        keys = kx[lo : lo + span]
        values = vx[lo : lo + span]
        allowed = (col > row) & (col <= row + tok) & (col + lo >= first)
        p, dp, top, delta = window_rows(
            qg_ref[here, 0:hd], qg_ref[here, hd:], keys, values, allowed, scale
        )
        st_ref[0:1, here] = top
        st_ref[1:2, here] = delta
        out_ref[here, 0:hd] = dot(p.astype(BF16), values).astype(BF16)
        delta = jnp.sum(p * dp, axis=1, keepdims=True)
        ds = (p * (dp - delta) * scale).astype(BF16)
        dq_ref[here, 0:hd] = dot(ds, keys).astype(BF16)


def window_keys(tok, hd, tile, kv_ref, qg_ref, near_ref, far_ref, far_keys, st_ref, dk_ref, dv_ref, kx, vx, qx, gx, stx):
    scale = 1.0 / math.sqrt(hd)
    neighbour(0, near_ref, 1, far_keys, (kx, vx), tok)
    neighbour(0, near_ref, 2, far_ref, (qx, gx), tok)
    kx[0:tok] = kv_ref[:, 0:hd]
    vx[0:tok] = kv_ref[:, hd:]
    qx[0:tok] = qg_ref[:, 0:hd]
    gx[0:tok] = qg_ref[:, hd:]
    stx[:, 0:tok] = st_ref[...]
    last = jnp.where(lax.axis_index("seq") == lax.axis_size("seq") - 1, tok, 2 * tok)
    span = tok + tile
    row = lax.broadcasted_iota(jnp.int32, (tile, span), 0)
    col = lax.broadcasted_iota(jnp.int32, (tile, span), 1)
    for lo in range(0, tok, tile):
        there = slice(tok + lo, tok + lo + tile)
        allowed = (col > row) & (col <= row + tok)
        _, _, top, delta = window_rows(
            qx[there], gx[there], kx[lo : lo + span], vx[lo : lo + span], allowed, scale
        )
        stx[0:1, there] = top
        stx[1:2, there] = delta
    for lo in range(0, tok, tile):
        here = slice(lo, lo + tile)
        queries = qx[lo : lo + span]
        grads = gx[lo : lo + span]
        allowed = (col >= row) & (col < row + tok) & (col + lo < last)
        s = dot(kx[here], queries, NT) * scale
        p = jnp.exp(jnp.where(allowed, s - stx[0:1, lo : lo + span], NEG))
        dv_ref[here] = dot(p.astype(BF16), grads).astype(BF16)
        dp = dot(vx[here], grads, NT)
        ds = (p * (dp - stx[1:2, lo : lo + span]) * scale).astype(BF16)
        dk_ref[here] = dot(ds, queries).astype(BF16)


def log2(n):
    return n.bit_length() - 1


def make_tables(cfg, lists_smem, src_tab, pos_tab, chunk_tab, count):
    shards, g, tok = cfg["shards"], cfg["g"], cfg["tok"]
    for s in range(shards):
        count[s] = 0

    def step(m, carry):
        s = lists_smem[m >> log2(cfg["per_row"]), (m & (cfg["per_row"] - 1)) * g] >> log2(tok)
        pos = count[s]
        count[s] = pos + 1
        src_tab[m] = s
        pos_tab[m] = pos
        chunk_tab[s * shards + pos] = m
        return carry

    lax.fori_loop(0, cfg["chunks"], step, 0, unroll=min(cfg["chunks"], 64))


def build_order(cfg, lists_ref, chunk_tab, s, order_ref):
    shards, g, tok, per = cfg["shards"], cfg["g"], cfg["tok"], cfg["per"]
    sub = lax.broadcasted_iota(jnp.int32, (g, per), 0)
    lane = lax.broadcasted_iota(jnp.int32, (g, per), 1)
    token = lax.broadcasted_iota(jnp.int32, (g, tok), 1)

    def step(k, carry):
        m = chunk_tab[s * shards + k]
        row = lists_ref[pl.ds(m >> log2(cfg["per_row"]), 1), :] - s * tok
        picked = jnp.where(lane == sub + (m & (cfg["per_row"] - 1)) * g, row, 0).astype(F32)
        column = jnp.sum(picked, axis=1, keepdims=True).astype(jnp.int32)
        order_ref[aligned(k, g), :] = jnp.where(column == token, 1.0, 0.0).astype(BF16)
        return carry

    lax.fori_loop(0, shards, step, 0, unroll=min(shards, 8))


def place(cfg, chunk_tab, s, rows_ref, to_ref):
    shards, g = cfg["shards"], cfg["g"]

    def step(k, carry):
        m = chunk_tab[s * shards + k]
        to_ref[aligned(m, g), :] = rows_ref[aligned(k, g), :]
        return carry

    lax.fori_loop(0, shards, step, 0, unroll=min(shards, 8))


def sort_blocks(cfg, lists_ref, chunk_tab, masks, arrived, rows_ref, orders, sorted_rows):
    for i, (mask, block) in enumerate(zip(masks, arrived)):
        s = lax.axis_index("seq") ^ mask
        order, rows = orders.at[i % 2], sorted_rows.at[i % 2]
        build_order(cfg, lists_ref, chunk_tab, s, order)
        rows[...] = dot(order[...], block[:, 0 : rows.shape[1]]).astype(BF16)
        place(cfg, chunk_tab, s, rows, rows_ref)


def sort_early(cfg, masks, *refs):
    (lists_smem, lists_ref, kv_in, qg_in), refs = refs[:4], refs[4:]
    arrived, refs = refs[: len(masks)], refs[len(masks) :]
    rows_ref, qg_ref, kv_ref, back_ref, src_tab, pos_tab, chunk_tab, count, orders, sorted_rows = refs
    me = lax.axis_index("seq")
    make_tables(cfg, lists_smem, src_tab, pos_tab, chunk_tab, count)
    build_order(cfg, lists_ref, chunk_tab, me, orders.at[0])
    own = orders[0]
    back_ref[...] = jnp.transpose(own)
    qg_ref[...] = dot(own, qg_in[...]).astype(BF16)
    kv_ref[...] = dot(own, kv_in[...]).astype(BF16)
    place(cfg, chunk_tab, me, kv_ref, rows_ref)
    sort_blocks(cfg, lists_ref, chunk_tab, masks, arrived, rows_ref, orders, sorted_rows)


def cluster_scores(cfg, masks, *refs):
    shards, g, hd = cfg["shards"], cfg["g"], cfg["hd"]
    (lists_ref, chunk_tab, qg_ref, rows_in), refs = refs[:4], refs[4:]
    arrived, refs = refs[: len(masks)], refs[len(masks) :]
    rows_ref, p_ref, ds_ref, st_ref, orders, sorted_rows = refs
    del rows_in
    scale = 1.0 / math.sqrt(hd)
    me = lax.axis_index("seq")
    sort_blocks(cfg, lists_ref, chunk_tab, masks, arrived, rows_ref, orders, sorted_rows)
    key_at = lax.broadcasted_iota(jnp.int32, (g, CLUS), 1)
    query_at = lax.broadcasted_iota(jnp.int32, (g, CLUS), 0)

    def step(k, carry):
        m = chunk_tab[me * shards + k]
        rank = (m & (shards - 1)) * g
        mine = aligned(k, g)
        whole = aligned(m >> log2(shards), CLUS)
        s = dot(qg_ref[mine, 0:hd], rows_ref[whole, 0:hd], NT) * scale
        dp = dot(qg_ref[mine, hd:], rows_ref[whole, hd:], NT)
        s = jnp.where(key_at <= query_at + rank, s, NEG)
        top = jnp.max(s, axis=1, keepdims=True)
        e = jnp.exp(s - top)
        total = jnp.sum(e, axis=1, keepdims=True)
        p = e * (1.0 / total)
        delta = jnp.sum(p * dp, axis=1, keepdims=True)
        p_ref[mine, :] = p.astype(BF16)
        ds_ref[mine, :] = (p * (dp - delta) * scale).astype(BF16)
        st_ref[pl.ds(k, 1), 0:g] = to_row(top + jnp.log(total))
        st_ref[pl.ds(shards + k, 1), 0:g] = to_row(delta)
        return carry

    lax.fori_loop(0, shards, step, 0, unroll=min(shards, 8))


def finish_queries(cfg, tile, *refs):
    shards, g, hd = cfg["shards"], cfg["g"], cfg["hd"]
    (chunk_tab, rows_ref, p_ref, ds_ref, back_ref), refs = refs[:5], refs[5:]
    kvw_ref, qgw_ref, near_ref, far_ref, out_ref, dq_ref, st_ref, outs, kx, vx = refs
    me = lax.axis_index("seq")

    def step(k, carry):
        m = chunk_tab[me * shards + k]
        mine = aligned(k, g)
        whole = aligned(m >> log2(shards), CLUS)
        outs[mine, 0:hd] = dot(p_ref[mine, :], rows_ref[whole, hd:]).astype(BF16)
        outs[mine, hd:] = dot(ds_ref[mine, :], rows_ref[whole, 0:hd]).astype(BF16)
        return carry

    lax.fori_loop(0, shards, step, 0, unroll=min(shards, 8))
    back = dot(back_ref[...], outs[...]).astype(BF16)
    out_ref[:, hd:] = back[:, 0:hd]
    dq_ref[:, hd:] = back[:, hd:]
    window_queries(cfg["tok"], hd, tile, kvw_ref, qgw_ref, near_ref, far_ref, out_ref, dq_ref, st_ref, kx, vx)


def cluster_keys(cfg, *refs):
    shards, g, hd = cfg["shards"], cfg["g"], cfg["hd"]
    (src_tab, pos_tab, chunk_tab, rows_in, qg_ref, kv_ref, back_ref, dkw_ref, dvw_ref, st_ref), refs = refs[:10], refs[10:]
    arrived, refs = refs[: shards - 1], refs[shards - 1 :]
    rows_ref, dk_ref, dv_ref, stats, outs = refs
    del rows_in
    scale = 1.0 / math.sqrt(hd)
    me = lax.axis_index("seq")
    place(cfg, chunk_tab, me, qg_ref, rows_ref)
    for mask in range(shards):
        st = st_ref if mask == 0 else arrived[mask - 1]
        stats[pl.ds(pl.multiple_of((me ^ mask) * 2 * shards, 2 * shards), 2 * shards), :] = st[...]
    query_at = lax.broadcasted_iota(jnp.int32, (g, CLUS), 1)
    key_at = lax.broadcasted_iota(jnp.int32, (g, CLUS), 0)

    def step(k, carry):
        m = chunk_tab[me * shards + k]
        first = m & ~(shards - 1)
        rank = (m & (shards - 1)) * g
        mine = aligned(k, g)
        whole = aligned(m >> log2(shards), CLUS)
        top, delta = [], []
        for j in range(shards):
            at = src_tab[first + j] * 2 * shards + pos_tab[first + j]
            top.append(stats[pl.ds(at, 1), 0:g])
            delta.append(stats[pl.ds(at + shards, 1), 0:g])
        queries = rows_ref[whole, 0:hd]
        grads = rows_ref[whole, hd:]
        s = dot(kv_ref[mine, 0:hd], queries, NT) * scale
        dp = dot(kv_ref[mine, hd:], grads, NT)
        allowed = query_at >= key_at + rank
        p = jnp.exp(jnp.where(allowed, s - jnp.concatenate(top, axis=1), NEG))
        ds = p * (dp - jnp.concatenate(delta, axis=1)) * scale
        outs[mine, 0:hd] = dot(ds.astype(BF16), queries).astype(BF16)
        outs[mine, hd:] = dot(p.astype(BF16), grads).astype(BF16)
        return carry

    lax.fori_loop(0, shards, step, 0, unroll=min(shards, 8))
    back = dot(back_ref[...], outs[...]).astype(BF16)
    dk_ref[:, 0:hd] = dkw_ref[...]
    dk_ref[:, hd:] = back[:, 0:hd]
    dv_ref[:, 0:hd] = dvw_ref[...]
    dv_ref[:, hd:] = back[:, hd:]


def partner(array, axis, mask):
    return lax.ppermute(array, axis, [(i, i ^ mask) for i in range(lax.axis_size(axis))])


def after(arrays, *earlier):
    return lax.optimization_barrier((arrays, earlier))[0]


def on_device(query_rows, key_rows, value_rows, out_grad, members):
    tok, width = query_rows.shape
    hd = width // 2
    shards = lax.axis_size("seq")
    heads = lax.axis_size("head")
    bits = log2(shards)
    me = lax.axis_index("seq")
    per = members.shape[0]
    total = per * shards * heads
    g = CLUS // shards
    cfg = dict(
        shards=shards, heads=heads, tok=tok, hd=hd, per=per, g=g, chunks=total // g, per_row=per // g
    )
    big = 2 if shards <= 8 else 4
    full = shape(tok, width)
    sides = [query_rows, key_rows, value_rows, out_grad]
    evens = list(range(2, shards, 2))

    kv_c, qg_c, kv_w, qg_w, *pieces, both, rim, spread = call(
        functools.partial(payloads, bits, hd),
        [full] * (bits + 3) + [shape(tok, 3 * width), full, shape(shards * heads, per, dtype=jnp.int32)],
        [pltpu.with_memory_space_constraint(x, pltpu.HBM) for x in [members.reshape(1, per)] + sides],
        scratch=[pltpu.VMEM((1, per), jnp.int32), pltpu.SemaphoreType.DMA((9,))],
        anywhere=(0, 1, 2, 3, 4),
        vmem=6 + bits,
    )
    got = {mask: partner(pieces[mask.bit_length() - 2], "seq", mask) for mask in evens}
    got[1] = partner(both, "seq", 1)
    lists = lax.all_to_all(after(spread, got[1]), ("seq", "head"), 0, 0, tiled=True)
    crossing = [(i, i + 1) for i in range(1, shards - 1, 2)] + [(shards - 1, 0)]
    crossing += [(b, a) for a, b in crossing]
    rim, rim_keys = after((rim, kv_w), lists)
    far = lax.ppermute(rim, "seq", crossing)
    far_keys = lax.ppermute(rim_keys, "seq", crossing)
    for mask in evens:
        got[mask + 1] = partner(after(got[mask], lists), "seq", 1)

    early = [1] + evens
    late = [mask + 1 for mask in evens]
    table = shape(total // g, dtype=jnp.int32)
    rows_shape = shape(total, 2 * hd)
    stat = shape(2 * shards, LANES, dtype=F32)
    orders = pltpu.VMEM((2, tok, tok), BF16)
    sorted_rows = pltpu.VMEM((2, tok, 2 * hd), BF16)

    rows, qg, kv, back, src, pos, chunk = call(
        functools.partial(sort_early, cfg, early),
        [rows_shape, full, full, shape(tok, tok), table, table, table],
        [lists, lists, kv_c, qg_c] + [got[mask] for mask in early],
        scratch=[pltpu.SMEM((shards,), jnp.int32), orders, sorted_rows],
        smem=(0,),
        smem_outs=(4, 5, 6),
        us=2.7,
        vmem=10 * big,
    )
    rows, p, ds, st_c = call(
        functools.partial(cluster_scores, cfg, late),
        [rows_shape, shape(tok, CLUS), shape(tok, CLUS), stat],
        [lists, chunk, qg, rows] + [got[mask] for mask in late],
        scratch=[orders, sorted_rows],
        smem=(1,),
        us=2.6,
        aliases={3: 0},
        vmem=6 * big,
    )
    tile = 256
    st = {mask: partner(st_c, "seq", mask) for mask in [1] + evens}
    attn_out, query_grad, st_w = call(
        functools.partial(finish_queries, cfg, tile),
        [full, full, shape(8, tok, dtype=F32)],
        [chunk, rows, p, ds, back, kv_w, qg_w, got[1], far],
        scratch=[pltpu.VMEM((tok, 2 * hd), BF16)] + [pltpu.VMEM((2 * tok, hd), BF16)] * 2,
        smem=(0,),
        us=3.7,
        vmem=5 * big,
    )
    for mask in evens:
        st[mask + 1] = partner(after(st[mask], st_w), "seq", 1)
    dk_w, dv_w = call(
        functools.partial(window_keys, tok, hd, tile),
        [shape(tok, hd)] * 2,
        [kv_w, qg_w, got[1], far, far_keys, st_w],
        scratch=[pltpu.VMEM((2 * tok, hd), BF16)] * 4 + [pltpu.VMEM((8, 2 * tok), F32)],
        us=2.1,
        vmem=10,
    )
    _, key_grad, value_grad = call(
        functools.partial(cluster_keys, cfg),
        [rows_shape, full, full],
        [src, pos, chunk, rows, qg, kv, back, dk_w, dv_w, st_c] + [st[mask] for mask in range(1, shards)],
        scratch=[pltpu.VMEM((2 * shards * shards, LANES), F32), pltpu.VMEM((tok, 2 * hd), BF16)],
        smem=(0, 1, 2),
        us=3.7,
        aliases={3: 0},
        vmem=4 * big,
    )
    return (attn_out, query_grad, key_grad, value_grad)


def solution(mesh):
    rows = P("seq", "head")
    return jax.shard_map(
        on_device,
        mesh=mesh,
        in_specs=(rows, rows, rows, rows, P(("seq", "head"))),
        out_specs=(rows, rows, rows, rows),
        check_vma=False,
    )
```

time: 82.3 us -> 43.8 us (0.53); the launches traced: 81 us -> 43.6 us
  Pallas kernels: 29.4 us -> 16.9 us
  starting transfers between devices: 30.5 us -> 18.7 us
  local copies, waits for them, and re-layouts: 6.19 us -> 0 us
  waiting for transfers between devices: 13 us -> 7.3 us
  other arithmetic: 0.84 us -> 0 us
    ppermute x24 -> x16, starting transfers between devices: 30.5 us -> 12.4 us  [the longest x14 9.78 us: partner(): lax.ppermute(array, axis, [(i, i ^ mask) for i in range(lax.axis_size(axi...]
    pallas_call x4 -> x6, Pallas kernels: 29.4 us -> 16.9 us  [call(): pl.pallas_call(body, out_shape=outs, in_specs=[pl.BlockSpec(memory_space=...]
    ppermute x24 -> x16, waiting for transfers between devices: 13 us -> 4.78 us  [the longest x14 4.78 us: partner(): lax.ppermute(array, axis, [(i, i ^ mask) for i in range(lax.axis_size(axi...]
    all_to_all x0 -> x1, starting transfers between devices: none -> 6.28 us  [on_device(): lax.all_to_all(after(spread, got[1]), ('seq', 'head'), 0, 0, tiled=True)]
    all_to_all x0 -> x1, waiting for transfers between devices: none -> 2.52 us  [on_device(): lax.all_to_all(after(spread, got[1]), ('seq', 'head'), 0, 0, tiled=True)]
    slice x2 -> x0, local copies, waits for them, and re-layouts: 2.27 us -> none  [the longest x1 1.13 us: on_device(): query_rows[:, :hd]]
    unnamed x38 -> x0, local copies, waits for them, and re-layouts: 2.09 us -> none
    concatenate x2 -> x0, local copies, waits for them, and re-layouts: 1.84 us -> none  [the longest x1 1.79 us: on_device(): lists = jnp.concatenate([lists, partner(lists, 'seq', 1)], axis=0)]
  transfers between devices with their start and end apart: 24 -> 17, of which waited for: 7 -> 2; matrix products, arithmetic and copies ran while one was open for 3% -> 0% of each run, Pallas kernels for 28% -> 26%
where the time goes in v2:
time: 43.8 us; the launch traced here: 43.6 us
  starting transfers between devices  18.7 us (43%)
  Pallas kernels  16.9 us (39%)
  waiting for transfers between devices  7.3 us (17%)
  between operations  0.74 us (2%)
    pallas_call x6, Pallas kernels, call(): pl.pallas_call(body, out_shape=outs, in_specs=[pl.BlockSpec(memory_space=...  16.9 us
    ppermute x14, starting transfers between devices, partner(): lax.ppermute(array, axis, [(i, i ^ mask) for i in range(lax.axis_size(axi...  9.78 us
    all_to_all x1, starting transfers between devices, on_device(): lax.all_to_all(after(spread, got[1]), ('seq', 'head'), 0, 0, tiled=True)  6.28 us
    ppermute x14, waiting for transfers between devices, partner(): lax.ppermute(array, axis, [(i, i ^ mask) for i in range(lax.axis_size(axi...  4.78 us
    all_to_all x1, waiting for transfers between devices, on_device(): lax.all_to_all(after(spread, got[1]), ('seq', 'head'), 0, 0, tiled=True)  2.52 us
    ppermute x1, starting transfers between devices, on_device(): far = lax.ppermute(rim, 'seq', crossing)  1.62 us
    ppermute x1, starting transfers between devices, on_device(): far_keys = lax.ppermute(rim_keys, 'seq', crossing)  1.03 us
  transfers between devices with their start and end apart: 17, of which 2 were waited for; matrix products, arithmetic and copies ran while one was open for 0% of the time, Pallas kernels for 26%

profile of v2, /device:TPU:0, one launch (start us, length us, event | category | flops | bytes accessed | tf_op | source)
XLA Modules:
  0.0 43.6 jit_solution(16605182141384701079)
XLA Ops:
  0.6 2.0 %shard_map.84 = (bf16[512,256]{1,0:T(8,128)(2,1)S(1)}, bf16[512,256]{1,0:T(8,128)(2,1)S(1)}, bf16[512,256]{1,0:T(8,128)(2,1)S(1)}, bf16[512,256]{1,0:T(8,128)(2,...) custom-call(s32[1,128]{1,0:T(1,128)} %bitcast.8, ...), custom_call_target="tpu_custom_call" | custom-call | bytes 3686912 | tf_op jit(solution)/shard_map/pallas_call | solution.py:33
  2.7 0.5 %collective-permute-start = (bf16[512,768]{1,0:T(8,128)(2,1)S(1)}, bf16[512,768]{1,0:T(8,128)(2,1)S(1)}, u32[]{:S(2)}, u32[]{:S(2)}) collective-permute-start(bf16[512,768]{1,0:T(8,128)(2,1)S(1)} %get-tuple-element.41), channel_id=1, source_target_pairs={{0,4},{4,0},{8,12},{12,8},{16,20},{20,16},{24,28},{28,24},{1,5},{5... | collective-permute-start | bytes 2359304 | tf_op jit(solution)/shard_map/ppermute | solution.py:371
  3.2 2.6 %collective-permute-start.2 = (bf16[512,256]{1,0:T(8,128)(2,1)S(1)}, bf16[512,256]{1,0:T(8,128)(2,1)S(1)}, u32[]{:S(2)}, u32[]{:S(2)}) collective-permute-start(bf16[512,256]{1,0:T(8,128)(2,1)S(1)} %get-tuple-element.46), channel_id=1, source_target_pairs={{0,16},{4,20},{8,24},{12,28},{16,0},{20,4},{24,8},{28,12},{1,17},{... | collective-permute-start | bytes 786440 | tf_op jit(solution)/shard_map/ppermute | solution.py:371
  5.8 1.4 %collective-permute-start.3 = (bf16[512,256]{1,0:T(8,128)(2,1)S(1)}, bf16[512,256]{1,0:T(8,128)(2,1)S(1)}, u32[]{:S(2)}, u32[]{:S(2)}) collective-permute-start(bf16[512,256]{1,0:T(8,128)(2,1)S(1)} %get-tuple-element.46), channel_id=1, source_target_pairs={{0,24},{4,28},{8,16},{12,20},{16,8},{20,12},{24,0},{28,4},{1,25},{... | collective-permute-start | bytes 786440 | tf_op jit(solution)/shard_map/ppermute | solution.py:371
  7.2 0.1 collective-permute-start.1
  7.3 0.0 collective-permute-done.refs_4_.refs_7_.near_ref
  7.3 6.3 %all-to-all-start = ((s32[32,1,128]{2,1,0:T(1,128)}), s32[32,1,128]{2,1,0:T(1,128)S(1)}, u32[]{:S(2)}, u32[]{:S(2)}) async-start(s32[32,1,128]{2,1,0:T(1,128)} %bitcast.2), calls=%async_computation | async-start | bytes 32768 | tf_op jit(solution)/shard_map/all_to_all | solution.py:406
  13.6 4.7 %collective-permute-done.2.refs_6_ = bf16[512,256]{1,0:T(8,128)(2,1)S(1)} collective-permute-done((bf16[512,256]{1,0:T(8,128)(2,1)S(1)}, bf16[512,256]{1,0:T(8,128)(2,1)S(1)}, u32[]{:S(2)}, u32[]{:S(2)}) %collective-permute-start.2) | collective-permute-done | bytes 262176 | tf_op jit(solution)/shard_map/ppermute | solution.py:371
  18.4 2.5 %all-to-all-done = s32[32,1,128]{2,1,0:T(1,128)S(1)} async-done(((s32[32,1,128]{2,1,0:T(1,128)}), s32[32,1,128]{2,1,0:T(1,128)S(1)}, u32[]{:S(2)}, u32[]{:S(2)}) %all-to-all-start) | async-done | bytes 16416 | tf_op jit(solution)/shard_map/all_to_all | solution.py:406
  20.9 0.0 collective-permute-start.5
  20.9 0.0 collective-permute-done.3.refs_7_
  20.9 0.5 %collective-permute-start.6 = (bf16[512,256]{1,0:T(8,128)(2,1)S(1)}, bf16[512,256]{1,0:T(8,128)(2,1)S(1)}, u32[]{:S(2)}, u32[]{:S(2)}) collective-permute-start(bf16[512,256]{1,0:T(8,128)(2,1)S(1)} %collective-permute-done.3.refs_7_), channel_id=1, source_target_pairs={{0,4},{4,0},{8,12},{12,8},{16,20},{20,16},{24,28},{28,24},{1,5},{5... | collective-permute-start | bytes 786440 | tf_op jit(solution)/shard_map/ppermute | solution.py:371
  21.4 0.0 collective-permute-done.1.refs_5_
  21.4 0.1 collective-permute-start.4
  21.5 1.6 %collective-permute-start.7 = (bf16[512,256]{1,0:T(8,128)(2,1)S(1)}, bf16[512,256]{1,0:T(8,128)(2,1)S(1)}, u32[]{:S(2)}, u32[]{:S(2)}) collective-permute-start(bf16[512,256]{1,0:T(8,128)(2,1)S(1)} %get-tuple-element.60), channel_id=1, source_target_pairs={{4,8},{12,16},{20,24},{28,0},{8,4},{16,12},{24,20},{0,28},{5,9},{1... | collective-permute-start | bytes 786440 | tf_op jit(solution)/shard_map/ppermute | solution.py:410
  23.1 1.0 %collective-permute-start.8 = (bf16[512,256]{1,0:T(8,128)(2,1)S(1)}, bf16[512,256]{1,0:T(8,128)(2,1)S(1)}, u32[]{:S(2)}, u32[]{:S(2)}) collective-permute-start(bf16[512,256]{1,0:T(8,128)(2,1)S(1)} %get-tuple-element.66.refs_5_.kv_ref), channel_id=1, source_target_pairs={{4,8},{12,16},{20,24},{28,0},{8,4},{16,12},{24,20},{0,28},{5,9},{1... | collective-permute-start | bytes 786440 | tf_op jit(solution)/shard_map/ppermute | solution.py:411
  24.1 2.7 %shard_map.85 = (bf16[4096,256]{1,0:T(8,128)(2,1)S(1)}, bf16[512,256]{1,0:T(8,128)(2,1)S(1)}, bf16[512,256]{1,0:T(8,128)(2,1)S(1)}, bf16[512,512]{1,0:T(8,128)(2...) custom-call(s32[32,128]{1,0:T(8,128)S(1)} %bitcast.5, s32[32,128]{1,0:T(8,128)S(1)} %bitcast.6, ...), custom_call_target="tpu_custom_call" | custom-call | flops 3104999936 | bytes 5276416 | tf_op jit(solution)/shard_map/pallas_call | solution.py:33
  26.8 0.0 collective-permute-done.5.refs_5_
  26.8 0.0 collective-permute-done.6.refs_6_
  26.8 0.0 collective-permute-done.4.refs_4_
  26.9 2.6 %shard_map.86 = (bf16[4096,256]{1,0:T(8,128)(2,1)S(1)}, bf16[512,512]{1,0:T(8,128)(2,1)S(1)}, bf16[512,512]{1,0:T(8,128)(2,1)S(1)}, f32[16,128]{1,0:T(8,128)S(1)}) custom-call(s32[32,128]{1,0:T(8,128)S(1)} %bitcast.7, s32[64]{0:T(128)S(1)} %get-tuple-element.47.refs_1_.refs_0_.refs_2_, ...), custom_call_target="tpu_custom_call", output_to_operand_aliasing={{0}: (3, {})} | custom-call | flops 2990000128 | bytes 6316288 | tf_op jit(solution)/shard_map/pallas_call | solution.py:33
  29.5 0.7 %collective-permute-start.14 = (f32[16,128]{1,0:T(8,128)S(1)}, f32[16,128]{1,0:T(8,128)S(1)}, u32[]{:S(2)}, u32[]{:S(2)}) collective-permute-start(f32[16,128]{1,0:T(8,128)S(1)} %get-tuple-element.70.refs_9_), channel_id=1, source_target_pairs={{0,24},{4,28},{8,16},{12,20},{16,8},{20,12},{24,0},{28,4},{1,25},{... | collective-permute-start | bytes 24584 | tf_op jit(solution)/shard_map/ppermute | solution.py:371
  30.2 1.4 %collective-permute-start.12 = (f32[16,128]{1,0:T(8,128)S(1)}, f32[16,128]{1,0:T(8,128)S(1)}, u32[]{:S(2)}, u32[]{:S(2)}) collective-permute-start(f32[16,128]{1,0:T(8,128)S(1)} %get-tuple-element.70.refs_9_), channel_id=1, source_target_pairs={{0,16},{4,20},{8,24},{12,28},{16,0},{20,4},{24,8},{28,12},{1,17},{... | collective-permute-start | bytes 24584 | tf_op jit(solution)/shard_map/ppermute | solution.py:371
  31.6 1.5 %collective-permute-start.10 = (f32[16,128]{1,0:T(8,128)S(1)}, f32[16,128]{1,0:T(8,128)S(1)}, u32[]{:S(2)}, u32[]{:S(2)}) collective-permute-start(f32[16,128]{1,0:T(8,128)S(1)} %get-tuple-element.70.refs_9_), channel_id=1, source_target_pairs={{0,8},{4,12},{8,0},{12,4},{16,24},{20,28},{24,16},{28,20},{1,9},{5... | collective-permute-start | bytes 24584 | tf_op jit(solution)/shard_map/ppermute | solution.py:371
  33.0 0.0 collective-permute-done.7.refs_8_.far_ref
  33.0 0.0 collective-permute-start.9
  33.0 3.7 %shard_map.87 = (bf16[512,256]{1,0:T(8,128)(2,1)}, bf16[512,256]{1,0:T(8,128)(2,1)}, f32[8,512]{1,0:T(8,128)S(1)}) custom-call(s32[64]{0:T(128)S(1)} %get-tuple-element.47.refs_1_.refs_0_.refs_2_, bf16[4096,256]{1,0:T(8,128)(2,1)S(1)} %get-tuple-element.53.refs_1_.refs_3_, bf16[512,512]{1,0:T(8,128)(2,1)S(1)} %get-tuple-element.54.refs_2_, ...), custom_call_target="tpu_custom_call" | custom-call | flops 4255000064 | bytes 5783808 | tf_op jit(solution)/shard_map/pallas_call | solution.py:33
  36.8 0.0 collective-permute-done.14.refs_15_
  36.8 0.5 %collective-permute-start.15 = (f32[16,128]{1,0:T(8,128)S(1)}, f32[16,128]{1,0:T(8,128)S(1)}, u32[]{:S(2)}, u32[]{:S(2)}) collective-permute-start(f32[16,128]{1,0:T(8,128)S(1)} %collective-permute-done.14.refs_15_), channel_id=1, source_target_pairs={{0,4},{4,0},{8,12},{12,8},{16,20},{20,16},{24,28},{28,24},{1,5},{5... | collective-permute-start | bytes 24584 | tf_op jit(solution)/shard_map/ppermute | solution.py:371
  37.2 0.0 collective-permute-done.12.refs_13_
  37.2 0.1 collective-permute-start.13
  37.3 0.0 collective-permute-done.10.refs_11_
  37.3 0.4 %collective-permute-start.11 = (f32[16,128]{1,0:T(8,128)S(1)}, f32[16,128]{1,0:T(8,128)S(1)}, u32[]{:S(2)}, u32[]{:S(2)}) collective-permute-start(f32[16,128]{1,0:T(8,128)S(1)} %collective-permute-done.10.refs_11_), channel_id=1, source_target_pairs={{0,4},{4,0},{8,12},{12,8},{16,20},{20,16},{24,28},{28,24},{1,5},{5... | collective-permute-start | bytes 24584 | tf_op jit(solution)/shard_map/ppermute | solution.py:371
  37.8 0.0 collective-permute-done.8.far_keys
  37.8 2.1 %shard_map.88 = (bf16[512,128]{1,0:T(8,128)(2,1)S(1)}, bf16[512,128]{1,0:T(8,128)(2,1)S(1)}) custom-call(bf16[512,256]{1,0:T(8,128)(2,1)S(1)} %get-tuple-element.66.refs_5_.kv_ref, bf16[512,256]{1,0:T(8,128)(2,1)S(1)} %get-tuple-element.58.refs_6_.qg_ref, bf16[512,768]{1,0:T(8,128)(2,1)S(1)} %collective-permute-done.refs_4_.refs_7_.near_ref, ...), custom_call_target="tpu_custom_call" | custom-call | flops 2415000064 | bytes 2113536 | tf_op jit(solution)/shard_map/pallas_call | solution.py:33
  39.9 0.0 collective-permute-done.9.refs_10_
  39.9 0.0 collective-permute-done.15.refs_16_
  39.9 0.0 collective-permute-done.13.refs_14_
  39.9 0.0 collective-permute-done.11.refs_12_
  39.9 3.7 %shard_map.89 = (bf16[4096,256]{1,0:T(8,128)(2,1)S(1)}, bf16[512,256]{1,0:T(8,128)(2,1)}, bf16[512,256]{1,0:T(8,128)(2,1)}) custom-call(s32[64]{0:T(128)S(1)} %get-tuple-element.63.refs_0_, s32[64]{0:T(128)S(1)} %get-tuple-element.64.refs_1_, s32[64]{0:T(128)S(1)} %get-tuple-element.47.refs_1_.refs_0_.refs_2_, ...), custom_call_target="tpu_custom_call", output_to_operand_aliasing={{0}: (3, {})} | custom-call | flops 4255000064 | bytes 6095616 | tf_op jit(solution)/shard_map/pallas_call | solution.py:33
Async XLA Ops:
  2.7 4.7 %collective-permute-start = (bf16[512,768]{1,0:T(8,128)(2,1)S(1)}, bf16[512,768]{1,0:T(8,128)(2,1)S(1)}, u32[]{:S(2)}, u32[]{:S(2)}) collective-permute-start(bf16[512,768]{1,0:T(8,128)(2,1)S(1)} %get-tuple-element.41), channel_id=1, source_target_pairs={{0,4},{4,0},{8,12},{12,8},{16,20},{20,16},{24,28},{28,24},{1,5},{5... | collective-permute-start | bytes 2359304 | tf_op jit(solution)/shard_map/ppermute | solution.py:371
  3.2 15.2 %collective-permute-start.2 = (bf16[512,256]{1,0:T(8,128)(2,1)S(1)}, bf16[512,256]{1,0:T(8,128)(2,1)S(1)}, u32[]{:S(2)}, u32[]{:S(2)}) collective-permute-start(bf16[512,256]{1,0:T(8,128)(2,1)S(1)} %get-tuple-element.46), channel_id=1, source_target_pairs={{0,16},{4,20},{8,24},{12,28},{16,0},{20,4},{24,8},{28,12},{1,17},{... | collective-permute-start | bytes 786440 | tf_op jit(solution)/shard_map/ppermute | solution.py:371
  5.8 15.1 %collective-permute-start.3 = (bf16[512,256]{1,0:T(8,128)(2,1)S(1)}, bf16[512,256]{1,0:T(8,128)(2,1)S(1)}, u32[]{:S(2)}, u32[]{:S(2)}) collective-permute-start(bf16[512,256]{1,0:T(8,128)(2,1)S(1)} %get-tuple-element.46), channel_id=1, source_target_pairs={{0,24},{4,28},{8,16},{12,20},{16,8},{20,12},{24,0},{28,4},{1,25},{... | collective-permute-start | bytes 786440 | tf_op jit(solution)/shard_map/ppermute | solution.py:371
  7.2 14.2 %collective-permute-start.1 = (bf16[512,256]{1,0:T(8,128)(2,1)S(1)}, bf16[512,256]{1,0:T(8,128)(2,1)S(1)}, u32[]{:S(2)}, u32[]{:S(2)}) collective-permute-start(bf16[512,256]{1,0:T(8,128)(2,1)S(1)} %get-tuple-element.45), channel_id=1, source_target_pairs={{0,8},{4,12},{8,0},{12,4},{16,24},{20,28},{24,16},{28,20},{1,9},{5... | collective-permute-start | bytes 786440 | tf_op jit(solution)/shard_map/ppermute | solution.py:371
  7.3 13.5 %all-to-all-start = ((s32[32,1,128]{2,1,0:T(1,128)}), s32[32,1,128]{2,1,0:T(1,128)S(1)}, u32[]{:S(2)}, u32[]{:S(2)}) async-start(s32[32,1,128]{2,1,0:T(1,128)} %bitcast.2), calls=%async_computation | async-start | bytes 32768 | tf_op jit(solution)/shard_map/all_to_all | solution.py:406
  20.9 6.0 %collective-permute-start.5 = (bf16[512,256]{1,0:T(8,128)(2,1)S(1)}, bf16[512,256]{1,0:T(8,128)(2,1)S(1)}, u32[]{:S(2)}, u32[]{:S(2)}) collective-permute-start(bf16[512,256]{1,0:T(8,128)(2,1)S(1)} %collective-permute-done.2.refs_6_), channel_id=1, source_target_pairs={{0,4},{4,0},{8,12},{12,8},{16,20},{20,16},{24,28},{28,24},{1,5},{5... | collective-permute-start | bytes 786440 | tf_op jit(solution)/shard_map/ppermute | solution.py:371
  20.9 6.0 %collective-permute-start.6 = (bf16[512,256]{1,0:T(8,128)(2,1)S(1)}, bf16[512,256]{1,0:T(8,128)(2,1)S(1)}, u32[]{:S(2)}, u32[]{:S(2)}) collective-permute-start(bf16[512,256]{1,0:T(8,128)(2,1)S(1)} %collective-permute-done.3.refs_7_), channel_id=1, source_target_pairs={{0,4},{4,0},{8,12},{12,8},{16,20},{20,16},{24,28},{28,24},{1,5},{5... | collective-permute-start | bytes 786440 | tf_op jit(solution)/shard_map/ppermute | solution.py:371
  21.4 5.5 %collective-permute-start.4 = (bf16[512,256]{1,0:T(8,128)(2,1)S(1)}, bf16[512,256]{1,0:T(8,128)(2,1)S(1)}, u32[]{:S(2)}, u32[]{:S(2)}) collective-permute-start(bf16[512,256]{1,0:T(8,128)(2,1)S(1)} %collective-permute-done.1.refs_5_), channel_id=1, source_target_pairs={{0,4},{4,0},{8,12},{12,8},{16,20},{20,16},{24,28},{28,24},{1,5},{5... | collective-permute-start | bytes 786440 | tf_op jit(solution)/shard_map/ppermute | solution.py:371
  21.5 11.5 %collective-permute-start.7 = (bf16[512,256]{1,0:T(8,128)(2,1)S(1)}, bf16[512,256]{1,0:T(8,128)(2,1)S(1)}, u32[]{:S(2)}, u32[]{:S(2)}) collective-permute-start(bf16[512,256]{1,0:T(8,128)(2,1)S(1)} %get-tuple-element.60), channel_id=1, source_target_pairs={{4,8},{12,16},{20,24},{28,0},{8,4},{16,12},{24,20},{0,28},{5,9},{1... | collective-permute-start | bytes 786440 | tf_op jit(solution)/shard_map/ppermute | solution.py:410
  23.1 14.7 %collective-permute-start.8 = (bf16[512,256]{1,0:T(8,128)(2,1)S(1)}, bf16[512,256]{1,0:T(8,128)(2,1)S(1)}, u32[]{:S(2)}, u32[]{:S(2)}) collective-permute-start(bf16[512,256]{1,0:T(8,128)(2,1)S(1)} %get-tuple-element.66.refs_5_.kv_ref), channel_id=1, source_target_pairs={{4,8},{12,16},{20,24},{28,0},{8,4},{16,12},{24,20},{0,28},{5,9},{1... | collective-permute-start | bytes 786440 | tf_op jit(solution)/shard_map/ppermute | solution.py:411
  29.5 7.3 %collective-permute-start.14 = (f32[16,128]{1,0:T(8,128)S(1)}, f32[16,128]{1,0:T(8,128)S(1)}, u32[]{:S(2)}, u32[]{:S(2)}) collective-permute-start(f32[16,128]{1,0:T(8,128)S(1)} %get-tuple-element.70.refs_9_), channel_id=1, source_target_pairs={{0,24},{4,28},{8,16},{12,20},{16,8},{20,12},{24,0},{28,4},{1,25},{... | collective-permute-start | bytes 24584 | tf_op jit(solution)/shard_map/ppermute | solution.py:371
  30.2 7.0 %collective-permute-start.12 = (f32[16,128]{1,0:T(8,128)S(1)}, f32[16,128]{1,0:T(8,128)S(1)}, u32[]{:S(2)}, u32[]{:S(2)}) collective-permute-start(f32[16,128]{1,0:T(8,128)S(1)} %get-tuple-element.70.refs_9_), channel_id=1, source_target_pairs={{0,16},{4,20},{8,24},{12,28},{16,0},{20,4},{24,8},{28,12},{1,17},{... | collective-permute-start | bytes 24584 | tf_op jit(solution)/shard_map/ppermute | solution.py:371
  31.6 5.8 %collective-permute-start.10 = (f32[16,128]{1,0:T(8,128)S(1)}, f32[16,128]{1,0:T(8,128)S(1)}, u32[]{:S(2)}, u32[]{:S(2)}) collective-permute-start(f32[16,128]{1,0:T(8,128)S(1)} %get-tuple-element.70.refs_9_), channel_id=1, source_target_pairs={{0,8},{4,12},{8,0},{12,4},{16,24},{20,28},{24,16},{28,20},{1,9},{5... | collective-permute-start | bytes 24584 | tf_op jit(solution)/shard_map/ppermute | solution.py:371
  33.0 6.9 %collective-permute-start.9 = (f32[16,128]{1,0:T(8,128)S(1)}, f32[16,128]{1,0:T(8,128)S(1)}, u32[]{:S(2)}, u32[]{:S(2)}) collective-permute-start(f32[16,128]{1,0:T(8,128)S(1)} %get-tuple-element.70.refs_9_), channel_id=1, source_target_pairs={{0,4},{4,0},{8,12},{12,8},{16,20},{20,16},{24,28},{28,24},{1,5},{5... | collective-permute-start | bytes 24584 | tf_op jit(solution)/shard_map/ppermute | solution.py:371
  36.8 3.1 %collective-permute-start.15 = (f32[16,128]{1,0:T(8,128)S(1)}, f32[16,128]{1,0:T(8,128)S(1)}, u32[]{:S(2)}, u32[]{:S(2)}) collective-permute-start(f32[16,128]{1,0:T(8,128)S(1)} %collective-permute-done.14.refs_15_), channel_id=1, source_target_pairs={{0,4},{4,0},{8,12},{12,8},{16,20},{20,16},{24,28},{28,24},{1,5},{5... | collective-permute-start | bytes 24584 | tf_op jit(solution)/shard_map/ppermute | solution.py:371
  37.2 2.6 %collective-permute-start.13 = (f32[16,128]{1,0:T(8,128)S(1)}, f32[16,128]{1,0:T(8,128)S(1)}, u32[]{:S(2)}, u32[]{:S(2)}) collective-permute-start(f32[16,128]{1,0:T(8,128)S(1)} %collective-permute-done.12.refs_13_), channel_id=1, source_target_pairs={{0,4},{4,0},{8,12},{12,8},{16,20},{20,16},{24,28},{28,24},{1,5},{5... | collective-permute-start | bytes 24584 | tf_op jit(solution)/shard_map/ppermute | solution.py:371
  37.3 2.6 %collective-permute-start.11 = (f32[16,128]{1,0:T(8,128)S(1)}, f32[16,128]{1,0:T(8,128)S(1)}, u32[]{:S(2)}, u32[]{:S(2)}) collective-permute-start(f32[16,128]{1,0:T(8,128)S(1)} %collective-permute-done.10.refs_11_), channel_id=1, source_target_pairs={{0,4},{4,0},{8,12},{12,8},{16,20},{20,16},{24,28},{28,24},{1,5},{5... | collective-permute-start | bytes 24584 | tf_op jit(solution)/shard_map/ppermute | solution.py:371

commit v3 on v2

v3 whole, which is shorter than its diff:
```python
import functools
import math

import jax
import jax.numpy as jnp
from jax import lax
from jax.experimental import pallas as pl
from jax.experimental.pallas import tpu as pltpu
from jax.sharding import PartitionSpec as P

CLUS = 512
WINDOW = 512
F32 = jnp.float32
BF16 = jnp.bfloat16
NEG = -1e30
LANES = 128

NN = (((1,), (0,)), ((), ()))
NT = (((1,), (1,)), ((), ()))


def dot(left, right, dims=NN):
    return lax.dot_general(left, right, dims, preferred_element_type=F32)


def call(body, outs, inputs, scratch=(), smem=(), hbm_outs=(), anywhere=(), us=0.0, aliases=None, vmem=8):
    def space(i, scalar):
        if i in scalar:
            return pltpu.SMEM
        return pl.ANY if i in anywhere else pltpu.VMEM

    moved = sum(x.size * x.dtype.itemsize for x in list(inputs) + list(outs))
    return pl.pallas_call(
        body,
        out_shape=outs,
        in_specs=[pl.BlockSpec(memory_space=space(i, smem)) for i in range(len(inputs))],
        out_specs=[
            pl.BlockSpec(memory_space=pl.ANY if i in hbm_outs else pltpu.VMEM) for i in range(len(outs))
        ],
        scratch_shapes=list(scratch),
        input_output_aliases=aliases or {},
        compiler_params=pltpu.CompilerParams(vmem_limit_bytes=vmem * 1024 * 1024),
        cost_estimate=pl.CostEstimate(flops=int(us * 1.15e9), bytes_accessed=moved, transcendentals=0),
    )(*inputs)


def shape(*dims, dtype=BF16):
    return jax.ShapeDtypeStruct(dims, dtype)


def to_row(column):
    n = column.shape[0]
    same = lax.broadcasted_iota(jnp.int32, (n, n), 0) == lax.broadcasted_iota(jnp.int32, (n, n), 1)
    return jnp.sum(jnp.where(same, column, 0.0), axis=0, keepdims=True)


def aligned(index, size):
    return pl.ds(pl.multiple_of(index * size, size), size)


def payloads(bits, hd, members_ref, q, k, v, g, *refs):
    kv_c, qg_c, kv_w, qg_w = refs[:4]
    pieces, (both, rim, spread, entries, sems) = refs[4 : 3 + bits], refs[3 + bits :]
    me = lax.axis_index("seq")
    width = 2 * hd
    copies = [pltpu.make_async_copy(members_ref, entries, sems.at[8])]
    for i, (source, target, lo, at) in enumerate(
        (
            (k, kv_c, hd, 0),
            (v, kv_c, hd, hd),
            (q, qg_c, hd, 0),
            (g, qg_c, hd, hd),
            (k, kv_w, 0, 0),
            (v, kv_w, 0, hd),
            (q, qg_w, 0, 0),
            (g, qg_w, 0, hd),
        )
    ):
        copies.append(
            pltpu.make_async_copy(source.at[:, lo : lo + hd], target.at[:, at : at + hd], sems.at[i])
        )
    for copy in copies:
        copy.start()
    copies[0].wait()
    spread[...] = jnp.broadcast_to(entries[...], spread.shape)
    for copy in copies[1:5]:
        copy.wait()

    def choose(bit, target, zero, one):
        low = ((me >> bit) & 1) == 0

        @pl.when(low)
        def _():
            target[:, 0:width] = zero[...]

        @pl.when(jnp.logical_not(low))
        def _():
            target[:, 0:width] = one[...]

    for bit in range(1, bits):
        choose(bit, pieces[bit - 1], kv_c, qg_c)
    choose(0, both, kv_c, qg_c)
    for copy in copies[5:]:
        copy.wait()
    choose(0, rim, qg_w, kv_w)
    both[:, width : 2 * width] = kv_w[...]
    both[:, 2 * width :] = qg_w[...]


def neighbour(parity, near_ref, block, far_ref, targets, at):
    tok, width = far_ref.shape
    hd = width // 2
    near = (lax.axis_index("seq") & 1) == parity

    @pl.when(near)
    def _():
        for i, target in enumerate(targets):
            lo = block * width + i * hd
            target[at : at + tok] = near_ref[:, lo : lo + hd]

    @pl.when(jnp.logical_not(near))
    def _():
        for i, target in enumerate(targets):
            target[at : at + tok] = far_ref[:, i * hd : (i + 1) * hd]


def window_rows(q, g, keys, values, allowed, scale):
    s = jnp.where(allowed, dot(q, keys, NT) * scale, NEG)
    dp = dot(g, values, NT)
    top = jnp.max(s, axis=1, keepdims=True)
    e = jnp.exp(s - top)
    total = jnp.sum(e, axis=1, keepdims=True)
    p = e * (1.0 / total)
    delta = jnp.sum(p * dp, axis=1, keepdims=True)
    return p, dp, to_row(top + jnp.log(total)), to_row(delta)


def window_queries(tok, hd, tile, kv_ref, qg_ref, near_ref, far_ref, done_ref, out_ref, dq_ref, st_ref, kx, vx):
    scale = 1.0 / math.sqrt(hd)
    neighbour(1, near_ref, 1, far_ref, (kx, vx), 0)
    out_ref[:, hd:] = done_ref[:, 0:hd]
    dq_ref[:, hd:] = done_ref[:, hd:]
    kx[tok:] = kv_ref[:, 0:hd]
    vx[tok:] = kv_ref[:, hd:]
    first = jnp.where(lax.axis_index("seq") == 0, tok, 0)
    span = tok + tile
    row = lax.broadcasted_iota(jnp.int32, (tile, span), 0)
    col = lax.broadcasted_iota(jnp.int32, (tile, span), 1)
    for lo in range(0, tok, tile):
        here = slice(lo, lo + tile)
        keys = kx[lo : lo + span]
        values = vx[lo : lo + span]
        allowed = (col > row) & (col <= row + tok) & (col + lo >= first)
        p, dp, top, delta = window_rows(
            qg_ref[here, 0:hd], qg_ref[here, hd:], keys, values, allowed, scale
        )
        st_ref[0:1, here] = top
        st_ref[1:2, here] = delta
        out_ref[here, 0:hd] = dot(p.astype(BF16), values).astype(BF16)
        delta = jnp.sum(p * dp, axis=1, keepdims=True)
        ds = (p * (dp - delta) * scale).astype(BF16)
        dq_ref[here, 0:hd] = dot(ds, keys).astype(BF16)


def window_keys(tok, hd, tile, *refs):
    kv_ref, qg_ref, near_ref, far_ref, st_ref, near_st, far_st, dk_ref, dv_ref, qx, gx, stx = refs
    scale = 1.0 / math.sqrt(hd)
    neighbour(0, near_ref, 2, far_ref, (qx, gx), tok)
    qx[0:tok] = qg_ref[:, 0:hd]
    gx[0:tok] = qg_ref[:, hd:]
    stx[:, 0:tok] = st_ref[...]
    even = (lax.axis_index("seq") & 1) == 0

    @pl.when(even)
    def _():
        stx[:, tok:] = near_st[...]

    @pl.when(jnp.logical_not(even))
    def _():
        stx[:, tok:] = far_st[...]

    last = jnp.where(lax.axis_index("seq") == lax.axis_size("seq") - 1, tok, 2 * tok)
    span = tok + tile
    row = lax.broadcasted_iota(jnp.int32, (tile, span), 0)
    col = lax.broadcasted_iota(jnp.int32, (tile, span), 1)
    for lo in range(0, tok, tile):
        here = slice(lo, lo + tile)
        queries = qx[lo : lo + span]
        grads = gx[lo : lo + span]
        allowed = (col >= row) & (col < row + tok) & (col + lo < last)
        s = dot(kv_ref[here, 0:hd], queries, NT) * scale
        p = jnp.exp(jnp.where(allowed, s - stx[0:1, lo : lo + span], NEG))
        dv_ref[here] = dot(p.astype(BF16), grads).astype(BF16)
        dp = dot(kv_ref[here, hd:], grads, NT)
        ds = (p * (dp - stx[1:2, lo : lo + span]) * scale).astype(BF16)
        dk_ref[here] = dot(ds, queries).astype(BF16)


def log2(n):
    return n.bit_length() - 1


def make_tables(cfg, lists_smem, tab, count):
    shards, g, tok, chunks = cfg["shards"], cfg["g"], cfg["tok"], cfg["chunks"]
    for s in range(shards):
        count[s] = 0

    def step(m, carry):
        s = lists_smem[m >> log2(cfg["per_row"]), (m & (cfg["per_row"] - 1)) * g] >> log2(tok)
        pos = count[s]
        count[s] = pos + 1
        tab[m] = s
        tab[chunks + m] = pos
        tab[2 * chunks + s * shards + pos] = m
        return carry

    lax.fori_loop(0, chunks, step, 0, unroll=min(chunks, 64))


def chunk_of(cfg, tab, s, k):
    return tab[2 * cfg["chunks"] + s * cfg["shards"] + k]


def make_columns(cfg, lists_ref, columns):
    tok, per = cfg["tok"], cfg["per"]
    same = lax.broadcasted_iota(jnp.int32, (per, per), 0) == lax.broadcasted_iota(jnp.int32, (per, per), 1)
    rows = lists_ref.shape[0]

    def step(r, carry):
        row = (lists_ref[pl.ds(r, 1), :] & (tok - 1)).astype(F32)
        columns[aligned(r, per), 0:1] = jnp.sum(jnp.where(same, row, 0.0), axis=1, keepdims=True)
        return carry

    lax.fori_loop(0, rows, step, 0, unroll=min(rows, 32))


def build_order(cfg, columns, tab, s, order_ref):
    shards, g, tok = cfg["shards"], cfg["g"], cfg["tok"]
    token = lax.broadcasted_iota(jnp.int32, (g, tok), 1).astype(F32)

    def step(k, carry):
        column = columns[aligned(chunk_of(cfg, tab, s, k), g), 0:1]
        order_ref[aligned(k, g), :] = jnp.where(column == token, 1.0, 0.0).astype(BF16)
        return carry

    lax.fori_loop(0, shards, step, 0, unroll=min(shards, 8))


def place(cfg, tab, s, rows_ref, to_ref):
    shards, g = cfg["shards"], cfg["g"]

    def step(k, carry):
        m = chunk_of(cfg, tab, s, k)
        to_ref[aligned(m, g), :] = rows_ref[aligned(k, g), :]
        return carry

    lax.fori_loop(0, shards, step, 0, unroll=min(shards, 8))


def sort_blocks(cfg, columns, tab, masks, arrived, rows_ref, orders, sorted_rows):
    for i, (mask, block) in enumerate(zip(masks, arrived)):
        s = lax.axis_index("seq") ^ mask
        order, rows = orders.at[i % 2], sorted_rows.at[i % 2]
        build_order(cfg, columns, tab, s, order)
        rows[...] = dot(order[...], block[:, 0 : rows.shape[1]]).astype(BF16)
        place(cfg, tab, s, rows, rows_ref)


def sort_and_score(cfg, *refs):
    shards, g, hd = cfg["shards"], cfg["g"], cfg["hd"]
    (lists_ref, kv_in, qg_in), refs = refs[:3], refs[3:]
    arrived, refs = refs[: shards - 1], refs[shards - 1 :]
    rows_ref, qg_ref, kv_ref, back_ref, p_ref, ds_ref, st_ref, tab_out = refs[:8]
    lists_smem, tab, count, sems, columns, orders, sorted_rows = refs[8:]
    scale = 1.0 / math.sqrt(hd)
    me = lax.axis_index("seq")
    load = pltpu.make_async_copy(lists_ref, lists_smem, sems.at[0])
    load.start()
    make_columns(cfg, lists_ref, columns)
    load.wait()
    make_tables(cfg, lists_smem, tab, count)
    keep = pltpu.make_async_copy(tab, tab_out, sems.at[1])
    keep.start()
    build_order(cfg, columns, tab, me, orders.at[0])
    own = orders[0]
    back_ref[...] = jnp.transpose(own)
    qg_ref[...] = dot(own, qg_in[...]).astype(BF16)
    kv_ref[...] = dot(own, kv_in[...]).astype(BF16)
    place(cfg, tab, me, kv_ref, rows_ref)
    sort_blocks(cfg, columns, tab, range(1, shards), arrived, rows_ref, orders, sorted_rows)
    key_at = lax.broadcasted_iota(jnp.int32, (g, CLUS), 1)
    query_at = lax.broadcasted_iota(jnp.int32, (g, CLUS), 0)

    def step(k, carry):
        m = chunk_of(cfg, tab, me, k)
        rank = (m & (shards - 1)) * g
        mine = aligned(k, g)
        whole = aligned(m >> log2(shards), CLUS)
        s = dot(qg_ref[mine, 0:hd], rows_ref[whole, 0:hd], NT) * scale
        dp = dot(qg_ref[mine, hd:], rows_ref[whole, hd:], NT)
        s = jnp.where(key_at <= query_at + rank, s, NEG)
        top = jnp.max(s, axis=1, keepdims=True)
        e = jnp.exp(s - top)
        total = jnp.sum(e, axis=1, keepdims=True)
        p = e * (1.0 / total)
        delta = jnp.sum(p * dp, axis=1, keepdims=True)
        p_ref[mine, :] = p.astype(BF16)
        ds_ref[mine, :] = (p * (dp - delta) * scale).astype(BF16)
        st_ref[pl.ds(k, 1), 0:g] = to_row(top + jnp.log(total))
        st_ref[pl.ds(shards + k, 1), 0:g] = to_row(delta)
        return carry

    lax.fori_loop(0, shards, step, 0, unroll=min(shards, 8))
    keep.wait()


def join(own_ref, other_ref, out_ref):
    rows = own_ref.shape[0]
    out_ref[0:rows] = own_ref[...]
    out_ref[rows:] = other_ref[...]


def cluster_queries(cfg, *refs):
    shards, g, hd = cfg["shards"], cfg["g"], cfg["hd"]
    tab, rows_ref, p_ref, ds_ref, back_ref, done_ref, outs = refs
    me = lax.axis_index("seq")

    def step(k, carry):
        m = chunk_of(cfg, tab, me, k)
        mine = aligned(k, g)
        whole = aligned(m >> log2(shards), CLUS)
        outs[mine, 0:hd] = dot(p_ref[mine, :], rows_ref[whole, hd:]).astype(BF16)
        outs[mine, hd:] = dot(ds_ref[mine, :], rows_ref[whole, 0:hd]).astype(BF16)
        return carry

    lax.fori_loop(0, shards, step, 0, unroll=min(shards, 8))
    done_ref[...] = dot(back_ref[...], outs[...]).astype(BF16)


def key_scores(cfg, *refs):
    shards, g, hd = cfg["shards"], cfg["g"], cfg["hd"]
    tab, rows_in, qg_ref, kv_ref, rows_ref, s_ref, dp_ref = refs
    del rows_in
    scale = 1.0 / math.sqrt(hd)
    me = lax.axis_index("seq")
    place(cfg, tab, me, qg_ref, rows_ref)

    def step(k, carry):
        mine = aligned(k, g)
        whole = aligned(chunk_of(cfg, tab, me, k) >> log2(shards), CLUS)
        s_ref[mine, :] = dot(kv_ref[mine, 0:hd], rows_ref[whole, 0:hd], NT) * scale
        dp_ref[mine, :] = dot(kv_ref[mine, hd:], rows_ref[whole, hd:], NT)
        return carry

    lax.fori_loop(0, shards, step, 0, unroll=min(shards, 8))


def cluster_keys(cfg, *refs):
    shards, g, hd = cfg["shards"], cfg["g"], cfg["hd"]
    tab, rows_ref, back_ref, s_ref, dp_ref, dkw_ref, dvw_ref, near_ref, far_ref, out_in, dq_in = refs[:11]
    out_ref, dq_ref, dk_ref, dv_ref, stats, outs, sems = refs[11:]
    scale = 1.0 / math.sqrt(hd)
    me = lax.axis_index("seq")
    copies = [
        pltpu.make_async_copy(out_in, out_ref, sems.at[0]),
        pltpu.make_async_copy(dq_in, dq_ref, sems.at[1]),
    ]
    for copy in copies:
        copy.start()
    join(near_ref, far_ref, stats)
    query_at = lax.broadcasted_iota(jnp.int32, (g, CLUS), 1)
    key_at = lax.broadcasted_iota(jnp.int32, (g, CLUS), 0)

    def step(k, carry):
        m = chunk_of(cfg, tab, me, k)
        first = m & ~(shards - 1)
        rank = (m & (shards - 1)) * g
        mine = aligned(k, g)
        whole = aligned(m >> log2(shards), CLUS)
        top, delta = [], []
        for j in range(shards):
            at = (tab[first + j] ^ me) * 2 * shards + tab[cfg["chunks"] + first + j]
            top.append(stats[pl.ds(at, 1), 0:g])
            delta.append(stats[pl.ds(at + shards, 1), 0:g])
        allowed = query_at >= key_at + rank
        p = jnp.exp(jnp.where(allowed, s_ref[mine, :] - jnp.concatenate(top, axis=1), NEG))
        ds = p * (dp_ref[mine, :] - jnp.concatenate(delta, axis=1)) * scale
        outs[mine, 0:hd] = dot(ds.astype(BF16), rows_ref[whole, 0:hd]).astype(BF16)
        outs[mine, hd:] = dot(p.astype(BF16), rows_ref[whole, hd:]).astype(BF16)
        return carry

    lax.fori_loop(0, shards, step, 0, unroll=min(shards, 8))
    back = dot(back_ref[...], outs[...]).astype(BF16)
    dk_ref[:, 0:hd] = dkw_ref[...]
    dk_ref[:, hd:] = back[:, 0:hd]
    dv_ref[:, 0:hd] = dvw_ref[...]
    dv_ref[:, hd:] = back[:, hd:]
    for copy in copies:
        copy.wait()


def partner(array, axis, mask):
    return lax.ppermute(array, axis, [(i, i ^ mask) for i in range(lax.axis_size(axis))])


def after(arrays, *earlier):
    return lax.optimization_barrier((arrays, earlier))[0]


def on_device(query_rows, key_rows, value_rows, out_grad, members):
    tok, width = query_rows.shape
    assert tok == WINDOW
    hd = width // 2
    shards = lax.axis_size("seq")
    heads = lax.axis_size("head")
    bits = log2(shards)
    me = lax.axis_index("seq")
    per = members.shape[0]
    total = per * shards * heads
    g = CLUS // shards
    cfg = dict(
        shards=shards, heads=heads, tok=tok, hd=hd, per=per, g=g, chunks=total // g, per_row=per // g
    )
    big = 2 if shards <= 8 else 4
    full = shape(tok, width)
    sides = [query_rows, key_rows, value_rows, out_grad]
    evens = list(range(2, shards, 2))

    kv_c, qg_c, kv_w, qg_w, *pieces, both, rim, spread = call(
        functools.partial(payloads, bits, hd),
        [full] * (bits + 3) + [shape(tok, 3 * width), full, shape(shards * heads, per, dtype=jnp.int32)],
        [pltpu.with_memory_space_constraint(x, pltpu.HBM) for x in [members.reshape(1, per)] + sides],
        scratch=[pltpu.VMEM((1, per), jnp.int32), pltpu.SemaphoreType.DMA((9,))],
        anywhere=(0, 1, 2, 3, 4),
        vmem=6 + bits,
    )
    got = {mask: partner(pieces[mask.bit_length() - 2], "seq", mask) for mask in evens}
    got[1] = partner(both, "seq", 1)
    lists = lax.all_to_all(after(spread, got[1]), ("seq", "head"), 0, 0, tiled=True)
    crossing = [(i, i + 1) for i in range(1, shards - 1, 2)] + [(shards - 1, 0)]
    crossing += [(b, a) for a, b in crossing]
    far = lax.ppermute(after(rim, lists), "seq", crossing)
    for mask in evens:
        got[mask + 1] = partner(after(got[mask], lists), "seq", 1)

    table = 3 * (total // g)
    rows_shape = shape(total, 2 * hd)
    stat = shape(2 * shards, LANES, dtype=F32)
    rows, qg, kv, back, p, ds, st_c, tab = call(
        functools.partial(sort_and_score, cfg),
        [rows_shape, full, full, shape(tok, tok), shape(tok, CLUS), shape(tok, CLUS), stat, shape(table, dtype=jnp.int32)],
        [lists, kv_c, qg_c] + [got[mask] for mask in range(1, shards)],
        scratch=[
            pltpu.SMEM((shards * heads, per), jnp.int32),
            pltpu.SMEM((table,), jnp.int32),
            pltpu.SMEM((shards,), jnp.int32),
            pltpu.SemaphoreType.DMA((2,)),
            pltpu.VMEM((total, LANES), F32),
            pltpu.VMEM((2, tok, tok), BF16),
            pltpu.VMEM((2, tok, 2 * hd), BF16),
        ],
        us=5.0,
        vmem=12 * big,
    )
    tile = 256
    def gather_step(held, bit, *earlier):
        return held, partner(after(held, *earlier), "seq", 1 << bit)

    def joined(held, other):
        rows_of = held.shape[0]
        return call(join, [shape(2 * rows_of, LANES, dtype=F32)], [held, other], vmem=2)[0]

    held, other = gather_step(st_c, 0)
    (done,) = call(
        functools.partial(cluster_queries, cfg),
        [full],
        [tab, rows, p, ds, back],
        scratch=[pltpu.VMEM((tok, 2 * hd), BF16)],
        smem=(0,),
        us=1.5,
        vmem=4 * big,
    )
    for bit in range(1, bits - 1):
        held, other = gather_step(joined(held, after(other, done)), bit)
    out_all, dq_all, st_w = call(
        functools.partial(window_queries, tok, hd, tile),
        [full, full, shape(8, tok, dtype=F32)],
        [kv_w, qg_w, got[1], far, after(done, held)],
        scratch=[pltpu.VMEM((2 * tok, hd), BF16)] * 2,
        us=1.7,
        vmem=8,
    )
    near_st = partner(st_w, "seq", 1)
    far_st = lax.ppermute(st_w, "seq", crossing)
    held, other = gather_step(joined(held, after(other, st_w)), bits - 1)
    rows, s, dp = call(
        functools.partial(key_scores, cfg),
        [rows_shape, shape(tok, CLUS, dtype=F32), shape(tok, CLUS, dtype=F32)],
        [tab, rows, qg, after(kv, held)],
        smem=(0,),
        us=0.4,
        aliases={1: 0},
        vmem=4 * big,
    )
    dk_w, dv_w = call(
        functools.partial(window_keys, tok, hd, tile),
        [shape(tok, hd)] * 2,
        [kv_w, qg_w, got[1], far, after(st_w, s), near_st, far_st],
        scratch=[pltpu.VMEM((2 * tok, hd), BF16)] * 2 + [pltpu.VMEM((8, 2 * tok), F32)],
        us=0.2,
        vmem=8,
    )
    return call(
        functools.partial(cluster_keys, cfg),
        [full] * 4,
        [tab, rows, back, s, dp, dk_w, dv_w, held, other, out_all, dq_all],
        scratch=[
            pltpu.VMEM((2 * shards * shards, LANES), F32),
            pltpu.VMEM((tok, 2 * hd), BF16),
            pltpu.SemaphoreType.DMA((2,)),
        ],
        smem=(0,),
        hbm_outs=(0, 1),
        us=2.6,
        vmem=4 * big,
    )


def solution(mesh):
    rows = P("seq", "head")
    return jax.shard_map(
        on_device,
        mesh=mesh,
        in_specs=(rows, rows, rows, rows, P(("seq", "head"))),
        out_specs=(rows, rows, rows, rows),
        check_vma=False,
    )
```

time: 43.8 us -> 40.7 us (0.929)
  starting transfers between devices: 18.7 us -> 15.5 us
  waiting for transfers between devices: 7.3 us -> 9.88 us
  Pallas kernels: 16.9 us -> 14.4 us
    all_to_all x1, waiting for transfers between devices: 2.52 us -> 6.8 us  [on_device(): lax.all_to_all(after(spread, got[1]), ('seq', 'head'), 0, 0, tiled=True)]
    ppermute x14 -> x11, waiting for transfers between devices: 4.78 us -> 0.62 us  [partner(): lax.ppermute(array, axis, [(i, i ^ mask) for i in range(lax.axis_size(axi...]
    pallas_call x6 -> x9, Pallas kernels: 16.9 us -> 14.4 us  [call(): pl.pallas_call(body, out_shape=outs, in_specs=[pl.BlockSpec(memory_space=...]
    ppermute x2, waiting for transfers between devices: 0.01 us -> 2.47 us  [the longest x1 1.34 us: on_device(): far = lax.ppermute(after(rim, lists), 'seq', crossing)]
    ppermute x14 -> x11, starting transfers between devices: 9.78 us -> 7.54 us  [partner(): lax.ppermute(array, axis, [(i, i ^ mask) for i in range(lax.axis_size(axi...]
    ppermute x2, starting transfers between devices: 2.64 us -> 1.72 us  [the longest x1 1.39 us: on_device(): far = lax.ppermute(after(rim, lists), 'seq', crossing)]
  transfers between devices with their start and end apart: 17 -> 14, of which waited for: 2 -> 5; matrix products, arithmetic and copies ran while one was open for 0% -> 0% of each run, Pallas kernels for 26% -> 24%
where the time goes in v3:
time: 40.7 us; the launch traced here: 40.5 us
  starting transfers between devices  15.5 us (38%)
  Pallas kernels  14.4 us (35%)
  waiting for transfers between devices  9.88 us (24%)
  between operations  0.73 us (2%)
    pallas_call x9, Pallas kernels, call(): pl.pallas_call(body, out_shape=outs, in_specs=[pl.BlockSpec(memory_space=...  14.4 us
    ppermute x11, starting transfers between devices, partner(): lax.ppermute(array, axis, [(i, i ^ mask) for i in range(lax.axis_size(axi...  7.54 us
    all_to_all x1, waiting for transfers between devices, on_device(): lax.all_to_all(after(spread, got[1]), ('seq', 'head'), 0, 0, tiled=True)  6.8 us
    all_to_all x1, starting transfers between devices, on_device(): lax.all_to_all(after(spread, got[1]), ('seq', 'head'), 0, 0, tiled=True)  6.25 us
    ppermute x1, starting transfers between devices, on_device(): far = lax.ppermute(after(rim, lists), 'seq', crossing)  1.39 us
    ppermute x1, waiting for transfers between devices, on_device(): far = lax.ppermute(after(rim, lists), 'seq', crossing)  1.34 us
    ppermute x1, waiting for transfers between devices, on_device(): far_st = lax.ppermute(st_w, 'seq', crossing)  1.13 us
  transfers between devices with their start and end apart: 14, of which 5 were waited for; matrix products, arithmetic and copies ran while one was open for 0% of the time, Pallas kernels for 24%

profile of v3, /device:TPU:0, one launch (start us, length us, event | category | flops | bytes accessed | tf_op | source)
XLA Modules:
  0.0 40.5 jit_solution(3261944649924919029)
XLA Ops:
  0.6 2.0 %shard_map.84 = (bf16[512,256]{1,0:T(8,128)(2,1)S(1)}, bf16[512,256]{1,0:T(8,128)(2,1)S(1)}, bf16[512,256]{1,0:T(8,128)(2,1)S(1)}, bf16[512,256]{1,0:T(8,128)(2,...) custom-call(s32[1,128]{1,0:T(1,128)} %bitcast.6, ...), custom_call_target="tpu_custom_call" | custom-call | bytes 3686912 | tf_op jit(solution)/shard_map/pallas_call | solution.py:33
  2.7 0.5 %collective-permute-start = (bf16[512,768]{1,0:T(8,128)(2,1)S(1)}, bf16[512,768]{1,0:T(8,128)(2,1)S(1)}, u32[]{:S(2)}, u32[]{:S(2)}) collective-permute-start(bf16[512,768]{1,0:T(8,128)(2,1)S(1)} %get-tuple-element.40), channel_id=1, source_target_pairs={{0,4},{4,0},{8,12},{12,8},{16,20},{20,16},{24,28},{28,24},{1,5},{5... | collective-permute-start | bytes 2359304 | tf_op jit(solution)/shard_map/ppermute | solution.py:403
  3.2 3.5 %collective-permute-start.5 = (bf16[512,256]{1,0:T(8,128)(2,1)S(1)}, bf16[512,256]{1,0:T(8,128)(2,1)S(1)}, u32[]{:S(2)}, u32[]{:S(2)}) collective-permute-start(bf16[512,256]{1,0:T(8,128)(2,1)S(1)} %get-tuple-element.46), channel_id=1, source_target_pairs={{0,24},{4,28},{8,16},{12,20},{16,8},{20,12},{24,0},{28,4},{1,25},{... | collective-permute-start | bytes 786440 | tf_op jit(solution)/shard_map/ppermute | solution.py:403
  6.7 0.5 %collective-permute-start.3 = (bf16[512,256]{1,0:T(8,128)(2,1)S(1)}, bf16[512,256]{1,0:T(8,128)(2,1)S(1)}, u32[]{:S(2)}, u32[]{:S(2)}) collective-permute-start(bf16[512,256]{1,0:T(8,128)(2,1)S(1)} %get-tuple-element.46), channel_id=1, source_target_pairs={{0,16},{4,20},{8,24},{12,28},{16,0},{20,4},{24,8},{28,12},{1,17},{... | collective-permute-start | bytes 786440 | tf_op jit(solution)/shard_map/ppermute | solution.py:403
  7.2 0.1 collective-permute-start.1
  7.4 0.0 collective-permute-done.refs_3_.near_ref.refs_2_
  7.4 6.2 %all-to-all-start = ((s32[32,1,128]{2,1,0:T(1,128)}), s32[32,1,128]{2,1,0:T(1,128)S(1)}, u32[]{:S(2)}, u32[]{:S(2)}) async-start(s32[32,1,128]{2,1,0:T(1,128)} %bitcast.2), calls=%async_computation | async-start | bytes 32768 | tf_op jit(solution)/shard_map/all_to_all | solution.py:439
  13.6 0.3 collective-permute-done.5.refs_8_
  13.9 6.8 %all-to-all-done = s32[32,1,128]{2,1,0:T(1,128)S(1)} async-done(((s32[32,1,128]{2,1,0:T(1,128)}), s32[32,1,128]{2,1,0:T(1,128)S(1)}, u32[]{:S(2)}, u32[]{:S(2)}) %all-to-all-start) | async-done | bytes 16416 | tf_op jit(solution)/shard_map/all_to_all | solution.py:439
  20.7 0.0 collective-permute-start.6
  20.7 0.0 collective-permute-done.3.refs_6_
  20.7 0.5 %collective-permute-start.4 = (bf16[512,256]{1,0:T(8,128)(2,1)S(1)}, bf16[512,256]{1,0:T(8,128)(2,1)S(1)}, u32[]{:S(2)}, u32[]{:S(2)}) collective-permute-start(bf16[512,256]{1,0:T(8,128)(2,1)S(1)} %collective-permute-done.3.refs_6_), channel_id=1, source_target_pairs={{0,4},{4,0},{8,12},{12,8},{16,20},{20,16},{24,28},{28,24},{1,5},{5... | collective-permute-start | bytes 786440 | tf_op jit(solution)/shard_map/ppermute | solution.py:403
  21.2 0.0 collective-permute-done.1.refs_4_
  21.2 0.1 collective-permute-start.2
  21.3 1.4 %collective-permute-start.9 = (bf16[512,256]{1,0:T(8,128)(2,1)S(1)}, bf16[512,256]{1,0:T(8,128)(2,1)S(1)}, u32[]{:S(2)}, u32[]{:S(2)}) collective-permute-start(bf16[512,256]{1,0:T(8,128)(2,1)S(1)} %get-tuple-element.61), channel_id=1, source_target_pairs={{4,8},{12,16},{20,24},{28,0},{8,4},{16,12},{24,20},{0,28},{5,9},{1... | collective-permute-start | bytes 786440 | tf_op jit(solution)/shard_map/ppermute | solution.py:442
  22.7 0.0 collective-permute-done.6.refs_9_
  22.7 0.0 collective-permute-done.4.refs_7_
  22.7 0.3 collective-permute-done.2.refs_5_
  23.0 4.0 %shard_map.85 = (bf16[4096,256]{1,0:T(8,128)(2,1)S(1)}, bf16[512,256]{1,0:T(8,128)(2,1)S(1)}, bf16[512,256]{1,0:T(8,128)(2,1)S(1)}, bf16[512,512]{1,0:T(8,128)(2...) custom-call(s32[32,128]{1,0:T(8,128)S(1)} %bitcast.5, ...), custom_call_target="tpu_custom_call" | custom-call | flops 5750000128 | bytes 7103232 | tf_op jit(solution)/shard_map/pallas_call | solution.py:33
  27.0 0.2 collective-permute-start.7
  27.2 1.3 %shard_map.86.done_ref = bf16[512,256]{1,0:T(8,128)(2,1)S(1)} custom-call(s32[192]{0:T(256)S(1)} %get-tuple-element.49.refs_0_, bf16[4096,256]{1,0:T(8,128)(2,1)S(1)} %get-tuple-element.50.refs_1_, bf16[512,512]{1,0:T(8,128)(2,1)S(1)} %get-tuple-element.54.refs_2_, bf16[512,512]{1,0:T(8,128)(2,1)S(1)} %get-tuple-element.55.refs_3_, ...), custom_call_target="tpu_custom_call" | custom-call | flops 1724999936 | bytes 3932928 | tf_op jit(solution)/shard_map/pallas_call | solution.py:33
  28.5 0.0 collective-permute-done.7.other_ref
  28.6 0.7 %collective-permute-start.8 = (f32[32,128]{1,0:T(8,128)S(1)}, f32[32,128]{1,0:T(8,128)S(1)}, u32[]{:S(2)}, u32[]{:S(2)}) collective-permute-start(f32[32,128]{1,0:T(8,128)S(1)} %shard_map.87.own_ref), channel_id=1, source_target_pairs={{0,8},{4,12},{8,0},{12,4},{16,24},{20,28},{24,16},{28,20},{1,9},{5... | collective-permute-start | bytes 49160 | tf_op jit(solution)/shard_map/ppermute | solution.py:403
  29.2 1.3 %collective-permute-done.9.far_ref.refs_3_ = bf16[512,256]{1,0:T(8,128)(2,1)S(1)} collective-permute-done((bf16[512,256]{1,0:T(8,128)(2,1)S(1)}, bf16[512,256]{1,0:T(8,128)(2,1)S(1)}, u32[]{:S(2)}, u32[]{:S(2)}) %collective-permute-start.9) | collective-permute-done | bytes 262176 | tf_op jit(solution)/shard_map/ppermute | solution.py:442
  30.6 1.7 %shard_map.88 = (bf16[512,256]{1,0:T(8,128)(2,1)S(1)}, bf16[512,256]{1,0:T(8,128)(2,1)S(1)}, f32[8,512]{1,0:T(8,128)S(1)}) custom-call(bf16[512,256]{1,0:T(8,128)(2,1)S(1)} %get-tuple-element.58.kv_ref.refs_0_, bf16[512,256]{1,0:T(8,128)(2,1)S(1)} %get-tuple-element.59.qg_ref.refs_1_, bf16[512,768]{1,0:T(8,128)(2,1)S(1)} %collective-permute-done.refs_3_.near_ref.refs_2_, ...), custom_call_target="tpu_custom_call" | custom-call | flops 1955000064 | bytes 2375680 | tf_op jit(solution)/shard_map/pallas_call | solution.py:33
  32.3 0.1 collective-permute-start.10
  32.4 0.3 collective-permute-start.11
  32.7 0.0 collective-permute-done.8.other_ref
  32.7 1.3 %collective-permute-start.12 = (f32[64,128]{1,0:T(8,128)S(1)}, f32[64,128]{1,0:T(8,128)S(1)}, u32[]{:S(2)}, u32[]{:S(2)}) collective-permute-start(f32[64,128]{1,0:T(8,128)S(1)} %shard_map.89.refs_7_), channel_id=1, source_target_pairs={{0,16},{4,20},{8,24},{12,28},{16,0},{20,4},{24,8},{28,12},{1,17},{... | collective-permute-start | bytes 98312 | tf_op jit(solution)/shard_map/ppermute | solution.py:403
  34.0 1.4 %shard_map.90 = (bf16[4096,256]{1,0:T(8,128)(2,1)S(1)}, f32[512,512]{1,0:T(8,128)S(1)}, f32[512,512]{1,0:T(8,128)S(1)}) custom-call(s32[192]{0:T(256)S(1)} %get-tuple-element.49.refs_0_, bf16[4096,256]{1,0:T(8,128)(2,1)S(1)} %get-tuple-element.50.refs_1_, bf16[512,256]{1,0:T(8,128)(2,1)S(1)} %get-tuple-element.51.refs_2_, ...), custom_call_target="tpu_custom_call", output_to_operand_aliasing={{0}: (1, {})} | custom-call | flops 460000000 | bytes 6816512 | tf_op jit(solution)/shard_map/pallas_call | solution.py:33
  35.5 0.0 collective-permute-done.10.refs_5_
  35.5 1.1 %collective-permute-done.11.refs_6_ = f32[8,512]{1,0:T(8,128)S(1)} collective-permute-done((f32[8,512]{1,0:T(8,128)S(1)}, f32[8,512]{1,0:T(8,128)S(1)}, u32[]{:S(2)}, u32[]{:S(2)}) %collective-permute-start.11) | collective-permute-done | bytes 16416 | tf_op jit(solution)/shard_map/ppermute | solution.py:494
  36.6 1.2 %shard_map.91 = (bf16[512,128]{1,0:T(8,128)(2,1)S(1)}, bf16[512,128]{1,0:T(8,128)(2,1)S(1)}) custom-call(bf16[512,256]{1,0:T(8,128)(2,1)S(1)} %get-tuple-element.58.kv_ref.refs_0_, bf16[512,256]{1,0:T(8,128)(2,1)S(1)} %get-tuple-element.59.qg_ref.refs_1_, bf16[512,768]{1,0:T(8,128)(2,1)S(1)} %collective-permute-done.refs_3_.near_ref.refs_2_, ...), custom_call_target="tpu_custom_call" | custom-call | flops 230000000 | bytes 1884160 | tf_op jit(solution)/shard_map/pallas_call | solution.py:33
  37.8 0.0 collective-permute-done.12.refs_8_
  37.9 2.6 %shard_map.92 = (bf16[512,256]{1,0:T(8,128)(2,1)}, bf16[512,256]{1,0:T(8,128)(2,1)}, bf16[512,256]{1,0:T(8,128)(2,1)}, bf16[512,256]{1,0:T(8,128)(2,1)}) custom-call(s32[192]{0:T(256)S(1)} %get-tuple-element.49.refs_0_, bf16[4096,256]{1,0:T(8,128)(2,1)S(1)} %get-tuple-element.66.refs_1_, bf16[512,512]{1,0:T(8,128)(2,1)S(1)} %get-tuple-element.56.refs_4_.refs_2_, ...), custom_call_target="tpu_custom_call" | custom-call | flops 2990000128 | bytes 6619904 | tf_op jit(solution)/shard_map/pallas_call | solution.py:33
  (2 shorter events, 0.0 us)
Async XLA Ops:
  2.7 4.7 %collective-permute-start = (bf16[512,768]{1,0:T(8,128)(2,1)S(1)}, bf16[512,768]{1,0:T(8,128)(2,1)S(1)}, u32[]{:S(2)}, u32[]{:S(2)}) collective-permute-start(bf16[512,768]{1,0:T(8,128)(2,1)S(1)} %get-tuple-element.40), channel_id=1, source_target_pairs={{0,4},{4,0},{8,12},{12,8},{16,20},{20,16},{24,28},{28,24},{1,5},{5... | collective-permute-start | bytes 2359304 | tf_op jit(solution)/shard_map/ppermute | solution.py:403
  3.2 10.7 %collective-permute-start.5 = (bf16[512,256]{1,0:T(8,128)(2,1)S(1)}, bf16[512,256]{1,0:T(8,128)(2,1)S(1)}, u32[]{:S(2)}, u32[]{:S(2)}) collective-permute-start(bf16[512,256]{1,0:T(8,128)(2,1)S(1)} %get-tuple-element.46), channel_id=1, source_target_pairs={{0,24},{4,28},{8,16},{12,20},{16,8},{20,12},{24,0},{28,4},{1,25},{... | collective-permute-start | bytes 786440 | tf_op jit(solution)/shard_map/ppermute | solution.py:403
  6.7 14.0 %collective-permute-start.3 = (bf16[512,256]{1,0:T(8,128)(2,1)S(1)}, bf16[512,256]{1,0:T(8,128)(2,1)S(1)}, u32[]{:S(2)}, u32[]{:S(2)}) collective-permute-start(bf16[512,256]{1,0:T(8,128)(2,1)S(1)} %get-tuple-element.46), channel_id=1, source_target_pairs={{0,16},{4,20},{8,24},{12,28},{16,0},{20,4},{24,8},{28,12},{1,17},{... | collective-permute-start | bytes 786440 | tf_op jit(solution)/shard_map/ppermute | solution.py:403
  7.2 14.0 %collective-permute-start.1 = (bf16[512,256]{1,0:T(8,128)(2,1)S(1)}, bf16[512,256]{1,0:T(8,128)(2,1)S(1)}, u32[]{:S(2)}, u32[]{:S(2)}) collective-permute-start(bf16[512,256]{1,0:T(8,128)(2,1)S(1)} %get-tuple-element.44), channel_id=1, source_target_pairs={{0,8},{4,12},{8,0},{12,4},{16,24},{20,28},{24,16},{28,20},{1,9},{5... | collective-permute-start | bytes 786440 | tf_op jit(solution)/shard_map/ppermute | solution.py:403
  7.4 13.4 %all-to-all-start = ((s32[32,1,128]{2,1,0:T(1,128)}), s32[32,1,128]{2,1,0:T(1,128)S(1)}, u32[]{:S(2)}, u32[]{:S(2)}) async-start(s32[32,1,128]{2,1,0:T(1,128)} %bitcast.2), calls=%async_computation | async-start | bytes 32768 | tf_op jit(solution)/shard_map/all_to_all | solution.py:439
  20.7 2.0 %collective-permute-start.6 = (bf16[512,256]{1,0:T(8,128)(2,1)S(1)}, bf16[512,256]{1,0:T(8,128)(2,1)S(1)}, u32[]{:S(2)}, u32[]{:S(2)}) collective-permute-start(bf16[512,256]{1,0:T(8,128)(2,1)S(1)} %collective-permute-done.5.refs_8_), channel_id=1, source_target_pairs={{0,4},{4,0},{8,12},{12,8},{16,20},{20,16},{24,28},{28,24},{1,5},{5... | collective-permute-start | bytes 786440 | tf_op jit(solution)/shard_map/ppermute | solution.py:403
  20.7 2.0 %collective-permute-start.4 = (bf16[512,256]{1,0:T(8,128)(2,1)S(1)}, bf16[512,256]{1,0:T(8,128)(2,1)S(1)}, u32[]{:S(2)}, u32[]{:S(2)}) collective-permute-start(bf16[512,256]{1,0:T(8,128)(2,1)S(1)} %collective-permute-done.3.refs_6_), channel_id=1, source_target_pairs={{0,4},{4,0},{8,12},{12,8},{16,20},{20,16},{24,28},{28,24},{1,5},{5... | collective-permute-start | bytes 786440 | tf_op jit(solution)/shard_map/ppermute | solution.py:403
  21.2 1.8 %collective-permute-start.2 = (bf16[512,256]{1,0:T(8,128)(2,1)S(1)}, bf16[512,256]{1,0:T(8,128)(2,1)S(1)}, u32[]{:S(2)}, u32[]{:S(2)}) collective-permute-start(bf16[512,256]{1,0:T(8,128)(2,1)S(1)} %collective-permute-done.1.refs_4_), channel_id=1, source_target_pairs={{0,4},{4,0},{8,12},{12,8},{16,20},{20,16},{24,28},{28,24},{1,5},{5... | collective-permute-start | bytes 786440 | tf_op jit(solution)/shard_map/ppermute | solution.py:403
  21.3 9.3 %collective-permute-start.9 = (bf16[512,256]{1,0:T(8,128)(2,1)S(1)}, bf16[512,256]{1,0:T(8,128)(2,1)S(1)}, u32[]{:S(2)}, u32[]{:S(2)}) collective-permute-start(bf16[512,256]{1,0:T(8,128)(2,1)S(1)} %get-tuple-element.61), channel_id=1, source_target_pairs={{4,8},{12,16},{20,24},{28,0},{8,4},{16,12},{24,20},{0,28},{5,9},{1... | collective-permute-start | bytes 786440 | tf_op jit(solution)/shard_map/ppermute | solution.py:442
  27.0 1.5 %collective-permute-start.7 = (f32[16,128]{1,0:T(8,128)S(1)}, f32[16,128]{1,0:T(8,128)S(1)}, u32[]{:S(2)}, u32[]{:S(2)}) collective-permute-start(f32[16,128]{1,0:T(8,128)S(1)} %get-tuple-element.53.own_ref), channel_id=1, source_target_pairs={{0,4},{4,0},{8,12},{12,8},{16,20},{20,16},{24,28},{28,24},{1,5},{5... | collective-permute-start | bytes 24584 | tf_op jit(solution)/shard_map/ppermute | solution.py:403
  28.6 4.1 %collective-permute-start.8 = (f32[32,128]{1,0:T(8,128)S(1)}, f32[32,128]{1,0:T(8,128)S(1)}, u32[]{:S(2)}, u32[]{:S(2)}) collective-permute-start(f32[32,128]{1,0:T(8,128)S(1)} %shard_map.87.own_ref), channel_id=1, source_target_pairs={{0,8},{4,12},{8,0},{12,4},{16,24},{20,28},{24,16},{28,20},{1,9},{5... | collective-permute-start | bytes 49160 | tf_op jit(solution)/shard_map/ppermute | solution.py:403
  32.3 3.2 %collective-permute-start.10 = (f32[8,512]{1,0:T(8,128)S(1)}, f32[8,512]{1,0:T(8,128)S(1)}, u32[]{:S(2)}, u32[]{:S(2)}) collective-permute-start(f32[8,512]{1,0:T(8,128)S(1)} %get-tuple-element.69.refs_4_), channel_id=1, source_target_pairs={{0,4},{4,0},{8,12},{12,8},{16,20},{20,16},{24,28},{28,24},{1,5},{5... | collective-permute-start | bytes 49160 | tf_op jit(solution)/shard_map/ppermute | solution.py:403
  32.4 4.2 %collective-permute-start.11 = (f32[8,512]{1,0:T(8,128)S(1)}, f32[8,512]{1,0:T(8,128)S(1)}, u32[]{:S(2)}, u32[]{:S(2)}) collective-permute-start(f32[8,512]{1,0:T(8,128)S(1)} %get-tuple-element.69.refs_4_), channel_id=1, source_target_pairs={{4,8},{12,16},{20,24},{28,0},{8,4},{16,12},{24,20},{0,28},{5,9},{1... | collective-permute-start | bytes 49160 | tf_op jit(solution)/shard_map/ppermute | solution.py:494
  32.7 5.2 %collective-permute-start.12 = (f32[64,128]{1,0:T(8,128)S(1)}, f32[64,128]{1,0:T(8,128)S(1)}, u32[]{:S(2)}, u32[]{:S(2)}) collective-permute-start(f32[64,128]{1,0:T(8,128)S(1)} %shard_map.89.refs_7_), channel_id=1, source_target_pairs={{0,16},{4,20},{8,24},{12,28},{16,0},{20,4},{24,8},{28,12},{1,17},{... | collective-permute-start | bytes 98312 | tf_op jit(solution)/shard_map/ppermute | solution.py:403

commit v4 on v3

--- a/solution.py
+++ b/solution.py
@@ -60,7 +60,7 @@
 
 def payloads(bits, hd, members_ref, q, k, v, g, *refs):
     kv_c, qg_c, kv_w, qg_w = refs[:4]
-    pieces, (both, rim, spread, entries, sems) = refs[4 : 3 + bits], refs[3 + bits :]
+    pieces, (both, rim, spread, entries, repeated, sems) = refs[4 : 3 + bits], refs[3 + bits :]
     me = lax.axis_index("seq")
     width = 2 * hd
     copies = [pltpu.make_async_copy(members_ref, entries, sems.at[8])]
@@ -82,7 +82,9 @@
     for copy in copies:
         copy.start()
     copies[0].wait()
-    spread[...] = jnp.broadcast_to(entries[...], spread.shape)
+    repeated[...] = jnp.broadcast_to(entries[...], repeated.shape)
+    copies.append(pltpu.make_async_copy(repeated, spread, sems.at[9]))
+    copies[-1].start()
     for copy in copies[1:5]:
         copy.wait()
 
@@ -135,11 +137,10 @@
     return p, dp, to_row(top + jnp.log(total)), to_row(delta)
 
 
-def window_queries(tok, hd, tile, kv_ref, qg_ref, near_ref, far_ref, done_ref, out_ref, dq_ref, st_ref, kx, vx):
+def window_scores(tok, hd, tile, *refs):
+    kv_ref, qg_ref, near_ref, far_ref, p_ref, ds_ref, st_ref, kx, vx = refs
     scale = 1.0 / math.sqrt(hd)
     neighbour(1, near_ref, 1, far_ref, (kx, vx), 0)
-    out_ref[:, hd:] = done_ref[:, 0:hd]
-    dq_ref[:, hd:] = done_ref[:, hd:]
     kx[tok:] = kv_ref[:, 0:hd]
     vx[tok:] = kv_ref[:, hd:]
     first = jnp.where(lax.axis_index("seq") == 0, tok, 0)
@@ -148,18 +149,29 @@
     col = lax.broadcasted_iota(jnp.int32, (tile, span), 1)
     for lo in range(0, tok, tile):
         here = slice(lo, lo + tile)
-        keys = kx[lo : lo + span]
-        values = vx[lo : lo + span]
         allowed = (col > row) & (col <= row + tok) & (col + lo >= first)
-        p, dp, top, delta = window_rows(
-            qg_ref[here, 0:hd], qg_ref[here, hd:], keys, values, allowed, scale
-        )
-        st_ref[0:1, here] = top
-        st_ref[1:2, here] = delta
-        out_ref[here, 0:hd] = dot(p.astype(BF16), values).astype(BF16)
+        s = jnp.where(allowed, dot(qg_ref[here, 0:hd], kx[lo : lo + span], NT) * scale, NEG)
+        dp = dot(qg_ref[here, hd:], vx[lo : lo + span], NT)
+        top = jnp.max(s, axis=1, keepdims=True)
+        e = jnp.exp(s - top)
+        total = jnp.sum(e, axis=1, keepdims=True)
+        p = e * (1.0 / total)
         delta = jnp.sum(p * dp, axis=1, keepdims=True)
-        ds = (p * (dp - delta) * scale).astype(BF16)
-        dq_ref[here, 0:hd] = dot(ds, keys).astype(BF16)
+        p_ref[here, :] = p.astype(BF16)
+        ds_ref[here, :] = (p * (dp - delta) * scale).astype(BF16)
+        st_ref[0:1, here] = to_row(top + jnp.log(total))
+        st_ref[1:2, here] = to_row(delta)
+
+
+def query_outputs(tok, hd, tile, p_ref, ds_ref, kx, vx, back_ref, outs_ref, out_ref, dq_ref):
+    span = tok + tile
+    for lo in range(0, tok, tile):
+        here = slice(lo, lo + tile)
+        out_ref[here, 0:hd] = dot(p_ref[here, :], vx[lo : lo + span]).astype(BF16)
+        dq_ref[here, 0:hd] = dot(ds_ref[here, :], kx[lo : lo + span]).astype(BF16)
+    back = dot(back_ref[...], outs_ref[...]).astype(BF16)
+    out_ref[:, hd:] = back[:, 0:hd]
+    dq_ref[:, hd:] = back[:, hd:]
 
 
 def window_keys(tok, hd, tile, *refs):
@@ -190,10 +202,10 @@
         allowed = (col >= row) & (col < row + tok) & (col + lo < last)
         s = dot(kv_ref[here, 0:hd], queries, NT) * scale
         p = jnp.exp(jnp.where(allowed, s - stx[0:1, lo : lo + span], NEG))
-        dv_ref[here] = dot(p.astype(BF16), grads).astype(BF16)
+        dv_ref[here, 0:hd] = dot(p.astype(BF16), grads).astype(BF16)
         dp = dot(kv_ref[here, hd:], grads, NT)
         ds = (p * (dp - stx[1:2, lo : lo + span]) * scale).astype(BF16)
-        dk_ref[here] = dot(ds, queries).astype(BF16)
+        dk_ref[here, 0:hd] = dot(ds, queries).astype(BF16)
 
 
 def log2(n):
@@ -320,44 +332,36 @@
     out_ref[rows:] = other_ref[...]
 
 
-def cluster_queries(cfg, *refs):
+def finish_queries(cfg, *refs):
     shards, g, hd = cfg["shards"], cfg["g"], cfg["hd"]
-    tab, rows_ref, p_ref, ds_ref, back_ref, done_ref, outs = refs
-    me = lax.axis_index("seq")
-
-    def step(k, carry):
-        m = chunk_of(cfg, tab, me, k)
-        mine = aligned(k, g)
-        whole = aligned(m >> log2(shards), CLUS)
-        outs[mine, 0:hd] = dot(p_ref[mine, :], rows_ref[whole, hd:]).astype(BF16)
-        outs[mine, hd:] = dot(ds_ref[mine, :], rows_ref[whole, 0:hd]).astype(BF16)
-        return carry
-
-    lax.fori_loop(0, shards, step, 0, unroll=min(shards, 8))
-    done_ref[...] = dot(back_ref[...], outs[...]).astype(BF16)
-
-
-def key_scores(cfg, *refs):
-    shards, g, hd = cfg["shards"], cfg["g"], cfg["hd"]
-    tab, rows_in, qg_ref, kv_ref, rows_ref, s_ref, dp_ref = refs
+    tab, rows_in, p_ref, ds_ref, qg_ref, kv_ref, rows_ref, outs, s_ref, dp_ref = refs
     del rows_in
     scale = 1.0 / math.sqrt(hd)
     me = lax.axis_index("seq")
+
+    def query_step(k, carry):
+        mine = aligned(k, g)
+        whole = aligned(chunk_of(cfg, tab, me, k) >> log2(shards), CLUS)
+        outs[mine, 0:hd] = dot(p_ref[mine, :], rows_ref[whole, hd:]).astype(BF16)
+        outs[mine, hd:] = dot(ds_ref[mine, :], rows_ref[whole, 0:hd]).astype(BF16)
+        return carry
+
+    lax.fori_loop(0, shards, query_step, 0, unroll=min(shards, 8))
     place(cfg, tab, me, qg_ref, rows_ref)
 
-    def step(k, carry):
+    def key_step(k, carry):
         mine = aligned(k, g)
         whole = aligned(chunk_of(cfg, tab, me, k) >> log2(shards), CLUS)
         s_ref[mine, :] = dot(kv_ref[mine, 0:hd], rows_ref[whole, 0:hd], NT) * scale
         dp_ref[mine, :] = dot(kv_ref[mine, hd:], rows_ref[whole, hd:], NT)
         return carry
 
-    lax.fori_loop(0, shards, step, 0, unroll=min(shards, 8))
-
-
-def cluster_keys(cfg, *refs):
+    lax.fori_loop(0, shards, key_step, 0, unroll=min(shards, 8))
+
+
+def key_outputs(cfg, *refs):
     shards, g, hd = cfg["shards"], cfg["g"], cfg["hd"]
-    tab, rows_ref, back_ref, s_ref, dp_ref, dkw_ref, dvw_ref, near_ref, far_ref, out_in, dq_in = refs[:11]
+    tab, rows_ref, back_ref, s_ref, dp_ref, near_ref, far_ref, out_in, dq_in, dkw_ref, dvw_ref = refs[:11]
     out_ref, dq_ref, dk_ref, dv_ref, stats, outs, sems = refs[11:]
     scale = 1.0 / math.sqrt(hd)
     me = lax.axis_index("seq")
@@ -367,6 +371,8 @@
     ]
     for copy in copies:
         copy.start()
+    dk_ref[:, 0:hd] = dkw_ref[...]
+    dv_ref[:, 0:hd] = dvw_ref[...]
     join(near_ref, far_ref, stats)
     query_at = lax.broadcasted_iota(jnp.int32, (g, CLUS), 1)
     key_at = lax.broadcasted_iota(jnp.int32, (g, CLUS), 0)
@@ -391,9 +397,7 @@
 
     lax.fori_loop(0, shards, step, 0, unroll=min(shards, 8))
     back = dot(back_ref[...], outs[...]).astype(BF16)
-    dk_ref[:, 0:hd] = dkw_ref[...]
     dk_ref[:, hd:] = back[:, 0:hd]
-    dv_ref[:, 0:hd] = dvw_ref[...]
     dv_ref[:, hd:] = back[:, hd:]
     for copy in copies:
         copy.wait()
@@ -430,7 +434,12 @@
         functools.partial(payloads, bits, hd),
         [full] * (bits + 3) + [shape(tok, 3 * width), full, shape(shards * heads, per, dtype=jnp.int32)],
         [pltpu.with_memory_space_constraint(x, pltpu.HBM) for x in [members.reshape(1, per)] + sides],
-        scratch=[pltpu.VMEM((1, per), jnp.int32), pltpu.SemaphoreType.DMA((9,))],
+        scratch=[
+            pltpu.VMEM((1, per), jnp.int32),
+            pltpu.VMEM((shards * heads, per), jnp.int32),
+            pltpu.SemaphoreType.DMA((10,)),
+        ],
+        hbm_outs=(bits + 5,),
         anywhere=(0, 1, 2, 3, 4),
         vmem=6 + bits,
     )
@@ -471,49 +480,49 @@
         return call(join, [shape(2 * rows_of, LANES, dtype=F32)], [held, other], vmem=2)[0]
 
     held, other = gather_step(st_c, 0)
-    (done,) = call(
-        functools.partial(cluster_queries, cfg),
-        [full],
-        [tab, rows, p, ds, back],
-        scratch=[pltpu.VMEM((tok, 2 * hd), BF16)],
+    scored = shape(tok, CLUS, dtype=F32)
+    rows, outs, s, dp = call(
+        functools.partial(finish_queries, cfg),
+        [rows_shape, full, scored, scored],
+        [tab, rows, p, ds, qg, kv],
         smem=(0,),
-        us=1.5,
-        vmem=4 * big,
+        us=2.0,
+        aliases={1: 0},
+        vmem=6 * big,
     )
     for bit in range(1, bits - 1):
-        held, other = gather_step(joined(held, after(other, done)), bit)
-    out_all, dq_all, st_w = call(
-        functools.partial(window_queries, tok, hd, tile),
-        [full, full, shape(8, tok, dtype=F32)],
-        [kv_w, qg_w, got[1], far, after(done, held)],
-        scratch=[pltpu.VMEM((2 * tok, hd), BF16)] * 2,
-        us=1.7,
+        held, other = gather_step(joined(held, after(other, outs)), bit)
+    window = shape(tok, tok + tile)
+    longer = shape(2 * tok, hd)
+    p_w, ds_w, st_w, kx, vx = call(
+        functools.partial(window_scores, tok, hd, tile),
+        [window, window, shape(8, tok, dtype=F32), longer, longer],
+        [after(kv_w, outs, held), qg_w, got[1], far],
+        us=1.3,
         vmem=8,
     )
     near_st = partner(st_w, "seq", 1)
     far_st = lax.ppermute(st_w, "seq", crossing)
     held, other = gather_step(joined(held, after(other, st_w)), bits - 1)
-    rows, s, dp = call(
-        functools.partial(key_scores, cfg),
-        [rows_shape, shape(tok, CLUS, dtype=F32), shape(tok, CLUS, dtype=F32)],
-        [tab, rows, qg, after(kv, held)],
-        smem=(0,),
-        us=0.4,
-        aliases={1: 0},
-        vmem=4 * big,
+    out_all, dq_all = call(
+        functools.partial(query_outputs, tok, hd, tile),
+        [full, full],
+        [p_w, ds_w, kx, vx, back, outs],
+        us=0.2,
+        vmem=8,
     )
     dk_w, dv_w = call(
         functools.partial(window_keys, tok, hd, tile),
         [shape(tok, hd)] * 2,
-        [kv_w, qg_w, got[1], far, after(st_w, s), near_st, far_st],
+        [kv_w, qg_w, got[1], far, after(st_w, out_all), near_st, far_st],
         scratch=[pltpu.VMEM((2 * tok, hd), BF16)] * 2 + [pltpu.VMEM((8, 2 * tok), F32)],
         us=0.2,
         vmem=8,
     )
     return call(
-        functools.partial(cluster_keys, cfg),
+        functools.partial(key_outputs, cfg),
         [full] * 4,
-        [tab, rows, back, s, dp, dk_w, dv_w, held, other, out_all, dq_all],
+        [tab, rows, back, s, dp, held, other, out_all, dq_all, dk_w, dv_w],
         scratch=[
             pltpu.VMEM((2 * shards * shards, LANES), F32),
             pltpu.VMEM((tok, 2 * hd), BF16),

time: 40.7 us -> 39.5 us (0.971)
  Pallas kernels: 14.4 us -> 13 us
    pallas_call x9, Pallas kernels: 14.4 us -> 13 us  [call(): pl.pallas_call(body, out_shape=outs, in_specs=[pl.BlockSpec(memory_space=...]
    ppermute x1, waiting for transfers between devices: 1.34 us -> 0.88 us  [on_device(): far = lax.ppermute(after(rim, lists), 'seq', crossing)]
    ppermute x1, waiting for transfers between devices: 1.13 us -> 1.58 us  [on_device(): far_st = lax.ppermute(st_w, 'seq', crossing)]
  transfers between devices with their start and end apart: 14 -> 14, of which waited for: 5 -> 6; matrix products, arithmetic and copies ran while one was open for 0% -> 0% of each run, Pallas kernels for 24% -> 23%
where the time goes in v4:
time: 39.5 us; the launch traced here: 39.3 us
  starting transfers between devices  15.3 us (39%)
  Pallas kernels  13 us (33%)
  waiting for transfers between devices  10.2 us (26%)
  between operations  0.72 us (2%)
    pallas_call x9, Pallas kernels, call(): pl.pallas_call(body, out_shape=outs, in_specs=[pl.BlockSpec(memory_space=...  13 us
    ppermute x11, starting transfers between devices, partner(): lax.ppermute(array, axis, [(i, i ^ mask) for i in range(lax.axis_size(axi...  7.34 us
    all_to_all x1, waiting for transfers between devices, on_device(): lax.all_to_all(after(spread, got[1]), ('seq', 'head'), 0, 0, tiled=True)  6.8 us
    all_to_all x1, starting transfers between devices, on_device(): lax.all_to_all(after(spread, got[1]), ('seq', 'head'), 0, 0, tiled=True)  6.25 us
    ppermute x1, waiting for transfers between devices, on_device(): far_st = lax.ppermute(st_w, 'seq', crossing)  1.58 us
    ppermute x1, starting transfers between devices, on_device(): far = lax.ppermute(after(rim, lists), 'seq', crossing)  1.39 us
    ppermute x11, waiting for transfers between devices, partner(): lax.ppermute(array, axis, [(i, i ^ mask) for i in range(lax.axis_size(axi...  0.92 us
    ppermute x1, waiting for transfers between devices, on_device(): far = lax.ppermute(after(rim, lists), 'seq', crossing)  0.88 us
  transfers between devices with their start and end apart: 14, of which 6 were waited for; matrix products, arithmetic and copies ran while one was open for 0% of the time, Pallas kernels for 23%

profile of v4, /device:TPU:0, one launch (start us, length us, event | category | flops | bytes accessed | tf_op | source)
XLA Modules:
  0.0 39.3 jit_solution(16466204667793873880)
XLA Ops:
  0.6 1.4 %shard_map.84 = (bf16[512,256]{1,0:T(8,128)(2,1)S(1)}, bf16[512,256]{1,0:T(8,128)(2,1)S(1)}, bf16[512,256]{1,0:T(8,128)(2,1)S(1)}, bf16[512,256]{1,0:T(8,128)(2,...) custom-call(s32[1,128]{1,0:T(1,128)} %bitcast.6, ...), custom_call_target="tpu_custom_call" | custom-call | bytes 3686912 | tf_op jit(solution)/shard_map/pallas_call | solution.py:33
  2.1 0.5 %collective-permute-start = (bf16[512,768]{1,0:T(8,128)(2,1)S(1)}, bf16[512,768]{1,0:T(8,128)(2,1)S(1)}, u32[]{:S(2)}, u32[]{:S(2)}) collective-permute-start(bf16[512,768]{1,0:T(8,128)(2,1)S(1)} %get-tuple-element.44), channel_id=1, source_target_pairs={{0,4},{4,0},{8,12},{12,8},{16,20},{20,16},{24,28},{28,24},{1,5},{5... | collective-permute-start | bytes 2359304 | tf_op jit(solution)/shard_map/ppermute | solution.py:407
  2.6 3.5 %collective-permute-start.5 = (bf16[512,256]{1,0:T(8,128)(2,1)S(1)}, bf16[512,256]{1,0:T(8,128)(2,1)S(1)}, u32[]{:S(2)}, u32[]{:S(2)}) collective-permute-start(bf16[512,256]{1,0:T(8,128)(2,1)S(1)} %get-tuple-element.50), channel_id=1, source_target_pairs={{0,24},{4,28},{8,16},{12,20},{16,8},{20,12},{24,0},{28,4},{1,25},{... | collective-permute-start | bytes 786440 | tf_op jit(solution)/shard_map/ppermute | solution.py:407
  6.1 0.5 %collective-permute-start.3 = (bf16[512,256]{1,0:T(8,128)(2,1)S(1)}, bf16[512,256]{1,0:T(8,128)(2,1)S(1)}, u32[]{:S(2)}, u32[]{:S(2)}) collective-permute-start(bf16[512,256]{1,0:T(8,128)(2,1)S(1)} %get-tuple-element.50), channel_id=1, source_target_pairs={{0,16},{4,20},{8,24},{12,28},{16,0},{20,4},{24,8},{28,12},{1,17},{... | collective-permute-start | bytes 786440 | tf_op jit(solution)/shard_map/ppermute | solution.py:407
  6.6 0.1 collective-permute-start.1
  6.8 0.0 collective-permute-done.refs_3_.refs_2_
  6.8 6.2 %all-to-all-start = ((s32[32,1,128]{2,1,0:T(1,128)}), s32[32,1,128]{2,1,0:T(1,128)S(1)}, u32[]{:S(2)}, u32[]{:S(2)}) async-start(s32[32,1,128]{2,1,0:T(1,128)} %bitcast.2), calls=%async_computation | async-start | bytes 32768 | tf_op jit(solution)/shard_map/all_to_all | solution.py:448
  13.0 0.3 collective-permute-done.5.refs_8_
  13.3 6.8 %all-to-all-done = s32[32,1,128]{2,1,0:T(1,128)S(1)} async-done(((s32[32,1,128]{2,1,0:T(1,128)}), s32[32,1,128]{2,1,0:T(1,128)S(1)}, u32[]{:S(2)}, u32[]{:S(2)}) %all-to-all-start) | async-done | bytes 16416 | tf_op jit(solution)/shard_map/all_to_all | solution.py:448
  20.1 0.0 collective-permute-done.3.refs_6_
  20.1 0.0 collective-permute-done.1.refs_4_
  20.1 0.0 collective-permute-start.2
  20.1 0.5 %collective-permute-start.4 = (bf16[512,256]{1,0:T(8,128)(2,1)S(1)}, bf16[512,256]{1,0:T(8,128)(2,1)S(1)}, u32[]{:S(2)}, u32[]{:S(2)}) collective-permute-start(bf16[512,256]{1,0:T(8,128)(2,1)S(1)} %collective-permute-done.3.refs_6_), channel_id=1, source_target_pairs={{0,4},{4,0},{8,12},{12,8},{16,20},{20,16},{24,28},{28,24},{1,5},{5... | collective-permute-start | bytes 786440 | tf_op jit(solution)/shard_map/ppermute | solution.py:407
  20.6 0.1 collective-permute-start.6
  20.7 1.4 %collective-permute-start.9 = (bf16[512,256]{1,0:T(8,128)(2,1)S(1)}, bf16[512,256]{1,0:T(8,128)(2,1)S(1)}, u32[]{:S(2)}, u32[]{:S(2)}) collective-permute-start(bf16[512,256]{1,0:T(8,128)(2,1)S(1)} %get-tuple-element.70), channel_id=1, source_target_pairs={{4,8},{12,16},{20,24},{28,0},{8,4},{16,12},{24,20},{0,28},{5,9},{1... | collective-permute-start | bytes 786440 | tf_op jit(solution)/shard_map/ppermute | solution.py:451
  22.1 0.0 collective-permute-done.2.refs_5_
  22.1 0.0 collective-permute-done.4.refs_7_
  22.1 0.3 collective-permute-done.6.refs_9_
  22.4 4.0 %shard_map.85 = (bf16[4096,256]{1,0:T(8,128)(2,1)S(1)}, bf16[512,256]{1,0:T(8,128)(2,1)S(1)}, bf16[512,256]{1,0:T(8,128)(2,1)S(1)}, bf16[512,512]{1,0:T(8,128)(2...) custom-call(s32[32,128]{1,0:T(8,128)S(1)} %bitcast.5, ...), custom_call_target="tpu_custom_call" | custom-call | flops 5750000128 | bytes 7103232 | tf_op jit(solution)/shard_map/pallas_call | solution.py:33
  26.5 0.2 collective-permute-start.7
  26.7 1.7 %shard_map.86 = (bf16[4096,256]{1,0:T(8,128)(2,1)S(1)}, bf16[512,256]{1,0:T(8,128)(2,1)S(1)}, f32[512,512]{1,0:T(8,128)S(1)}, f32[512,512]{1,0:T(8,128)S(1)}) custom-call(s32[192]{0:T(256)S(1)} %get-tuple-element.53.refs_0_, bf16[4096,256]{1,0:T(8,128)(2,1)S(1)} %get-tuple-element.54.refs_1_, ...), custom_call_target="tpu_custom_call", output_to_operand_aliasing={{0}: (1, {})} | custom-call | flops 2300000000 | bytes 8127232 | tf_op jit(solution)/shard_map/pallas_call | solution.py:33
  28.4 0.0 collective-permute-done.7.other_ref
  28.4 0.7 %collective-permute-start.8 = (f32[32,128]{1,0:T(8,128)S(1)}, f32[32,128]{1,0:T(8,128)S(1)}, u32[]{:S(2)}, u32[]{:S(2)}) collective-permute-start(f32[32,128]{1,0:T(8,128)S(1)} %shard_map.87.own_ref), channel_id=1, source_target_pairs={{0,8},{4,12},{8,0},{12,4},{16,24},{20,28},{24,16},{28,20},{1,9},{5... | collective-permute-start | bytes 49160 | tf_op jit(solution)/shard_map/ppermute | solution.py:407
  29.1 0.9 %collective-permute-done.9.refs_3_ = bf16[512,256]{1,0:T(8,128)(2,1)S(1)} collective-permute-done((bf16[512,256]{1,0:T(8,128)(2,1)S(1)}, bf16[512,256]{1,0:T(8,128)(2,1)S(1)}, u32[]{:S(2)}, u32[]{:S(2)}) %collective-permute-start.9) | collective-permute-done | bytes 262176 | tf_op jit(solution)/shard_map/ppermute | solution.py:451
  30.0 1.2 %shard_map.88 = (bf16[512,768]{1,0:T(8,128)(2,1)S(1)}, bf16[512,768]{1,0:T(8,128)(2,1)S(1)}, f32[8,512]{1,0:T(8,128)S(1)}, bf16[1024,128]{1,0:T(8,128)(2,1)S(1)}, bf16[1024,128]{1,0:T(8,128)(2,1)S(1)}) custom-call(bf16[512,256]{1,0:T(8,128)(2,1)S(1)} %get-tuple-element.67.refs_0_, bf16[512,256]{1,0:T(8,128)(2,1)S(1)} %get-tuple-element.68.refs_1_, ...), custom_call_target="tpu_custom_call" | custom-call | flops 1495000064 | bytes 3686400 | tf_op jit(solution)/shard_map/pallas_call | solution.py:33
  31.2 0.3 collective-permute-start.12
  31.5 0.4 %collective-permute-start.11 = (f32[8,512]{1,0:T(8,128)S(1)}, f32[8,512]{1,0:T(8,128)S(1)}, u32[]{:S(2)}, u32[]{:S(2)}) collective-permute-start(f32[8,512]{1,0:T(8,128)S(1)} %get-tuple-element.79.refs_4_), channel_id=1, source_target_pairs={{0,4},{4,0},{8,12},{12,8},{16,20},{20,16},{24,28},{28,24},{1,5},{5... | collective-permute-start | bytes 49160 | tf_op jit(solution)/shard_map/ppermute | solution.py:407
  31.9 0.3 collective-permute-done.8.other_ref
  32.2 0.8 %collective-permute-start.10 = (f32[64,128]{1,0:T(8,128)S(1)}, f32[64,128]{1,0:T(8,128)S(1)}, u32[]{:S(2)}, u32[]{:S(2)}) collective-permute-start(f32[64,128]{1,0:T(8,128)S(1)} %shard_map.89.refs_5_), channel_id=1, source_target_pairs={{0,16},{4,20},{8,24},{12,28},{16,0},{20,4},{24,8},{28,12},{1,17},{... | collective-permute-start | bytes 98312 | tf_op jit(solution)/shard_map/ppermute | solution.py:407
  33.0 0.7 %shard_map.90 = (bf16[512,256]{1,0:T(8,128)(2,1)S(1)}, bf16[512,256]{1,0:T(8,128)(2,1)S(1)}) custom-call(bf16[512,768]{1,0:T(8,128)(2,1)S(1)} %get-tuple-element.73.p_ref, bf16[512,768]{1,0:T(8,128)(2,1)S(1)} %get-tuple-element.74.ds_ref, bf16[1024,128]{1,0:T(8,128)(2,1)S(1)} %get-tuple-element.75.kx, bf16[1024,128]{1,0:T(8,128)(2,1)S(1)} %get-tuple-element.76.vx, ...), custom_call_target="tpu_custom_call" | custom-call | flops 230000000 | bytes 3407872 | tf_op jit(solution)/shard_map/pallas_call | solution.py:33
  33.7 1.6 %collective-permute-done.12.refs_6_ = f32[8,512]{1,0:T(8,128)S(1)} collective-permute-done((f32[8,512]{1,0:T(8,128)S(1)}, f32[8,512]{1,0:T(8,128)S(1)}, u32[]{:S(2)}, u32[]{:S(2)}) %collective-permute-start.12) | collective-permute-done | bytes 16416 | tf_op jit(solution)/shard_map/ppermute | solution.py:505
  35.3 0.0 collective-permute-done.11.refs_5_
  35.3 1.2 %shard_map.91 = (bf16[512,128]{1,0:T(8,128)(2,1)S(1)}, bf16[512,128]{1,0:T(8,128)(2,1)S(1)}) custom-call(bf16[512,256]{1,0:T(8,128)(2,1)S(1)} %get-tuple-element.67.refs_0_, bf16[512,256]{1,0:T(8,128)(2,1)S(1)} %get-tuple-element.68.refs_1_, bf16[512,768]{1,0:T(8,128)(2,1)S(1)} %collective-permute-done.refs_3_.refs_2_, ...), custom_call_target="tpu_custom_call" | custom-call | flops 230000000 | bytes 1884160 | tf_op jit(solution)/shard_map/pallas_call | solution.py:33
  36.6 0.0 collective-permute-done.10.refs_6_
  36.6 2.7 %shard_map.92 = (bf16[512,256]{1,0:T(8,128)(2,1)}, bf16[512,256]{1,0:T(8,128)(2,1)}, bf16[512,256]{1,0:T(8,128)(2,1)}, bf16[512,256]{1,0:T(8,128)(2,1)}) custom-call(s32[192]{0:T(256)S(1)} %get-tuple-element.53.refs_0_, bf16[4096,256]{1,0:T(8,128)(2,1)S(1)} %get-tuple-element.59.refs_1_, bf16[512,512]{1,0:T(8,128)(2,1)S(1)} %get-tuple-element.60.back_ref.refs_2_, ...), custom_call_target="tpu_custom_call" | custom-call | flops 2990000128 | bytes 6619904 | tf_op jit(solution)/shard_map/pallas_call | solution.py:33
  (2 shorter events, 0.0 us)
Async XLA Ops:
  2.1 4.7 %collective-permute-start = (bf16[512,768]{1,0:T(8,128)(2,1)S(1)}, bf16[512,768]{1,0:T(8,128)(2,1)S(1)}, u32[]{:S(2)}, u32[]{:S(2)}) collective-permute-start(bf16[512,768]{1,0:T(8,128)(2,1)S(1)} %get-tuple-element.44), channel_id=1, source_target_pairs={{0,4},{4,0},{8,12},{12,8},{16,20},{20,16},{24,28},{28,24},{1,5},{5... | collective-permute-start | bytes 2359304 | tf_op jit(solution)/shard_map/ppermute | solution.py:407
  2.6 10.7 %collective-permute-start.5 = (bf16[512,256]{1,0:T(8,128)(2,1)S(1)}, bf16[512,256]{1,0:T(8,128)(2,1)S(1)}, u32[]{:S(2)}, u32[]{:S(2)}) collective-permute-start(bf16[512,256]{1,0:T(8,128)(2,1)S(1)} %get-tuple-element.50), channel_id=1, source_target_pairs={{0,24},{4,28},{8,16},{12,20},{16,8},{20,12},{24,0},{28,4},{1,25},{... | collective-permute-start | bytes 786440 | tf_op jit(solution)/shard_map/ppermute | solution.py:407
  6.1 14.0 %collective-permute-start.3 = (bf16[512,256]{1,0:T(8,128)(2,1)S(1)}, bf16[512,256]{1,0:T(8,128)(2,1)S(1)}, u32[]{:S(2)}, u32[]{:S(2)}) collective-permute-start(bf16[512,256]{1,0:T(8,128)(2,1)S(1)} %get-tuple-element.50), channel_id=1, source_target_pairs={{0,16},{4,20},{8,24},{12,28},{16,0},{20,4},{24,8},{28,12},{1,17},{... | collective-permute-start | bytes 786440 | tf_op jit(solution)/shard_map/ppermute | solution.py:407
  6.6 13.5 %collective-permute-start.1 = (bf16[512,256]{1,0:T(8,128)(2,1)S(1)}, bf16[512,256]{1,0:T(8,128)(2,1)S(1)}, u32[]{:S(2)}, u32[]{:S(2)}) collective-permute-start(bf16[512,256]{1,0:T(8,128)(2,1)S(1)} %get-tuple-element.48), channel_id=1, source_target_pairs={{0,8},{4,12},{8,0},{12,4},{16,24},{20,28},{24,16},{28,20},{1,9},{5... | collective-permute-start | bytes 786440 | tf_op jit(solution)/shard_map/ppermute | solution.py:407
  6.8 13.4 %all-to-all-start = ((s32[32,1,128]{2,1,0:T(1,128)}), s32[32,1,128]{2,1,0:T(1,128)S(1)}, u32[]{:S(2)}, u32[]{:S(2)}) async-start(s32[32,1,128]{2,1,0:T(1,128)} %bitcast.2), calls=%async_computation | async-start | bytes 32768 | tf_op jit(solution)/shard_map/all_to_all | solution.py:448
  20.1 2.0 %collective-permute-start.2 = (bf16[512,256]{1,0:T(8,128)(2,1)S(1)}, bf16[512,256]{1,0:T(8,128)(2,1)S(1)}, u32[]{:S(2)}, u32[]{:S(2)}) collective-permute-start(bf16[512,256]{1,0:T(8,128)(2,1)S(1)} %collective-permute-done.1.refs_4_), channel_id=1, source_target_pairs={{0,4},{4,0},{8,12},{12,8},{16,20},{20,16},{24,28},{28,24},{1,5},{5... | collective-permute-start | bytes 786440 | tf_op jit(solution)/shard_map/ppermute | solution.py:407
  20.1 2.0 %collective-permute-start.4 = (bf16[512,256]{1,0:T(8,128)(2,1)S(1)}, bf16[512,256]{1,0:T(8,128)(2,1)S(1)}, u32[]{:S(2)}, u32[]{:S(2)}) collective-permute-start(bf16[512,256]{1,0:T(8,128)(2,1)S(1)} %collective-permute-done.3.refs_6_), channel_id=1, source_target_pairs={{0,4},{4,0},{8,12},{12,8},{16,20},{20,16},{24,28},{28,24},{1,5},{5... | collective-permute-start | bytes 786440 | tf_op jit(solution)/shard_map/ppermute | solution.py:407
  20.6 1.8 %collective-permute-start.6 = (bf16[512,256]{1,0:T(8,128)(2,1)S(1)}, bf16[512,256]{1,0:T(8,128)(2,1)S(1)}, u32[]{:S(2)}, u32[]{:S(2)}) collective-permute-start(bf16[512,256]{1,0:T(8,128)(2,1)S(1)} %collective-permute-done.5.refs_8_), channel_id=1, source_target_pairs={{0,4},{4,0},{8,12},{12,8},{16,20},{20,16},{24,28},{28,24},{1,5},{5... | collective-permute-start | bytes 786440 | tf_op jit(solution)/shard_map/ppermute | solution.py:407
  20.7 9.3 %collective-permute-start.9 = (bf16[512,256]{1,0:T(8,128)(2,1)S(1)}, bf16[512,256]{1,0:T(8,128)(2,1)S(1)}, u32[]{:S(2)}, u32[]{:S(2)}) collective-permute-start(bf16[512,256]{1,0:T(8,128)(2,1)S(1)} %get-tuple-element.70), channel_id=1, source_target_pairs={{4,8},{12,16},{20,24},{28,0},{8,4},{16,12},{24,20},{0,28},{5,9},{1... | collective-permute-start | bytes 786440 | tf_op jit(solution)/shard_map/ppermute | solution.py:451
  26.5 1.9 %collective-permute-start.7 = (f32[16,128]{1,0:T(8,128)S(1)}, f32[16,128]{1,0:T(8,128)S(1)}, u32[]{:S(2)}, u32[]{:S(2)}) collective-permute-start(f32[16,128]{1,0:T(8,128)S(1)} %get-tuple-element.63.own_ref), channel_id=1, source_target_pairs={{0,4},{4,0},{8,12},{12,8},{16,20},{20,16},{24,28},{28,24},{1,5},{5... | collective-permute-start | bytes 24584 | tf_op jit(solution)/shard_map/ppermute | solution.py:407
  28.4 3.8 %collective-permute-start.8 = (f32[32,128]{1,0:T(8,128)S(1)}, f32[32,128]{1,0:T(8,128)S(1)}, u32[]{:S(2)}, u32[]{:S(2)}) collective-permute-start(f32[32,128]{1,0:T(8,128)S(1)} %shard_map.87.own_ref), channel_id=1, source_target_pairs={{0,8},{4,12},{8,0},{12,4},{16,24},{20,28},{24,16},{28,20},{1,9},{5... | collective-permute-start | bytes 49160 | tf_op jit(solution)/shard_map/ppermute | solution.py:407
  31.2 4.1 %collective-permute-start.12 = (f32[8,512]{1,0:T(8,128)S(1)}, f32[8,512]{1,0:T(8,128)S(1)}, u32[]{:S(2)}, u32[]{:S(2)}) collective-permute-start(f32[8,512]{1,0:T(8,128)S(1)} %get-tuple-element.79.refs_4_), channel_id=1, source_target_pairs={{4,8},{12,16},{20,24},{28,0},{8,4},{16,12},{24,20},{0,28},{5,9},{1... | collective-permute-start | bytes 49160 | tf_op jit(solution)/shard_map/ppermute | solution.py:505
  31.5 3.8 %collective-permute-start.11 = (f32[8,512]{1,0:T(8,128)S(1)}, f32[8,512]{1,0:T(8,128)S(1)}, u32[]{:S(2)}, u32[]{:S(2)}) collective-permute-start(f32[8,512]{1,0:T(8,128)S(1)} %get-tuple-element.79.refs_4_), channel_id=1, source_target_pairs={{0,4},{4,0},{8,12},{12,8},{16,20},{20,16},{24,28},{28,24},{1,5},{5... | collective-permute-start | bytes 49160 | tf_op jit(solution)/shard_map/ppermute | solution.py:407
  32.2 4.3 %collective-permute-start.10 = (f32[64,128]{1,0:T(8,128)S(1)}, f32[64,128]{1,0:T(8,128)S(1)}, u32[]{:S(2)}, u32[]{:S(2)}) collective-permute-start(f32[64,128]{1,0:T(8,128)S(1)} %shard_map.89.refs_5_), channel_id=1, source_target_pairs={{0,16},{4,20},{8,24},{12,28},{16,0},{20,4},{24,8},{28,12},{1,17},{... | collective-permute-start | bytes 98312 | tf_op jit(solution)/shard_map/ppermute | solution.py:407

commit v5 on v4

--- a/solution.py
+++ b/solution.py
@@ -163,7 +163,9 @@
         st_ref[1:2, here] = to_row(delta)
 
 
-def query_outputs(tok, hd, tile, p_ref, ds_ref, kx, vx, back_ref, outs_ref, out_ref, dq_ref):
+def query_outputs(tok, hd, tile, *refs):
+    p_ref, ds_ref, kx, vx, back_ref, outs_ref = refs[:6]
+    out_ref, dq_ref = refs[10:12]
     span = tok + tile
     for lo in range(0, tok, tile):
         here = slice(lo, lo + tile)
@@ -172,40 +174,37 @@
     back = dot(back_ref[...], outs_ref[...]).astype(BF16)
     out_ref[:, hd:] = back[:, 0:hd]
     dq_ref[:, hd:] = back[:, hd:]
-
-
-def window_keys(tok, hd, tile, *refs):
-    kv_ref, qg_ref, near_ref, far_ref, st_ref, near_st, far_st, dk_ref, dv_ref, qx, gx, stx = refs
+    window_key_scores(tok, hd, tile, *refs[6:10], *refs[12:])
+
+
+def window_key_scores(tok, hd, tile, kv_ref, qg_ref, near_ref, far_ref, s_ref, dp_ref, qx, gx):
     scale = 1.0 / math.sqrt(hd)
     neighbour(0, near_ref, 2, far_ref, (qx, gx), tok)
     qx[0:tok] = qg_ref[:, 0:hd]
     gx[0:tok] = qg_ref[:, hd:]
-    stx[:, 0:tok] = st_ref[...]
-    even = (lax.axis_index("seq") & 1) == 0
-
-    @pl.when(even)
-    def _():
-        stx[:, tok:] = near_st[...]
-
-    @pl.when(jnp.logical_not(even))
-    def _():
-        stx[:, tok:] = far_st[...]
-
     last = jnp.where(lax.axis_index("seq") == lax.axis_size("seq") - 1, tok, 2 * tok)
     span = tok + tile
     row = lax.broadcasted_iota(jnp.int32, (tile, span), 0)
     col = lax.broadcasted_iota(jnp.int32, (tile, span), 1)
     for lo in range(0, tok, tile):
         here = slice(lo, lo + tile)
-        queries = qx[lo : lo + span]
-        grads = gx[lo : lo + span]
         allowed = (col >= row) & (col < row + tok) & (col + lo < last)
-        s = dot(kv_ref[here, 0:hd], queries, NT) * scale
-        p = jnp.exp(jnp.where(allowed, s - stx[0:1, lo : lo + span], NEG))
-        dv_ref[here, 0:hd] = dot(p.astype(BF16), grads).astype(BF16)
-        dp = dot(kv_ref[here, hd:], grads, NT)
-        ds = (p * (dp - stx[1:2, lo : lo + span]) * scale).astype(BF16)
-        dk_ref[here, 0:hd] = dot(ds, queries).astype(BF16)
+        s = dot(kv_ref[here, 0:hd], qx[lo : lo + span], NT) * scale
+        s_ref[here, :] = jnp.where(allowed, s, NEG)
+        dp_ref[here, :] = dot(kv_ref[here, hd:], gx[lo : lo + span], NT)
+
+
+def window_keys(tok, hd, tile, s_ref, dp_ref, qx, gx, st_ref, next_ref, dk_ref, dv_ref, stx):
+    scale = 1.0 / math.sqrt(hd)
+    stx[:, 0:tok] = st_ref[...]
+    stx[:, tok:] = next_ref[...]
+    span = tok + tile
+    for lo in range(0, tok, tile):
+        here = slice(lo, lo + tile)
+        p = jnp.exp(s_ref[here, :] - stx[0:1, lo : lo + span])
+        dv_ref[here, 0:hd] = dot(p.astype(BF16), gx[lo : lo + span]).astype(BF16)
+        ds = (p * (dp_ref[here, :] - stx[1:2, lo : lo + span]) * scale).astype(BF16)
+        dk_ref[here, 0:hd] = dot(ds, qx[lo : lo + span]).astype(BF16)
 
 
 def log2(n):
@@ -359,20 +358,23 @@
     lax.fori_loop(0, shards, key_step, 0, unroll=min(shards, 8))
 
 
-def key_outputs(cfg, *refs):
+def key_outputs(cfg, tile, *refs):
     shards, g, hd = cfg["shards"], cfg["g"], cfg["hd"]
-    tab, rows_ref, back_ref, s_ref, dp_ref, near_ref, far_ref, out_in, dq_in, dkw_ref, dvw_ref = refs[:11]
-    out_ref, dq_ref, dk_ref, dv_ref, stats, outs, sems = refs[11:]
+    (tab_ref, rows_ref, back_ref, s_ref, dp_ref, near_ref, far_ref, out_in, dq_in), refs = refs[:9], refs[9:]
+    window, (out_ref, dq_ref, dk_ref, dv_ref), refs = refs[:6], refs[6:10], refs[10:]
+    tab, stats, outs, sems = refs[:4]
     scale = 1.0 / math.sqrt(hd)
     me = lax.axis_index("seq")
     copies = [
         pltpu.make_async_copy(out_in, out_ref, sems.at[0]),
         pltpu.make_async_copy(dq_in, dq_ref, sems.at[1]),
     ]
+    load = pltpu.make_async_copy(tab_ref, tab, sems.at[2])
+    load.start()
     for copy in copies:
         copy.start()
-    dk_ref[:, 0:hd] = dkw_ref[...]
-    dv_ref[:, 0:hd] = dvw_ref[...]
+    window_keys(cfg["tok"], hd, tile, *window, dk_ref, dv_ref, *refs[4:])
+    load.wait()
     join(near_ref, far_ref, stats)
     query_at = lax.broadcasted_iota(jnp.int32, (g, CLUS), 1)
     key_at = lax.broadcasted_iota(jnp.int32, (g, CLUS), 0)
@@ -479,7 +481,7 @@
         rows_of = held.shape[0]
         return call(join, [shape(2 * rows_of, LANES, dtype=F32)], [held, other], vmem=2)[0]
 
-    held, other = gather_step(st_c, 0)
+    other, beyond = partner(st_c, "seq", 1), partner(st_c, "seq", 2)
     scored = shape(tok, CLUS, dtype=F32)
     rows, outs, s, dp = call(
         functools.partial(finish_queries, cfg),
@@ -490,48 +492,42 @@
         aliases={1: 0},
         vmem=6 * big,
     )
-    for bit in range(1, bits - 1):
-        held, other = gather_step(joined(held, after(other, outs)), bit)
+    behind = partner(after(beyond, outs), "seq", 1)
     window = shape(tok, tok + tile)
     longer = shape(2 * tok, hd)
     p_w, ds_w, st_w, kx, vx = call(
         functools.partial(window_scores, tok, hd, tile),
         [window, window, shape(8, tok, dtype=F32), longer, longer],
-        [after(kv_w, outs, held), qg_w, got[1], far],
+        [after(kv_w, outs), qg_w, got[1], far],
         us=1.3,
         vmem=8,
     )
-    near_st = partner(st_w, "seq", 1)
-    far_st = lax.ppermute(st_w, "seq", crossing)
-    held, other = gather_step(joined(held, after(other, st_w)), bits - 1)
-    out_all, dq_all = call(
+    held, other = joined(st_c, other), joined(beyond, after(behind, st_w))
+    for bit in range(2, bits):
+        held, other = gather_step(joined(held, other), bit)
+    st_next = lax.ppermute(st_w, "seq", [((i + 1) % shards, i) for i in range(shards)])
+    scores = shape(tok, tok + tile, dtype=F32)
+    out_all, dq_all, s_w, dp_w, qx, gx = call(
         functools.partial(query_outputs, tok, hd, tile),
-        [full, full],
-        [p_w, ds_w, kx, vx, back, outs],
+        [full, full, scores, scores, longer, longer],
+        [p_w, ds_w, kx, vx, back, outs, kv_w, qg_w, got[1], far],
         us=0.2,
-        vmem=8,
-    )
-    dk_w, dv_w = call(
-        functools.partial(window_keys, tok, hd, tile),
-        [shape(tok, hd)] * 2,
-        [kv_w, qg_w, got[1], far, after(st_w, out_all), near_st, far_st],
-        scratch=[pltpu.VMEM((2 * tok, hd), BF16)] * 2 + [pltpu.VMEM((8, 2 * tok), F32)],
-        us=0.2,
-        vmem=8,
+        vmem=12,
     )
     return call(
-        functools.partial(key_outputs, cfg),
+        functools.partial(key_outputs, cfg, tile),
         [full] * 4,
-        [tab, rows, back, s, dp, held, other, out_all, dq_all, dk_w, dv_w],
+        [tab, rows, back, s, dp, held, other, out_all, dq_all, s_w, dp_w, qx, gx, st_w, st_next],
         scratch=[
+            pltpu.SMEM((table,), jnp.int32),
             pltpu.VMEM((2 * shards * shards, LANES), F32),
             pltpu.VMEM((tok, 2 * hd), BF16),
-            pltpu.SemaphoreType.DMA((2,)),
+            pltpu.SemaphoreType.DMA((3,)),
+            pltpu.VMEM((8, 2 * tok), F32),
         ],
-        smem=(0,),
         hbm_outs=(0, 1),
-        us=2.6,
-        vmem=4 * big,
+        us=3.3,
+        vmem=5 * big,
     )
 
 

time: 39.5 us -> 38.4 us (0.972)
  waiting for transfers between devices: 10.2 us -> 9.21 us
    ppermute x1, waiting for transfers between devices: 1.58 us -> 0.01 us  [on_device(): lax.ppermute(st_w, 'seq', [((i + 1) % shards, i) for i in range(shards)])]
    ppermute x11, waiting for transfers between devices: 0.92 us -> 2.4 us  [partner(): lax.ppermute(array, axis, [(i, i ^ mask) for i in range(lax.axis_size(axi...]
    ppermute x1, starting transfers between devices: 0.33 us -> 1.27 us  [on_device(): lax.ppermute(st_w, 'seq', [((i + 1) % shards, i) for i in range(shards)])]
    ppermute x1, waiting for transfers between devices: 0.88 us -> 0.01 us  [on_device(): far = lax.ppermute(after(rim, lists), 'seq', crossing)]
    ppermute x11, starting transfers between devices: 7.34 us -> 6.57 us  [partner(): lax.ppermute(array, axis, [(i, i ^ mask) for i in range(lax.axis_size(axi...]
  transfers between devices with their start and end apart: 14 -> 14, of which waited for: 6 -> 5; matrix products, arithmetic and copies ran while one was open for 0% -> 0% of each run, Pallas kernels for 23% -> 22%
where the time goes in v5:
time: 38.4 us; the launch traced here: 38.2 us
  starting transfers between devices  15.5 us (40%)
  Pallas kernels  12.8 us (33%)
  waiting for transfers between devices  9.21 us (24%)
  between operations  0.73 us (2%)
    pallas_call x9, Pallas kernels, call(): pl.pallas_call(body, out_shape=outs, in_specs=[pl.BlockSpec(memory_space=...  12.8 us
    all_to_all x1, waiting for transfers between devices, on_device(): lax.all_to_all(after(spread, got[1]), ('seq', 'head'), 0, 0, tiled=True)  6.8 us
    ppermute x11, starting transfers between devices, partner(): lax.ppermute(array, axis, [(i, i ^ mask) for i in range(lax.axis_size(axi...  6.57 us
    all_to_all x1, starting transfers between devices, on_device(): lax.all_to_all(after(spread, got[1]), ('seq', 'head'), 0, 0, tiled=True)  6.25 us
    ppermute x11, waiting for transfers between devices, partner(): lax.ppermute(array, axis, [(i, i ^ mask) for i in range(lax.axis_size(axi...  2.4 us
    ppermute x1, starting transfers between devices, on_device(): far = lax.ppermute(after(rim, lists), 'seq', crossing)  1.39 us
    ppermute x1, starting transfers between devices, on_device(): lax.ppermute(st_w, 'seq', [((i + 1) % shards, i) for i in range(shards)])  1.27 us
  transfers between devices with their start and end apart: 14, of which 5 were waited for; matrix products, arithmetic and copies ran while one was open for 0% of the time, Pallas kernels for 22%

profile of v5, /device:TPU:0, one launch (start us, length us, event | category | flops | bytes accessed | tf_op | source)
XLA Modules:
  0.0 38.2 jit_solution(16442760949601849884)
XLA Ops:
  0.6 1.4 %shard_map.84 = (bf16[512,256]{1,0:T(8,128)(2,1)S(1)}, bf16[512,256]{1,0:T(8,128)(2,1)S(1)}, bf16[512,256]{1,0:T(8,128)(2,1)S(1)}, bf16[512,256]{1,0:T(8,128)(2,...) custom-call(s32[1,128]{1,0:T(1,128)} %bitcast.6, ...), custom_call_target="tpu_custom_call" | custom-call | bytes 3686912 | tf_op jit(solution)/shard_map/pallas_call | solution.py:33
  2.1 0.5 %collective-permute-start = (bf16[512,768]{1,0:T(8,128)(2,1)S(1)}, bf16[512,768]{1,0:T(8,128)(2,1)S(1)}, u32[]{:S(2)}, u32[]{:S(2)}) collective-permute-start(bf16[512,768]{1,0:T(8,128)(2,1)S(1)} %get-tuple-element.45), channel_id=1, source_target_pairs={{0,4},{4,0},{8,12},{12,8},{16,20},{20,16},{24,28},{28,24},{1,5},{5... | collective-permute-start | bytes 2359304 | tf_op jit(solution)/shard_map/ppermute | solution.py:409
  2.6 3.5 %collective-permute-start.5 = (bf16[512,256]{1,0:T(8,128)(2,1)S(1)}, bf16[512,256]{1,0:T(8,128)(2,1)S(1)}, u32[]{:S(2)}, u32[]{:S(2)}) collective-permute-start(bf16[512,256]{1,0:T(8,128)(2,1)S(1)} %get-tuple-element.51), channel_id=1, source_target_pairs={{0,24},{4,28},{8,16},{12,20},{16,8},{20,12},{24,0},{28,4},{1,25},{... | collective-permute-start | bytes 786440 | tf_op jit(solution)/shard_map/ppermute | solution.py:409
  6.1 0.5 %collective-permute-start.3 = (bf16[512,256]{1,0:T(8,128)(2,1)S(1)}, bf16[512,256]{1,0:T(8,128)(2,1)S(1)}, u32[]{:S(2)}, u32[]{:S(2)}) collective-permute-start(bf16[512,256]{1,0:T(8,128)(2,1)S(1)} %get-tuple-element.51), channel_id=1, source_target_pairs={{0,16},{4,20},{8,24},{12,28},{16,0},{20,4},{24,8},{28,12},{1,17},{... | collective-permute-start | bytes 786440 | tf_op jit(solution)/shard_map/ppermute | solution.py:409
  6.6 0.1 collective-permute-start.1
  6.8 0.0 collective-permute-done.refs_3_.refs_2_.refs_8_
  6.8 6.2 %all-to-all-start = ((s32[32,1,128]{2,1,0:T(1,128)}), s32[32,1,128]{2,1,0:T(1,128)S(1)}, u32[]{:S(2)}, u32[]{:S(2)}) async-start(s32[32,1,128]{2,1,0:T(1,128)} %bitcast.2), calls=%async_computation | async-start | bytes 32768 | tf_op jit(solution)/shard_map/all_to_all | solution.py:450
  13.0 0.3 collective-permute-done.5.refs_8_
  13.3 6.8 %all-to-all-done = s32[32,1,128]{2,1,0:T(1,128)S(1)} async-done(((s32[32,1,128]{2,1,0:T(1,128)}), s32[32,1,128]{2,1,0:T(1,128)S(1)}, u32[]{:S(2)}, u32[]{:S(2)}) %all-to-all-start) | async-done | bytes 16416 | tf_op jit(solution)/shard_map/all_to_all | solution.py:450
  20.1 0.0 collective-permute-start.6
  20.1 0.0 collective-permute-done.3.refs_6_
  20.1 0.5 %collective-permute-start.4 = (bf16[512,256]{1,0:T(8,128)(2,1)S(1)}, bf16[512,256]{1,0:T(8,128)(2,1)S(1)}, u32[]{:S(2)}, u32[]{:S(2)}) collective-permute-start(bf16[512,256]{1,0:T(8,128)(2,1)S(1)} %collective-permute-done.3.refs_6_), channel_id=1, source_target_pairs={{0,4},{4,0},{8,12},{12,8},{16,20},{20,16},{24,28},{28,24},{1,5},{5... | collective-permute-start | bytes 786440 | tf_op jit(solution)/shard_map/ppermute | solution.py:409
  20.6 0.0 collective-permute-done.1.refs_4_
  20.6 0.1 collective-permute-start.2
  20.7 1.4 %collective-permute-start.10 = (bf16[512,256]{1,0:T(8,128)(2,1)S(1)}, bf16[512,256]{1,0:T(8,128)(2,1)S(1)}, u32[]{:S(2)}, u32[]{:S(2)}) collective-permute-start(bf16[512,256]{1,0:T(8,128)(2,1)S(1)} %get-tuple-element.71), channel_id=1, source_target_pairs={{4,8},{12,16},{20,24},{28,0},{8,4},{16,12},{24,20},{0,28},{5,9},{1... | collective-permute-start | bytes 786440 | tf_op jit(solution)/shard_map/ppermute | solution.py:453
  22.1 0.0 collective-permute-done.6.refs_9_
  22.1 0.0 collective-permute-done.4.refs_7_
  22.1 0.3 collective-permute-done.2.refs_5_
  22.4 4.0 %shard_map.85 = (bf16[4096,256]{1,0:T(8,128)(2,1)S(1)}, bf16[512,256]{1,0:T(8,128)(2,1)S(1)}, bf16[512,256]{1,0:T(8,128)(2,1)S(1)}, bf16[512,512]{1,0:T(8,128)(2...) custom-call(s32[32,128]{1,0:T(8,128)S(1)} %bitcast.5, ...), custom_call_target="tpu_custom_call" | custom-call | flops 5750000128 | bytes 7103232 | tf_op jit(solution)/shard_map/pallas_call | solution.py:33
  26.4 0.6 %collective-permute-start.8 = (f32[16,128]{1,0:T(8,128)S(1)}, f32[16,128]{1,0:T(8,128)S(1)}, u32[]{:S(2)}, u32[]{:S(2)}) collective-permute-start(f32[16,128]{1,0:T(8,128)S(1)} %get-tuple-element.64.own_ref), channel_id=1, source_target_pairs={{0,8},{4,12},{8,0},{12,4},{16,24},{20,28},{24,16},{28,20},{1,9},{5... | collective-permute-start | bytes 24584 | tf_op jit(solution)/shard_map/ppermute | solution.py:409
  27.1 0.0 collective-permute-start.7
  27.1 1.7 %shard_map.86 = (bf16[4096,256]{1,0:T(8,128)(2,1)S(1)}, bf16[512,256]{1,0:T(8,128)(2,1)S(1)}, f32[512,512]{1,0:T(8,128)S(1)}, f32[512,512]{1,0:T(8,128)S(1)}) custom-call(s32[192]{0:T(256)S(1)} %get-tuple-element.54.refs_0_, bf16[4096,256]{1,0:T(8,128)(2,1)S(1)} %get-tuple-element.55.refs_1_, ...), custom_call_target="tpu_custom_call", output_to_operand_aliasing={{0}: (1, {})} | custom-call | flops 2300000000 | bytes 8127232 | tf_op jit(solution)/shard_map/pallas_call | solution.py:33
  28.8 1.3 %collective-permute-done.8.own_ref = f32[16,128]{1,0:T(8,128)S(1)} collective-permute-done((f32[16,128]{1,0:T(8,128)S(1)}, f32[16,128]{1,0:T(8,128)S(1)}, u32[]{:S(2)}, u32[]{:S(2)}) %collective-permute-start.8) | collective-permute-done | bytes 8224 | tf_op jit(solution)/shard_map/ppermute | solution.py:409
  30.2 0.0 collective-permute-start.9
  30.2 0.0 collective-permute-done.10.refs_3_.refs_9_
  30.2 1.2 %shard_map.88 = (bf16[512,768]{1,0:T(8,128)(2,1)S(1)}, bf16[512,768]{1,0:T(8,128)(2,1)S(1)}, f32[8,512]{1,0:T(8,128)S(1)}, bf16[1024,128]{1,0:T(8,128)(2,1)S(1)}, bf16[1024,128]{1,0:T(8,128)(2,1)S(1)}) custom-call(bf16[512,256]{1,0:T(8,128)(2,1)S(1)} %get-tuple-element.68.refs_0_.refs_6_, bf16[512,256]{1,0:T(8,128)(2,1)S(1)} %get-tuple-element.69.refs_1_.refs_7_, ...), custom_call_target="tpu_custom_call" | custom-call | flops 1495000064 | bytes 3686400 | tf_op jit(solution)/shard_map/pallas_call | solution.py:33
  31.4 0.0 collective-permute-done.7.other_ref
  31.4 0.0 collective-permute-done.9.other_ref
  31.5 0.7 %collective-permute-start.11 = (f32[64,128]{1,0:T(8,128)S(1)}, f32[64,128]{1,0:T(8,128)S(1)}, u32[]{:S(2)}, u32[]{:S(2)}) collective-permute-start(f32[64,128]{1,0:T(8,128)S(1)} %shard_map.90.refs_5_), channel_id=1, source_target_pairs={{0,16},{4,20},{8,24},{12,28},{16,0},{20,4},{24,8},{28,12},{1,17},{... | collective-permute-start | bytes 98312 | tf_op jit(solution)/shard_map/ppermute | solution.py:409
  32.1 1.3 %collective-permute-start.12 = (f32[8,512]{1,0:T(8,128)S(1)}, f32[8,512]{1,0:T(8,128)S(1)}, u32[]{:S(2)}, u32[]{:S(2)}) collective-permute-start(f32[8,512]{1,0:T(8,128)S(1)} %get-tuple-element.72.refs_13_), channel_id=1, source_target_pairs={{4,0},{8,4},{12,8},{16,12},{20,16},{24,20},{28,24},{0,28},{5,1},{9... | collective-permute-start | bytes 49160 | tf_op jit(solution)/shard_map/ppermute | solution.py:508
  33.4 1.6 %shard_map.91 = (bf16[512,256]{1,0:T(8,128)(2,1)S(1)}, bf16[512,256]{1,0:T(8,128)(2,1)S(1)}, f32[512,768]{1,0:T(8,128)S(1)}, f32[512,768]{1,0:T(8,128)S(1)}, bf1...) custom-call(bf16[512,768]{1,0:T(8,128)(2,1)S(1)} %get-tuple-element.74.refs_0_, ...), custom_call_target="tpu_custom_call" | custom-call | flops 230000000 | bytes 8650752 | tf_op jit(solution)/shard_map/pallas_call | solution.py:33
  35.0 0.0 collective-permute-done.12.refs_14_
  35.0 0.5 %collective-permute-done.11.refs_6_ = f32[64,128]{1,0:T(8,128)S(1)} collective-permute-done((f32[64,128]{1,0:T(8,128)S(1)}, f32[64,128]{1,0:T(8,128)S(1)}, u32[]{:S(2)}, u32[]{:S(2)}) %collective-permute-start.11) | collective-permute-done | bytes 32800 | tf_op jit(solution)/shard_map/ppermute | solution.py:409
  35.4 2.8 %shard_map.92 = (bf16[512,256]{1,0:T(8,128)(2,1)}, bf16[512,256]{1,0:T(8,128)(2,1)}, bf16[512,256]{1,0:T(8,128)(2,1)}, bf16[512,256]{1,0:T(8,128)(2,1)}) custom-call(s32[192]{0:T(256)S(1)} %get-tuple-element.54.refs_0_, bf16[4096,256]{1,0:T(8,128)(2,1)S(1)} %get-tuple-element.60.refs_1_, bf16[512,512]{1,0:T(8,128)(2,1)S(1)} %get-tuple-element.61.refs_4_.refs_2_, ...), custom_call_target="tpu_custom_call" | custom-call | flops 3795000064 | bytes 10060544 | tf_op jit(solution)/shard_map/pallas_call | solution.py:33
  (3 shorter events, 0.0 us)
Async XLA Ops:
  2.1 4.7 %collective-permute-start = (bf16[512,768]{1,0:T(8,128)(2,1)S(1)}, bf16[512,768]{1,0:T(8,128)(2,1)S(1)}, u32[]{:S(2)}, u32[]{:S(2)}) collective-permute-start(bf16[512,768]{1,0:T(8,128)(2,1)S(1)} %get-tuple-element.45), channel_id=1, source_target_pairs={{0,4},{4,0},{8,12},{12,8},{16,20},{20,16},{24,28},{28,24},{1,5},{5... | collective-permute-start | bytes 2359304 | tf_op jit(solution)/shard_map/ppermute | solution.py:409
  2.6 10.7 %collective-permute-start.5 = (bf16[512,256]{1,0:T(8,128)(2,1)S(1)}, bf16[512,256]{1,0:T(8,128)(2,1)S(1)}, u32[]{:S(2)}, u32[]{:S(2)}) collective-permute-start(bf16[512,256]{1,0:T(8,128)(2,1)S(1)} %get-tuple-element.51), channel_id=1, source_target_pairs={{0,24},{4,28},{8,16},{12,20},{16,8},{20,12},{24,0},{28,4},{1,25},{... | collective-permute-start | bytes 786440 | tf_op jit(solution)/shard_map/ppermute | solution.py:409
  6.1 14.0 %collective-permute-start.3 = (bf16[512,256]{1,0:T(8,128)(2,1)S(1)}, bf16[512,256]{1,0:T(8,128)(2,1)S(1)}, u32[]{:S(2)}, u32[]{:S(2)}) collective-permute-start(bf16[512,256]{1,0:T(8,128)(2,1)S(1)} %get-tuple-element.51), channel_id=1, source_target_pairs={{0,16},{4,20},{8,24},{12,28},{16,0},{20,4},{24,8},{28,12},{1,17},{... | collective-permute-start | bytes 786440 | tf_op jit(solution)/shard_map/ppermute | solution.py:409
  6.6 14.0 %collective-permute-start.1 = (bf16[512,256]{1,0:T(8,128)(2,1)S(1)}, bf16[512,256]{1,0:T(8,128)(2,1)S(1)}, u32[]{:S(2)}, u32[]{:S(2)}) collective-permute-start(bf16[512,256]{1,0:T(8,128)(2,1)S(1)} %get-tuple-element.49), channel_id=1, source_target_pairs={{0,8},{4,12},{8,0},{12,4},{16,24},{20,28},{24,16},{28,20},{1,9},{5... | collective-permute-start | bytes 786440 | tf_op jit(solution)/shard_map/ppermute | solution.py:409
  6.8 13.4 %all-to-all-start = ((s32[32,1,128]{2,1,0:T(1,128)}), s32[32,1,128]{2,1,0:T(1,128)S(1)}, u32[]{:S(2)}, u32[]{:S(2)}) async-start(s32[32,1,128]{2,1,0:T(1,128)} %bitcast.2), calls=%async_computation | async-start | bytes 32768 | tf_op jit(solution)/shard_map/all_to_all | solution.py:450
  20.1 2.0 %collective-permute-start.6 = (bf16[512,256]{1,0:T(8,128)(2,1)S(1)}, bf16[512,256]{1,0:T(8,128)(2,1)S(1)}, u32[]{:S(2)}, u32[]{:S(2)}) collective-permute-start(bf16[512,256]{1,0:T(8,128)(2,1)S(1)} %collective-permute-done.5.refs_8_), channel_id=1, source_target_pairs={{0,4},{4,0},{8,12},{12,8},{16,20},{20,16},{24,28},{28,24},{1,5},{5... | collective-permute-start | bytes 786440 | tf_op jit(solution)/shard_map/ppermute | solution.py:409
  20.1 2.0 %collective-permute-start.4 = (bf16[512,256]{1,0:T(8,128)(2,1)S(1)}, bf16[512,256]{1,0:T(8,128)(2,1)S(1)}, u32[]{:S(2)}, u32[]{:S(2)}) collective-permute-start(bf16[512,256]{1,0:T(8,128)(2,1)S(1)} %collective-permute-done.3.refs_6_), channel_id=1, source_target_pairs={{0,4},{4,0},{8,12},{12,8},{16,20},{20,16},{24,28},{28,24},{1,5},{5... | collective-permute-start | bytes 786440 | tf_op jit(solution)/shard_map/ppermute | solution.py:409
  20.6 1.8 %collective-permute-start.2 = (bf16[512,256]{1,0:T(8,128)(2,1)S(1)}, bf16[512,256]{1,0:T(8,128)(2,1)S(1)}, u32[]{:S(2)}, u32[]{:S(2)}) collective-permute-start(bf16[512,256]{1,0:T(8,128)(2,1)S(1)} %collective-permute-done.1.refs_4_), channel_id=1, source_target_pairs={{0,4},{4,0},{8,12},{12,8},{16,20},{20,16},{24,28},{28,24},{1,5},{5... | collective-permute-start | bytes 786440 | tf_op jit(solution)/shard_map/ppermute | solution.py:409
  20.7 9.5 %collective-permute-start.10 = (bf16[512,256]{1,0:T(8,128)(2,1)S(1)}, bf16[512,256]{1,0:T(8,128)(2,1)S(1)}, u32[]{:S(2)}, u32[]{:S(2)}) collective-permute-start(bf16[512,256]{1,0:T(8,128)(2,1)S(1)} %get-tuple-element.71), channel_id=1, source_target_pairs={{4,8},{12,16},{20,24},{28,0},{8,4},{16,12},{24,20},{0,28},{5,9},{1... | collective-permute-start | bytes 786440 | tf_op jit(solution)/shard_map/ppermute | solution.py:453
  26.4 3.7 %collective-permute-start.8 = (f32[16,128]{1,0:T(8,128)S(1)}, f32[16,128]{1,0:T(8,128)S(1)}, u32[]{:S(2)}, u32[]{:S(2)}) collective-permute-start(f32[16,128]{1,0:T(8,128)S(1)} %get-tuple-element.64.own_ref), channel_id=1, source_target_pairs={{0,8},{4,12},{8,0},{12,4},{16,24},{20,28},{24,16},{28,20},{1,9},{5... | collective-permute-start | bytes 24584 | tf_op jit(solution)/shard_map/ppermute | solution.py:409
  27.1 4.3 %collective-permute-start.7 = (f32[16,128]{1,0:T(8,128)S(1)}, f32[16,128]{1,0:T(8,128)S(1)}, u32[]{:S(2)}, u32[]{:S(2)}) collective-permute-start(f32[16,128]{1,0:T(8,128)S(1)} %get-tuple-element.64.own_ref), channel_id=1, source_target_pairs={{0,4},{4,0},{8,12},{12,8},{16,20},{20,16},{24,28},{28,24},{1,5},{5... | collective-permute-start | bytes 24584 | tf_op jit(solution)/shard_map/ppermute | solution.py:409
  30.2 1.3 %collective-permute-start.9 = (f32[16,128]{1,0:T(8,128)S(1)}, f32[16,128]{1,0:T(8,128)S(1)}, u32[]{:S(2)}, u32[]{:S(2)}) collective-permute-start(f32[16,128]{1,0:T(8,128)S(1)} %collective-permute-done.8.own_ref), channel_id=1, source_target_pairs={{0,4},{4,0},{8,12},{12,8},{16,20},{20,16},{24,28},{28,24},{1,5},{5... | collective-permute-start | bytes 24584 | tf_op jit(solution)/shard_map/ppermute | solution.py:409
  31.5 4.0 %collective-permute-start.11 = (f32[64,128]{1,0:T(8,128)S(1)}, f32[64,128]{1,0:T(8,128)S(1)}, u32[]{:S(2)}, u32[]{:S(2)}) collective-permute-start(f32[64,128]{1,0:T(8,128)S(1)} %shard_map.90.refs_5_), channel_id=1, source_target_pairs={{0,16},{4,20},{8,24},{12,28},{16,0},{20,4},{24,8},{28,12},{1,17},{... | collective-permute-start | bytes 98312 | tf_op jit(solution)/shard_map/ppermute | solution.py:409
  32.1 2.9 %collective-permute-start.12 = (f32[8,512]{1,0:T(8,128)S(1)}, f32[8,512]{1,0:T(8,128)S(1)}, u32[]{:S(2)}, u32[]{:S(2)}) collective-permute-start(f32[8,512]{1,0:T(8,128)S(1)} %get-tuple-element.72.refs_13_), channel_id=1, source_target_pairs={{4,0},{8,4},{12,8},{16,12},{20,16},{24,20},{28,24},{0,28},{5,1},{9... | collective-permute-start | bytes 49160 | tf_op jit(solution)/shard_map/ppermute | solution.py:508

commit v6 on v5

--- a/solution.py
+++ b/solution.py
@@ -473,7 +473,7 @@
         us=5.0,
         vmem=12 * big,
     )
-    tile = 256
+    tile = 128
     def gather_step(held, bit, *earlier):
         return held, partner(after(held, *earlier), "seq", 1 << bit)
 

time: 38.4 us -> 38.5 us (level)
  no operation moved by 1% of the time
where the time goes in v6:
time: 38.5 us; the launch traced here: 38.3 us
  starting transfers between devices  15.5 us (40%)
  Pallas kernels  12.8 us (33%)
  waiting for transfers between devices  9.27 us (24%)
  between operations  0.73 us (2%)
    pallas_call x9, Pallas kernels, call(): pl.pallas_call(body, out_shape=outs, in_specs=[pl.BlockSpec(memory_space=...  12.8 us
    all_to_all x1, waiting for transfers between devices, on_device(): lax.all_to_all(after(spread, got[1]), ('seq', 'head'), 0, 0, tiled=True)  6.8 us
    ppermute x11, starting transfers between devices, partner(): lax.ppermute(array, axis, [(i, i ^ mask) for i in range(lax.axis_size(axi...  6.57 us
    all_to_all x1, starting transfers between devices, on_device(): lax.all_to_all(after(spread, got[1]), ('seq', 'head'), 0, 0, tiled=True)  6.25 us
    ppermute x11, waiting for transfers between devices, partner(): lax.ppermute(array, axis, [(i, i ^ mask) for i in range(lax.axis_size(axi...  2.46 us
    ppermute x1, starting transfers between devices, on_device(): far = lax.ppermute(after(rim, lists), 'seq', crossing)  1.39 us
    ppermute x1, starting transfers between devices, on_device(): lax.ppermute(st_w, 'seq', [((i + 1) % shards, i) for i in range(shards)])  1.29 us
  transfers between devices with their start and end apart: 14, of which 5 were waited for; matrix products, arithmetic and copies ran while one was open for 0% of the time, Pallas kernels for 22%

profile of v6, /device:TPU:0, one launch (start us, length us, event | category | flops | bytes accessed | tf_op | source)
XLA Modules:
  0.0 38.3 jit_solution(1231956153690681220)
XLA Ops:
  0.6 1.4 %shard_map.84 = (bf16[512,256]{1,0:T(8,128)(2,1)S(1)}, bf16[512,256]{1,0:T(8,128)(2,1)S(1)}, bf16[512,256]{1,0:T(8,128)(2,1)S(1)}, bf16[512,256]{1,0:T(8,128)(2,...) custom-call(s32[1,128]{1,0:T(1,128)} %bitcast.6, ...), custom_call_target="tpu_custom_call" | custom-call | bytes 3686912 | tf_op jit(solution)/shard_map/pallas_call | solution.py:33
  2.1 0.5 %collective-permute-start = (bf16[512,768]{1,0:T(8,128)(2,1)S(1)}, bf16[512,768]{1,0:T(8,128)(2,1)S(1)}, u32[]{:S(2)}, u32[]{:S(2)}) collective-permute-start(bf16[512,768]{1,0:T(8,128)(2,1)S(1)} %get-tuple-element.45), channel_id=1, source_target_pairs={{0,4},{4,0},{8,12},{12,8},{16,20},{20,16},{24,28},{28,24},{1,5},{5... | collective-permute-start | bytes 2359304 | tf_op jit(solution)/shard_map/ppermute | solution.py:409
  2.6 3.5 %collective-permute-start.5 = (bf16[512,256]{1,0:T(8,128)(2,1)S(1)}, bf16[512,256]{1,0:T(8,128)(2,1)S(1)}, u32[]{:S(2)}, u32[]{:S(2)}) collective-permute-start(bf16[512,256]{1,0:T(8,128)(2,1)S(1)} %get-tuple-element.51), channel_id=1, source_target_pairs={{0,24},{4,28},{8,16},{12,20},{16,8},{20,12},{24,0},{28,4},{1,25},{... | collective-permute-start | bytes 786440 | tf_op jit(solution)/shard_map/ppermute | solution.py:409
  6.1 0.5 %collective-permute-start.3 = (bf16[512,256]{1,0:T(8,128)(2,1)S(1)}, bf16[512,256]{1,0:T(8,128)(2,1)S(1)}, u32[]{:S(2)}, u32[]{:S(2)}) collective-permute-start(bf16[512,256]{1,0:T(8,128)(2,1)S(1)} %get-tuple-element.51), channel_id=1, source_target_pairs={{0,16},{4,20},{8,24},{12,28},{16,0},{20,4},{24,8},{28,12},{1,17},{... | collective-permute-start | bytes 786440 | tf_op jit(solution)/shard_map/ppermute | solution.py:409
  6.6 0.1 collective-permute-start.1
  6.8 0.0 collective-permute-done.refs_3_.refs_2_.refs_8_
  6.8 6.2 %all-to-all-start = ((s32[32,1,128]{2,1,0:T(1,128)}), s32[32,1,128]{2,1,0:T(1,128)S(1)}, u32[]{:S(2)}, u32[]{:S(2)}) async-start(s32[32,1,128]{2,1,0:T(1,128)} %bitcast.2), calls=%async_computation | async-start | bytes 32768 | tf_op jit(solution)/shard_map/all_to_all | solution.py:450
  13.0 0.3 collective-permute-done.5.refs_8_
  13.3 6.8 %all-to-all-done = s32[32,1,128]{2,1,0:T(1,128)S(1)} async-done(((s32[32,1,128]{2,1,0:T(1,128)}), s32[32,1,128]{2,1,0:T(1,128)S(1)}, u32[]{:S(2)}, u32[]{:S(2)}) %all-to-all-start) | async-done | bytes 16416 | tf_op jit(solution)/shard_map/all_to_all | solution.py:450
  20.1 0.0 collective-permute-start.6
  20.1 0.0 collective-permute-done.3.refs_6_
  20.1 0.5 %collective-permute-start.4 = (bf16[512,256]{1,0:T(8,128)(2,1)S(1)}, bf16[512,256]{1,0:T(8,128)(2,1)S(1)}, u32[]{:S(2)}, u32[]{:S(2)}) collective-permute-start(bf16[512,256]{1,0:T(8,128)(2,1)S(1)} %collective-permute-done.3.refs_6_), channel_id=1, source_target_pairs={{0,4},{4,0},{8,12},{12,8},{16,20},{20,16},{24,28},{28,24},{1,5},{5... | collective-permute-start | bytes 786440 | tf_op jit(solution)/shard_map/ppermute | solution.py:409
  20.6 0.0 collective-permute-done.1.refs_4_
  20.6 0.1 collective-permute-start.2
  20.7 1.4 %collective-permute-start.10 = (bf16[512,256]{1,0:T(8,128)(2,1)S(1)}, bf16[512,256]{1,0:T(8,128)(2,1)S(1)}, u32[]{:S(2)}, u32[]{:S(2)}) collective-permute-start(bf16[512,256]{1,0:T(8,128)(2,1)S(1)} %get-tuple-element.71), channel_id=1, source_target_pairs={{4,8},{12,16},{20,24},{28,0},{8,4},{16,12},{24,20},{0,28},{5,9},{1... | collective-permute-start | bytes 786440 | tf_op jit(solution)/shard_map/ppermute | solution.py:453
  22.1 0.0 collective-permute-done.6.refs_9_
  22.1 0.0 collective-permute-done.4.refs_7_
  22.1 0.3 collective-permute-done.2.refs_5_
  22.4 4.0 %shard_map.85 = (bf16[4096,256]{1,0:T(8,128)(2,1)S(1)}, bf16[512,256]{1,0:T(8,128)(2,1)S(1)}, bf16[512,256]{1,0:T(8,128)(2,1)S(1)}, bf16[512,512]{1,0:T(8,128)(2...) custom-call(s32[32,128]{1,0:T(8,128)S(1)} %bitcast.5, ...), custom_call_target="tpu_custom_call" | custom-call | flops 5750000128 | bytes 7103232 | tf_op jit(solution)/shard_map/pallas_call | solution.py:33
  26.4 0.6 %collective-permute-start.8 = (f32[16,128]{1,0:T(8,128)S(1)}, f32[16,128]{1,0:T(8,128)S(1)}, u32[]{:S(2)}, u32[]{:S(2)}) collective-permute-start(f32[16,128]{1,0:T(8,128)S(1)} %get-tuple-element.64.own_ref), channel_id=1, source_target_pairs={{0,8},{4,12},{8,0},{12,4},{16,24},{20,28},{24,16},{28,20},{1,9},{5... | collective-permute-start | bytes 24584 | tf_op jit(solution)/shard_map/ppermute | solution.py:409
  27.1 0.0 collective-permute-start.7
  27.1 1.7 %shard_map.86 = (bf16[4096,256]{1,0:T(8,128)(2,1)S(1)}, bf16[512,256]{1,0:T(8,128)(2,1)S(1)}, f32[512,512]{1,0:T(8,128)S(1)}, f32[512,512]{1,0:T(8,128)S(1)}) custom-call(s32[192]{0:T(256)S(1)} %get-tuple-element.54.refs_0_, bf16[4096,256]{1,0:T(8,128)(2,1)S(1)} %get-tuple-element.55.refs_1_, ...), custom_call_target="tpu_custom_call", output_to_operand_aliasing={{0}: (1, {})} | custom-call | flops 2300000000 | bytes 8127232 | tf_op jit(solution)/shard_map/pallas_call | solution.py:33
  28.8 1.3 %collective-permute-done.8.own_ref = f32[16,128]{1,0:T(8,128)S(1)} collective-permute-done((f32[16,128]{1,0:T(8,128)S(1)}, f32[16,128]{1,0:T(8,128)S(1)}, u32[]{:S(2)}, u32[]{:S(2)}) %collective-permute-start.8) | collective-permute-done | bytes 8224 | tf_op jit(solution)/shard_map/ppermute | solution.py:409
  30.2 0.0 collective-permute-start.9
  30.2 0.0 collective-permute-done.10.refs_3_.refs_9_
  30.2 1.2 %shard_map.88 = (bf16[512,640]{1,0:T(8,128)(2,1)S(1)}, bf16[512,640]{1,0:T(8,128)(2,1)S(1)}, f32[8,512]{1,0:T(8,128)S(1)}, bf16[1024,128]{1,0:T(8,128)(2,1)S(1)}, bf16[1024,128]{1,0:T(8,128)(2,1)S(1)}) custom-call(bf16[512,256]{1,0:T(8,128)(2,1)S(1)} %get-tuple-element.68.refs_0_.refs_6_, bf16[512,256]{1,0:T(8,128)(2,1)S(1)} %get-tuple-element.69.refs_1_.refs_7_, ...), custom_call_target="tpu_custom_call" | custom-call | flops 1495000064 | bytes 3424256 | tf_op jit(solution)/shard_map/pallas_call | solution.py:33
  31.4 0.0 collective-permute-done.7.other_ref
  31.4 0.0 collective-permute-done.9.other_ref
  31.4 0.7 %collective-permute-start.11 = (f32[64,128]{1,0:T(8,128)S(1)}, f32[64,128]{1,0:T(8,128)S(1)}, u32[]{:S(2)}, u32[]{:S(2)}) collective-permute-start(f32[64,128]{1,0:T(8,128)S(1)} %shard_map.90.refs_5_), channel_id=1, source_target_pairs={{0,16},{4,20},{8,24},{12,28},{16,0},{20,4},{24,8},{28,12},{1,17},{... | collective-permute-start | bytes 98312 | tf_op jit(solution)/shard_map/ppermute | solution.py:409
  32.1 1.3 %collective-permute-start.12 = (f32[8,512]{1,0:T(8,128)S(1)}, f32[8,512]{1,0:T(8,128)S(1)}, u32[]{:S(2)}, u32[]{:S(2)}) collective-permute-start(f32[8,512]{1,0:T(8,128)S(1)} %get-tuple-element.72.refs_13_), channel_id=1, source_target_pairs={{4,0},{8,4},{12,8},{16,12},{20,16},{24,20},{28,24},{0,28},{5,1},{9... | collective-permute-start | bytes 49160 | tf_op jit(solution)/shard_map/ppermute | solution.py:508
  33.4 1.5 %shard_map.91 = (bf16[512,256]{1,0:T(8,128)(2,1)S(1)}, bf16[512,256]{1,0:T(8,128)(2,1)S(1)}, f32[512,640]{1,0:T(8,128)S(1)}, f32[512,640]{1,0:T(8,128)S(1)}, bf1...) custom-call(bf16[512,640]{1,0:T(8,128)(2,1)S(1)} %get-tuple-element.74.refs_0_, ...), custom_call_target="tpu_custom_call" | custom-call | flops 230000000 | bytes 7864320 | tf_op jit(solution)/shard_map/pallas_call | solution.py:33
  34.9 0.0 collective-permute-done.12.refs_14_
  34.9 0.5 %collective-permute-done.11.refs_6_ = f32[64,128]{1,0:T(8,128)S(1)} collective-permute-done((f32[64,128]{1,0:T(8,128)S(1)}, f32[64,128]{1,0:T(8,128)S(1)}, u32[]{:S(2)}, u32[]{:S(2)}) %collective-permute-start.11) | collective-permute-done | bytes 32800 | tf_op jit(solution)/shard_map/ppermute | solution.py:409
  35.4 2.9 %shard_map.92 = (bf16[512,256]{1,0:T(8,128)(2,1)}, bf16[512,256]{1,0:T(8,128)(2,1)}, bf16[512,256]{1,0:T(8,128)(2,1)}, bf16[512,256]{1,0:T(8,128)(2,1)}) custom-call(s32[192]{0:T(256)S(1)} %get-tuple-element.54.refs_0_, bf16[4096,256]{1,0:T(8,128)(2,1)S(1)} %get-tuple-element.60.refs_1_, bf16[512,512]{1,0:T(8,128)(2,1)S(1)} %get-tuple-element.61.refs_4_.refs_2_, ...), custom_call_target="tpu_custom_call" | custom-call | flops 3795000064 | bytes 9536256 | tf_op jit(solution)/shard_map/pallas_call | solution.py:33
  (3 shorter events, 0.0 us)
Async XLA Ops:
  2.1 4.7 %collective-permute-start = (bf16[512,768]{1,0:T(8,128)(2,1)S(1)}, bf16[512,768]{1,0:T(8,128)(2,1)S(1)}, u32[]{:S(2)}, u32[]{:S(2)}) collective-permute-start(bf16[512,768]{1,0:T(8,128)(2,1)S(1)} %get-tuple-element.45), channel_id=1, source_target_pairs={{0,4},{4,0},{8,12},{12,8},{16,20},{20,16},{24,28},{28,24},{1,5},{5... | collective-permute-start | bytes 2359304 | tf_op jit(solution)/shard_map/ppermute | solution.py:409
  2.6 10.7 %collective-permute-start.5 = (bf16[512,256]{1,0:T(8,128)(2,1)S(1)}, bf16[512,256]{1,0:T(8,128)(2,1)S(1)}, u32[]{:S(2)}, u32[]{:S(2)}) collective-permute-start(bf16[512,256]{1,0:T(8,128)(2,1)S(1)} %get-tuple-element.51), channel_id=1, source_target_pairs={{0,24},{4,28},{8,16},{12,20},{16,8},{20,12},{24,0},{28,4},{1,25},{... | collective-permute-start | bytes 786440 | tf_op jit(solution)/shard_map/ppermute | solution.py:409
  6.1 14.0 %collective-permute-start.3 = (bf16[512,256]{1,0:T(8,128)(2,1)S(1)}, bf16[512,256]{1,0:T(8,128)(2,1)S(1)}, u32[]{:S(2)}, u32[]{:S(2)}) collective-permute-start(bf16[512,256]{1,0:T(8,128)(2,1)S(1)} %get-tuple-element.51), channel_id=1, source_target_pairs={{0,16},{4,20},{8,24},{12,28},{16,0},{20,4},{24,8},{28,12},{1,17},{... | collective-permute-start | bytes 786440 | tf_op jit(solution)/shard_map/ppermute | solution.py:409
  6.6 14.0 %collective-permute-start.1 = (bf16[512,256]{1,0:T(8,128)(2,1)S(1)}, bf16[512,256]{1,0:T(8,128)(2,1)S(1)}, u32[]{:S(2)}, u32[]{:S(2)}) collective-permute-start(bf16[512,256]{1,0:T(8,128)(2,1)S(1)} %get-tuple-element.49), channel_id=1, source_target_pairs={{0,8},{4,12},{8,0},{12,4},{16,24},{20,28},{24,16},{28,20},{1,9},{5... | collective-permute-start | bytes 786440 | tf_op jit(solution)/shard_map/ppermute | solution.py:409
  6.8 13.4 %all-to-all-start = ((s32[32,1,128]{2,1,0:T(1,128)}), s32[32,1,128]{2,1,0:T(1,128)S(1)}, u32[]{:S(2)}, u32[]{:S(2)}) async-start(s32[32,1,128]{2,1,0:T(1,128)} %bitcast.2), calls=%async_computation | async-start | bytes 32768 | tf_op jit(solution)/shard_map/all_to_all | solution.py:450
  20.1 2.0 %collective-permute-start.6 = (bf16[512,256]{1,0:T(8,128)(2,1)S(1)}, bf16[512,256]{1,0:T(8,128)(2,1)S(1)}, u32[]{:S(2)}, u32[]{:S(2)}) collective-permute-start(bf16[512,256]{1,0:T(8,128)(2,1)S(1)} %collective-permute-done.5.refs_8_), channel_id=1, source_target_pairs={{0,4},{4,0},{8,12},{12,8},{16,20},{20,16},{24,28},{28,24},{1,5},{5... | collective-permute-start | bytes 786440 | tf_op jit(solution)/shard_map/ppermute | solution.py:409
  20.1 2.0 %collective-permute-start.4 = (bf16[512,256]{1,0:T(8,128)(2,1)S(1)}, bf16[512,256]{1,0:T(8,128)(2,1)S(1)}, u32[]{:S(2)}, u32[]{:S(2)}) collective-permute-start(bf16[512,256]{1,0:T(8,128)(2,1)S(1)} %collective-permute-done.3.refs_6_), channel_id=1, source_target_pairs={{0,4},{4,0},{8,12},{12,8},{16,20},{20,16},{24,28},{28,24},{1,5},{5... | collective-permute-start | bytes 786440 | tf_op jit(solution)/shard_map/ppermute | solution.py:409
  20.6 1.8 %collective-permute-start.2 = (bf16[512,256]{1,0:T(8,128)(2,1)S(1)}, bf16[512,256]{1,0:T(8,128)(2,1)S(1)}, u32[]{:S(2)}, u32[]{:S(2)}) collective-permute-start(bf16[512,256]{1,0:T(8,128)(2,1)S(1)} %collective-permute-done.1.refs_4_), channel_id=1, source_target_pairs={{0,4},{4,0},{8,12},{12,8},{16,20},{20,16},{24,28},{28,24},{1,5},{5... | collective-permute-start | bytes 786440 | tf_op jit(solution)/shard_map/ppermute | solution.py:409
  20.7 9.5 %collective-permute-start.10 = (bf16[512,256]{1,0:T(8,128)(2,1)S(1)}, bf16[512,256]{1,0:T(8,128)(2,1)S(1)}, u32[]{:S(2)}, u32[]{:S(2)}) collective-permute-start(bf16[512,256]{1,0:T(8,128)(2,1)S(1)} %get-tuple-element.71), channel_id=1, source_target_pairs={{4,8},{12,16},{20,24},{28,0},{8,4},{16,12},{24,20},{0,28},{5,9},{1... | collective-permute-start | bytes 786440 | tf_op jit(solution)/shard_map/ppermute | solution.py:453
  26.4 3.7 %collective-permute-start.8 = (f32[16,128]{1,0:T(8,128)S(1)}, f32[16,128]{1,0:T(8,128)S(1)}, u32[]{:S(2)}, u32[]{:S(2)}) collective-permute-start(f32[16,128]{1,0:T(8,128)S(1)} %get-tuple-element.64.own_ref), channel_id=1, source_target_pairs={{0,8},{4,12},{8,0},{12,4},{16,24},{20,28},{24,16},{28,20},{1,9},{5... | collective-permute-start | bytes 24584 | tf_op jit(solution)/shard_map/ppermute | solution.py:409
  27.1 4.3 %collective-permute-start.7 = (f32[16,128]{1,0:T(8,128)S(1)}, f32[16,128]{1,0:T(8,128)S(1)}, u32[]{:S(2)}, u32[]{:S(2)}) collective-permute-start(f32[16,128]{1,0:T(8,128)S(1)} %get-tuple-element.64.own_ref), channel_id=1, source_target_pairs={{0,4},{4,0},{8,12},{12,8},{16,20},{20,16},{24,28},{28,24},{1,5},{5... | collective-permute-start | bytes 24584 | tf_op jit(solution)/shard_map/ppermute | solution.py:409
  30.2 1.2 %collective-permute-start.9 = (f32[16,128]{1,0:T(8,128)S(1)}, f32[16,128]{1,0:T(8,128)S(1)}, u32[]{:S(2)}, u32[]{:S(2)}) collective-permute-start(f32[16,128]{1,0:T(8,128)S(1)} %collective-permute-done.8.own_ref), channel_id=1, source_target_pairs={{0,4},{4,0},{8,12},{12,8},{16,20},{20,16},{24,28},{28,24},{1,5},{5... | collective-permute-start | bytes 24584 | tf_op jit(solution)/shard_map/ppermute | solution.py:409
  31.4 4.0 %collective-permute-start.11 = (f32[64,128]{1,0:T(8,128)S(1)}, f32[64,128]{1,0:T(8,128)S(1)}, u32[]{:S(2)}, u32[]{:S(2)}) collective-permute-start(f32[64,128]{1,0:T(8,128)S(1)} %shard_map.90.refs_5_), channel_id=1, source_target_pairs={{0,16},{4,20},{8,24},{12,28},{16,0},{20,4},{24,8},{28,12},{1,17},{... | collective-permute-start | bytes 98312 | tf_op jit(solution)/shard_map/ppermute | solution.py:409
  32.1 2.8 %collective-permute-start.12 = (f32[8,512]{1,0:T(8,128)S(1)}, f32[8,512]{1,0:T(8,128)S(1)}, u32[]{:S(2)}, u32[]{:S(2)}) collective-permute-start(f32[8,512]{1,0:T(8,128)S(1)} %get-tuple-element.72.refs_13_), channel_id=1, source_target_pairs={{4,0},{8,4},{12,8},{16,12},{20,16},{24,20},{28,24},{0,28},{5,1},{9... | collective-permute-start | bytes 49160 | tf_op jit(solution)/shard_map/ppermute | solution.py:508
